TPU v7x, 32 devices: a whole 2x2x4 slice. The times are simulated.
32 devices in a mesh: section: 4 (over y, x), tensor: 4 (over z), dp: 2 (over core).
Axes of the slice: x: 2, y: 2, z: 4, core: 2. Of those that a mesh axis runs over, the one named last changes fastest.
Arguments:
- tokens: bfloat16 [4, 2048, 1024], P('section', 'dp', 'tensor'), may hold values from -6 to 6
- lengths: int32 [2, 6], P('dp'), may hold values from 1 to 1024, 4096 in all within a row
- gains: float32 [4, 1024], P('section'), may hold values from 0.5 to 1.5
- qk_gains: float32 [2, 64], replicated, may hold values from 0.5 to 1.5
- conv_kernel: bfloat16 [3, 1024], P(None, 'tensor'), may hold values from -3.5 to 3.5
- conv_in: bfloat16 [1024, 3, 1024], P(('section', 'dp'), None, 'tensor'), may hold values from -0.1875 to 0.1875
- conv_out: bfloat16 [1024, 1024], P('tensor', ('section', 'dp')), may hold values from -0.1875 to 0.1875
- ffn1_in: bfloat16 [1024, 2, 4608], P(('section', 'dp'), None, 'tensor'), may hold values from -0.1875 to 0.1875
- ffn1_out: bfloat16 [4608, 1024], P('tensor', ('section', 'dp')), may hold values from -0.09375 to 0.09375
- attn_qkv: bfloat16 [1024, 8, 256], P(('section', 'dp'), 'tensor'), may hold values from -0.1875 to 0.1875
- attn_out: bfloat16 [1024, 1024], P('tensor', ('section', 'dp')), may hold values from -3 to 3
- ffn2_in: bfloat16 [1024, 2, 4608], P(('section', 'dp'), None, 'tensor'), may hold values from -0.1875 to 0.1875
- ffn2_out: bfloat16 [4608, 1024], P('tensor', ('section', 'dp')), may hold values from -0.09375 to 0.09375
- cotangent: bfloat16 [4, 2048, 1024], P('section', 'dp', 'tensor'), may hold values from -6 to 6
Outputs:
- output: bfloat16 [4, 2048, 1024], P('section', 'dp', 'tensor')
- input_grad: bfloat16 [4, 2048, 1024], P('section', 'dp', 'tensor')
- gains_grad: float32 [4, 1024], replicated
- qk_gains_grad: float32 [2, 64], replicated
- conv_kernel_grad: float32 [3, 1024], replicated
- conv_in_grad: float32 [1024, 3, 1024], P(('section', 'dp'), None, 'tensor')
- conv_out_grad: float32 [1024, 1024], P('tensor', ('section', 'dp'))
- ffn1_in_grad: float32 [1024, 2, 4608], P(('section', 'dp'), None, 'tensor')
- ffn1_out_grad: float32 [4608, 1024], P('tensor', ('section', 'dp'))
- attn_qkv_grad: float32 [1024, 8, 256], P(('section', 'dp'), 'tensor')
- attn_out_grad: float32 [1024, 1024], P('tensor', ('section', 'dp'))
- ffn2_in_grad: float32 [1024, 2, 4608], P(('section', 'dp'), None, 'tensor')
- ffn2_out_grad: float32 [4608, 1024], P('tensor', ('section', 'dp'))
Inputs may be any that keep to these rules, and one draw needn't show every extreme that they name: Each row holds the lengths of the 6 sequences packed one after another in a replica's stream; they sum to 4096, and the longest is exactly 1024.
All inputs are finite; a program needn't handle non-finite values.
Results may differ from a plain program's by a relative error of at most 0.025.
Values may be sent and summed in bfloat16 or wider, within the bound.
No kernel may reach another device: no remote copies, remote signals or barrier semaphores. Data moves between devices by JAX's collectives and lax.ppermute only.
A program may use at most 640 MiB of HBM per device.

v0:
```python
import functools

import jax
import jax.numpy as jnp
from jax import lax
from jax.experimental import pallas as pl
from jax.experimental.pallas import tpu as pltpu
from jax.sharding import PartitionSpec as P

EPSILON = 1e-05
ROTARY_BASE = 1000000.0
NEGATIVE = -1e30
AXES = ("section", "tensor", "dp")
LOW = jnp.bfloat16
WIDE = jnp.float32
RANKS = 4
LONGEST = 1024


class Place:
    def __init__(self):
        self.sections = lax.axis_size("section")
        self.depth = lax.axis_size("tensor")
        self.replicas = lax.axis_size("dp")
        self.rings = self.replicas // 2
        section = lax.axis_index("section")
        self.z = lax.axis_index("tensor")
        replica = lax.axis_index("dp")
        self.half, self.side = section // 2, section % 2
        self.ring, self.core = replica // 2, replica % 2
        self.rank = 2 * self.side + self.core

    def move(self, values, target):
        route = []
        for half in range(self.sections // 2):
            for side in range(2):
                for z in range(self.depth):
                    for ring in range(self.rings):
                        for core in range(2):
                            goal = target(half, side, z, ring, core)
                            if goal is not None:
                                route.append(
                                    (self.flat(half, side, z, ring, core), self.flat(*goal))
                                )
        return lax.ppermute(values, AXES, route)

    def flat(self, half, side, z, ring, core):
        return ((half * 2 + side) * self.depth + z) * self.replicas + ring * 2 + core

    def to_rank(self, values, k):
        return self.move(
            values, lambda half, side, z, ring, core: (half, side ^ (k >> 1), z, ring, core ^ (k & 1))
        )

    def to_half(self, values):
        return self.move(
            values, lambda half, side, z, ring, core: (1 - half, side, z, ring, core)
        )

    def up(self, values, distance=1):
        return self.move(
            values,
            lambda half, side, z, ring, core: (half, side, z + distance, ring, core)
            if 0 <= z + distance < self.depth
            else None,
        )

    def to_ring(self, values, distance):
        return self.move(
            values,
            lambda half, side, z, ring, core: (half, side, z, (ring + distance) % self.rings, core),
        )

    def across_z(self, values, bit):
        return self.move(
            values, lambda half, side, z, ring, core: (half, side, z ^ bit, ring, core)
        )

    def across_ring(self, values, bit):
        return self.move(
            values, lambda half, side, z, ring, core: (half, side, z, ring ^ bit, core)
        )

    def turn(self, values):
        width = values.shape[-1] // 2
        turned = jnp.concatenate([values[..., width:], values[..., :width]], axis=-1)
        return jnp.where(self.half == 0, values, turned)

    def by_rank(self, blocks):
        return [
            lax.select_n(jnp.bitwise_xor(self.rank, b), *blocks) for b in range(RANKS)
        ]

    def mirrored(self, stacked, place):
        count = stacked.shape[0]
        flipped = jnp.concatenate([stacked[:1], stacked[:0:-1]], axis=0)
        return lax.dynamic_slice_in_dim(
            jnp.concatenate([flipped, flipped], axis=0), count - place, count, 0
        )

    def rolled(self, stacked, place):
        count = stacked.shape[0]
        return lax.dynamic_slice_in_dim(
            jnp.concatenate([stacked, stacked], axis=0), count - place, count, 0
        )

    def gather_z(self, values):
        upward, downward = [values], [values]
        for _ in range(self.depth - 1):
            upward.append(self.up(upward[-1], 1))
            downward.append(self.up(downward[-1], -1))
        return [values] + [
            upward[s] + downward[self.depth - s] for s in range(1, self.depth)
        ]

    def scatter_z(self, parts):
        upward = downward = None
        for t in range(1, self.depth):
            rest = self.depth - t
            ahead = jnp.where(self.z < t, parts[t], 0).astype(LOW)
            behind = jnp.where(self.z >= rest, parts[rest], 0).astype(LOW)
            if upward is not None:
                ahead = (ahead.astype(WIDE) + upward.astype(WIDE)).astype(LOW)
                behind = (behind.astype(WIDE) + downward.astype(WIDE)).astype(LOW)
            upward, downward = self.up(ahead, 1), self.up(behind, -1)
        return (parts[0].astype(WIDE) + upward.astype(WIDE) + downward.astype(WIDE)).astype(LOW)

    def gather_half(self, values):
        return jnp.concatenate([values, self.to_half(values)], axis=-1)

    def scatter_half(self, values):
        width = values.shape[-1] // 2
        other = self.to_half(values[..., width:].astype(LOW))
        return (values[..., :width].astype(WIDE) + other.astype(WIDE)).astype(LOW)

    def exchange(self, parts):
        if self.rings > 1:
            found = [parts] + [self.to_ring(parts, k) for k in range(1, self.rings)]
            parts = self.mirrored(jnp.stack(found), self.ring)
        else:
            parts = parts[None]
        blocks = []
        for k in range(RANKS):
            part = lax.dynamic_index_in_dim(
                parts, jnp.bitwise_xor(self.rank, k), 1, keepdims=False
            )
            blocks.append(part if k == 0 else self.to_rank(part, k))
        blocks = self.by_rank(blocks)
        ordered = [
            blocks[2 * side + core][ring]
            for side in range(2)
            for ring in range(self.rings)
            for core in range(2)
        ]
        return jnp.concatenate(ordered, axis=-1)

    def exchange_back(self, values):
        block = values.shape[-1] // (RANKS * self.rings)
        grid = values.reshape(values.shape[0], 2, self.rings, 2, block)
        stacked = jnp.stack(
            [grid[:, side, :, core] for side in range(2) for core in range(2)]
        ).transpose(0, 2, 1, 3)
        blocks = []
        for k in range(RANKS):
            part = lax.dynamic_index_in_dim(
                stacked, jnp.bitwise_xor(self.rank, k), 0, keepdims=False
            )
            blocks.append(part if k == 0 else self.to_rank(part, k))
        parts = jnp.stack(self.by_rank(blocks), axis=1)
        if self.rings == 1:
            return parts[0]
        total = lax.dynamic_index_in_dim(parts, self.ring, 0, keepdims=False).astype(WIDE)
        for k in range(1, self.rings):
            sent = lax.dynamic_index_in_dim(
                parts, (self.ring + k) % self.rings, 0, keepdims=False
            )
            total = total + self.to_ring(sent, k).astype(WIDE)
        return total

    def gather_rows(self, values):
        mate = self.to_rank(values, 1)
        across = self.to_rank(values, 2)
        return [values, mate, across, self.to_rank(across, 1)]

    def scatter_rows(self, blocks):
        rows = blocks[0].shape[0]
        came = self.to_rank(jnp.concatenate([blocks[1], blocks[3]], axis=0).astype(LOW), 1)
        across = (blocks[2].astype(WIDE) + came[rows:].astype(WIDE)).astype(LOW)
        own = blocks[0].astype(WIDE) + came[:rows].astype(WIDE)
        return own + self.to_rank(across, 2).astype(WIDE)

    def total(self, values):
        for k in (1, 2):
            values = values + self.to_rank(values, k)
        values = values + self.to_half(values)
        bit = 1
        while bit < self.depth:
            values = values + self.across_z(values, bit)
            bit *= 2
        bit = 1
        while bit < self.rings:
            values = values + self.across_ring(values, bit)
            bit *= 2
        return values


def times(a, b):
    return lax.dot_general(a, b, (((1,), (0,)), ((), ())), preferred_element_type=WIDE)


def times_rows(a, b):
    return lax.dot_general(a, b, (((1,), (1,)), ((), ())), preferred_element_type=WIDE)


def columns_times(a, b):
    return lax.dot_general(a, b, (((0,), (0,)), ((), ())), preferred_element_type=WIDE)


def root_norm(values, gain_row):
    return (
        values * lax.rsqrt(jnp.mean(values * values, axis=-1, keepdims=True) + EPSILON) * gain_row
    )


def root_norm_back(inputs, gain_row, grad, arriving):
    widened = inputs.astype(WIDE)
    inverse = lax.rsqrt(jnp.mean(widened * widened, axis=-1, keepdims=True) + EPSILON)
    unit_rows = widened * inverse
    scaled = grad * gain_row
    through = inverse * (scaled - unit_rows * jnp.mean(scaled * unit_rows, axis=-1, keepdims=True))
    gain_grad = jnp.sum(grad * unit_rows, axis=0)
    return ((arriving.astype(WIDE) + through).astype(LOW), gain_grad)


def angles(offsets, head_width):
    inverse = ROTARY_BASE ** (-jnp.arange(0, head_width, 2).astype(WIDE) / head_width)
    phases = offsets.astype(WIDE)[:, None] * inverse[None, :]
    phases = jnp.concatenate([phases, phases], axis=1)
    return (jnp.cos(phases), jnp.sin(phases))


def rotary(values, cosine_rows, sine_rows):
    half_width = values.shape[-1] // 2
    turned = jnp.concatenate([-values[..., half_width:], values[..., :half_width]], axis=-1)
    return values * cosine_rows + turned * sine_rows


def split_heads(packed, head_gains, cosine_rows, sine_rows):
    size_head = packed.shape[-1] // 4
    queries = packed[..., : 2 * size_head].reshape(packed.shape[0], packed.shape[1], 2, size_head)
    key_heads = packed[..., 2 * size_head : 3 * size_head]
    value_heads = packed[..., 3 * size_head :]
    queries = rotary(
        root_norm(queries, head_gains[0]),
        cosine_rows[:, None, None, :],
        sine_rows[:, None, None, :],
    )
    key_heads = rotary(
        root_norm(key_heads, head_gains[1]), cosine_rows[:, None, :], sine_rows[:, None, :]
    )
    return (queries, key_heads, value_heads)


def block_weights(offsets, queries, keys, scale):
    scores = (
        lax.dot_general(queries, keys, (((1,), (1,)), ((), ())), preferred_element_type=WIDE)
        * scale
    )
    rows, window = offsets.shape[0], keys.shape[0]
    shape = (rows, window)
    back = (
        lax.broadcasted_iota(jnp.int32, shape, 0)
        + LONGEST
        - lax.broadcasted_iota(jnp.int32, shape, 1)
    )
    allowed = (back >= 0) & (back <= offsets)
    allowed = jnp.concatenate([allowed.astype(WIDE)] * (queries.shape[0] // rows), axis=0) > 0.5
    scores = jnp.where(allowed, scores, NEGATIVE)
    weights = jnp.exp(scores - jnp.max(scores, axis=-1, keepdims=True))
    return weights / jnp.sum(weights, axis=-1, keepdims=True)


def attend_kernel(scale, offsets_ref, queries_ref, keys_ref, values_ref, out_ref):
    rows, width = queries_ref.shape[2], queries_ref.shape[3]
    low = pl.multiple_of(pl.program_id(1) * rows, rows)
    window = pl.ds(low, LONGEST + rows)
    queries = queries_ref[0].reshape(2 * rows, width)
    weights = block_weights(offsets_ref[...], queries, keys_ref[0, window, :], scale)
    result = jnp.dot(
        weights.astype(LOW), values_ref[0, window, :], preferred_element_type=WIDE
    ).astype(LOW)
    out_ref[0] = result.reshape(2, rows, width)


def attend_back_kernel(
    scale,
    offsets_ref,
    queries_ref,
    keys_ref,
    values_ref,
    grad_ref,
    queries_grad_ref,
    keys_grad_ref,
    values_grad_ref,
):
    rows, width = queries_ref.shape[2], queries_ref.shape[3]

    @pl.when(pl.program_id(1) == 0)
    def _():
        keys_grad_ref[...] = jnp.zeros_like(keys_grad_ref)
        values_grad_ref[...] = jnp.zeros_like(values_grad_ref)

    low = pl.multiple_of(pl.program_id(1) * rows, rows)
    window = pl.ds(low, LONGEST + rows)
    queries = queries_ref[0].reshape(2 * rows, width)
    grad = grad_ref[0].reshape(2 * rows, width)
    keys, values = keys_ref[0, window, :], values_ref[0, window, :]
    weights = block_weights(offsets_ref[...], queries, keys, scale)
    flow = lax.dot_general(grad, values, (((1,), (1,)), ((), ())), preferred_element_type=WIDE)
    inner = jnp.sum(weights * flow, axis=-1, keepdims=True)
    score_grad = (weights * (flow - inner)).astype(LOW)
    values_grad_ref[0, window, :] += lax.dot_general(
        weights.astype(LOW), grad, (((0,), (0,)), ((), ())), preferred_element_type=WIDE
    )
    keys_grad_ref[0, window, :] += (
        lax.dot_general(
            score_grad, queries, (((0,), (0,)), ((), ())), preferred_element_type=WIDE
        )
        * scale
    )
    queries_grad = jnp.dot(score_grad, keys, preferred_element_type=WIDE) * scale
    queries_grad_ref[0] = queries_grad.astype(LOW).reshape(2, rows, width)


def attention_specs(queries, keys, rows):
    groups, _, total, width = queries.shape
    grid = (groups, total // rows)
    offsets_spec = pl.BlockSpec((rows, 1), lambda g, i: (i, 0))
    rows_spec = pl.BlockSpec((1, 2, rows, width), lambda g, i: (g, 0, i, 0))
    keys_spec = pl.BlockSpec((1, keys.shape[1], width), lambda g, i: (g, 0, 0))
    return (grid, offsets_spec, rows_spec, keys_spec)


def attend(offsets, queries, keys, values, rows):
    grid, offsets_spec, rows_spec, keys_spec = attention_specs(queries, keys, rows)
    return pl.pallas_call(
        functools.partial(attend_kernel, queries.shape[-1] ** (-0.5)),
        grid=grid,
        in_specs=[offsets_spec, rows_spec, keys_spec, keys_spec],
        out_specs=rows_spec,
        out_shape=jax.ShapeDtypeStruct(queries.shape, LOW),
        compiler_params=pltpu.CompilerParams(vmem_limit_bytes=48 << 20),
        name="attend",
    )(offsets[:, None], queries, keys, values)


def attend_back(offsets, queries, keys, values, grad, rows):
    grid, offsets_spec, rows_spec, keys_spec = attention_specs(queries, keys, rows)
    return pl.pallas_call(
        functools.partial(attend_back_kernel, queries.shape[-1] ** (-0.5)),
        grid=grid,
        in_specs=[offsets_spec, rows_spec, keys_spec, keys_spec, rows_spec],
        out_specs=[rows_spec, keys_spec, keys_spec],
        out_shape=[
            jax.ShapeDtypeStruct(queries.shape, LOW),
            jax.ShapeDtypeStruct(keys.shape, WIDE),
            jax.ShapeDtypeStruct(keys.shape, WIDE),
        ],
        compiler_params=pltpu.CompilerParams(vmem_limit_bytes=48 << 20),
        name="attend_back",
    )(offsets[:, None], queries, keys, values, grad)


def local(
    tokens,
    lengths,
    gains,
    qk_gains,
    conv_kernel,
    conv_in,
    conv_out,
    ffn1_in,
    ffn1_out,
    attn_qkv,
    attn_out,
    ffn2_in,
    ffn2_out,
    cotangent,
):
    here = Place()
    depth = here.depth
    stretch = tokens.shape[1]
    slice_width = tokens.shape[2]
    model_width = slice_width * depth
    stream_rows = here.sections * stretch
    team_rows = stream_rows // depth
    own_rows = team_rows // RANKS
    head_width = attn_qkv.shape[2] // 4
    groups_here = attn_qkv.shape[1]
    groups = groups_here * depth // RANKS
    block_width = conv_in.shape[0]
    query_rows = min(256, team_rows)

    teams = depth // here.sections

    def row_goal(k):
        def goal(half, side, z, ring, core):
            part = (z + k) % depth
            rank = part % RANKS
            batch = half * 2 + side
            return (core, rank // 2, batch * (depth // RANKS) + part // RANKS, ring, rank % 2)

        return goal

    def flat_goal(k):
        return {
            here.flat(*source): here.flat(*row_goal(k)(*source))
            for source in (
                (half, side, z, ring, core)
                for half in range(here.sections // 2)
                for side in range(2)
                for z in range(depth)
                for ring in range(here.rings)
                for core in range(2)
            )
        }

    own_part = (here.z % (depth // RANKS)) * RANKS + here.rank

    def rows_in(values):
        grid = values[0].reshape(depth, own_rows, slice_width)
        pieces = []
        for k in range(depth):
            piece = lax.dynamic_index_in_dim(grid, (here.z + k) % depth, 0, keepdims=False)
            pieces.append(lax.ppermute(piece, AXES, sorted(flat_goal(k).items())))
        columns = here.mirrored(jnp.stack(pieces), own_part)
        return here.turn(columns.transpose(1, 0, 2).reshape(own_rows, model_width))

    def rows_out(values):
        grid = here.turn(values).reshape(own_rows, depth, slice_width)
        pieces = []
        for k in range(depth):
            piece = lax.dynamic_index_in_dim(
                grid, (own_part - k) % depth, 1, keepdims=False
            )
            route = sorted((goal, source) for source, goal in flat_goal(k).items())
            pieces.append(lax.ppermute(piece, AXES, route))
        return here.rolled(jnp.stack(pieces), here.z).reshape(1, stretch, slice_width)

    def by_ranks(values):
        kinds, rows, columns = values.shape
        share = rows // RANKS
        return (
            values.reshape(kinds, RANKS, share, columns)
            .transpose(1, 0, 2, 3)
            .reshape(RANKS, kinds * share, columns)
        )

    def from_ranks(values, kinds):
        _, rows, columns = values.shape
        share = rows // kinds
        return (
            values.reshape(RANKS, kinds, share, columns)
            .transpose(1, 0, 2, 3)
            .reshape(kinds, RANKS * share, columns)
        )

    def slots_together(slots, kinds):
        rows, columns = slots[0].shape
        return jnp.stack(
            [slot.reshape(kinds, rows // kinds, columns) for slot in slots], axis=1
        ).reshape(kinds * depth * (rows // kinds), columns)

    def slots_apart(values, kinds):
        rows, columns = values.shape
        grid = values.reshape(kinds, depth, rows // (kinds * depth), columns)
        return [grid[:, s].reshape(rows // depth, columns) for s in range(depth)]

    def inward(values):
        return values.transpose(1, 2, 0)

    def gather_z_first(values, kinds):
        slots = here.gather_z(here.exchange(by_ranks(values)))
        return slots_together([here.gather_half(slot) for slot in slots], kinds)

    def scatter_half_first(grad, kinds):
        parts = [here.scatter_half(part) for part in slots_apart(grad.astype(LOW), kinds)]
        return from_ranks(here.exchange_back(here.scatter_z(parts)), kinds)

    taps = conv_kernel.shape[0]
    share = slice_width // RANKS
    mixer_parts = here.exchange(
        by_ranks(jnp.concatenate([inward(conv_in), conv_out[None]], axis=0))
    )
    own_taps = lax.dynamic_slice_in_dim(conv_kernel, here.rank * share, share, 1)
    own_taps = jnp.pad(own_taps, ((0, 16 - taps), (0, mixer_parts.shape[1] - share)))
    mixer_slots = here.gather_z(
        here.gather_half(jnp.concatenate([mixer_parts, own_taps], axis=0))
    )
    mixer_weights = slots_together([slot[: 4 * share] for slot in mixer_slots], 4)
    channels = depth * share
    mixer_inward, mixer_outward = mixer_weights[: 3 * channels], mixer_weights[3 * channels :]
    kernel = jnp.concatenate(
        [slot[4 * share : 4 * share + taps, :share] for slot in mixer_slots], axis=1
    ).astype(WIDE)

    first_inward = gather_z_first(inward(ffn1_in), 2)
    first_outward = gather_z_first(ffn1_out[None], 1)

    heads_rows = attn_out.shape[0] // groups_here
    heads_parts = jnp.concatenate(
        [inward(attn_qkv), attn_out.reshape(groups_here, heads_rows, -1)], axis=1
    )
    heads_size = heads_parts.shape[1]
    heads_parts = here.mirrored(jnp.stack(here.gather_z(heads_parts)), here.z)
    heads_weights = here.gather_half(
        here.exchange(heads_parts.reshape(RANKS, groups * heads_size, block_width))
    ).reshape(groups, heads_size, model_width)
    heads_inward = heads_weights[:, : heads_size - heads_rows].reshape(-1, model_width)
    heads_outward = heads_weights[:, heads_size - heads_rows :].reshape(-1, model_width)

    second_inward = gather_z_first(inward(ffn2_in), 2)
    second_outward = gather_z_first(ffn2_out[None], 1)

    own_lengths = jnp.where(here.half == here.core, lengths[0], here.to_rank(lengths[0], 1))
    places = here.z * team_rows + jnp.arange(team_rows + 2, dtype=jnp.int32)
    passed = (places[:, None] >= jnp.cumsum(own_lengths)[None, :]).astype(jnp.int32)
    offsets = places - jnp.sum(passed * own_lengths[None, :], axis=1)
    first_mask = (offsets >= 1).astype(WIDE)[:, None]
    second_mask = (offsets >= 2).astype(WIDE)[:, None]
    offsets = offsets[:team_rows]
    cosine_rows, sine_rows = angles(offsets, head_width)
    all_gains = here.turn(lax.all_gather(gains, "section", axis=0, tiled=True))

    def gather_ordered(values):
        return jnp.concatenate(here.by_rank(here.gather_rows(values)), axis=0)

    def gather_any(values):
        return jnp.concatenate(here.gather_rows(values), axis=0)

    def scatter_ordered(values):
        grid = values.astype(LOW).reshape(RANKS, own_rows, model_width)
        return here.scatter_rows(
            [
                lax.dynamic_index_in_dim(
                    grid, jnp.bitwise_xor(here.rank, k), 0, keepdims=False
                )
                for k in range(RANKS)
            ]
        )

    def scatter_any(values):
        grid = values.astype(LOW).reshape(RANKS, own_rows, model_width)
        return here.scatter_rows([grid[k] for k in range(RANKS)])

    def joined(residual, update):
        return (residual.astype(WIDE) + update).astype(LOW)

    def neighbour_rows(values, distance):
        moved = here.up(values, distance)
        return jnp.roll(
            moved.reshape(values.shape[0], depth, share), distance, axis=1
        ).reshape(values.shape)

    def mixer_forward(residual):
        normed = gather_ordered(root_norm(residual.astype(WIDE), all_gains[0]).astype(LOW))
        projected = times_rows(normed, mixer_inward)
        before, gate, after = (
            projected[:, :channels],
            projected[:, channels : 2 * channels],
            projected[:, 2 * channels :],
        )
        product = before * after
        tail = neighbour_rows(product[-2:], 1)
        extended = jnp.concatenate([tail, product], axis=0)
        once = extended[1:-1] * first_mask[:team_rows]
        twice = extended[:-2] * second_mask[:team_rows]
        mixed = kernel[2] * product + kernel[1] * once + kernel[0] * twice
        gated = (gate * mixed).astype(LOW)
        update = scatter_ordered(times(gated, mixer_outward))
        return joined(residual, update), (
            residual, normed, before, gate, after, product, once, twice, mixed, gated,
        )

    def mixer_backward(arriving, saved):
        residual, normed, before, gate, after, product, once, twice, mixed, gated = saved
        full = gather_ordered(arriving)
        gated_grad = times_rows(full, mixer_outward)
        outward_grad = columns_times(gated, full)
        gate_grad = gated_grad * mixed
        mixed_grad = gated_grad * gate
        extended = jnp.concatenate([mixed_grad, neighbour_rows(mixed_grad[:2], -1)], axis=0)
        product_grad = (
            kernel[2] * mixed_grad
            + kernel[1] * extended[1:-1] * first_mask[1:-1]
            + kernel[0] * extended[2:] * second_mask[2:]
        )
        kernel_grad = jnp.stack(
            [
                jnp.sum(mixed_grad * twice, axis=0),
                jnp.sum(mixed_grad * once, axis=0),
                jnp.sum(mixed_grad * product, axis=0),
            ]
        )
        low = jnp.concatenate(
            [product_grad * after, gate_grad, product_grad * before], axis=1
        ).astype(LOW)
        update = scatter_ordered(times(low, mixer_inward))
        grad = jnp.concatenate([columns_times(low, normed), outward_grad], axis=0)
        leaving, gain_grad = root_norm_back(residual, all_gains[0], update, arriving)
        return leaving, gain_grad, kernel_grad, grad

    def feed_forward(residual, gain_row, inward_weights, outward_weights):
        normed = gather_any(root_norm(residual.astype(WIDE), gain_row).astype(LOW))
        gate_up = times_rows(normed, inward_weights)
        width = gate_up.shape[1] // 2
        hidden = (jax.nn.silu(gate_up[:, :width]) * gate_up[:, width:]).astype(LOW)
        update = scatter_any(times(hidden, outward_weights))
        return joined(residual, update), (residual, normed, gate_up, hidden)

    def feed_backward(arriving, saved, gain_row, inward_weights, outward_weights):
        residual, normed, gate_up, hidden = saved
        full = gather_any(arriving)
        outward_grad = columns_times(hidden, full)
        hidden_grad = times_rows(full, outward_weights)
        width = gate_up.shape[1] // 2
        gate, up = gate_up[:, :width], gate_up[:, width:]
        sigmoid = jax.nn.sigmoid(gate)
        low = jnp.concatenate(
            [
                hidden_grad * up * (sigmoid * (1 + gate * (1 - sigmoid))),
                hidden_grad * (gate * sigmoid),
            ],
            axis=1,
        ).astype(LOW)
        update = scatter_any(times(low, inward_weights))
        inward_grad = columns_times(low, normed)
        leaving, gain_grad = root_norm_back(residual, gain_row, update, arriving)
        return leaving, gain_grad, inward_grad, outward_grad

    halo_steps = LONGEST // team_rows

    def heads_forward(residual):
        normed = gather_ordered(root_norm(residual.astype(WIDE), all_gains[2]).astype(LOW))
        packed = times_rows(normed, heads_inward).reshape(team_rows, groups, 4 * head_width)
        queries, keys, values = split_heads(packed, qk_gains, cosine_rows, sine_rows)
        queries = queries.astype(LOW).transpose(1, 2, 0, 3)
        pairs = jnp.stack([keys, values]).astype(LOW).transpose(0, 2, 1, 3)
        window = jnp.concatenate(
            [here.up(pairs, step) for step in range(halo_steps, 0, -1)] + [pairs], axis=2
        )
        attended = attend(offsets, queries, window[0], window[1], query_rows)
        flat = attended.transpose(2, 0, 1, 3).reshape(team_rows, -1)
        update = scatter_ordered(times(flat, heads_outward))
        return joined(residual, update), (residual, normed, packed, queries, window, flat)

    def heads_backward(arriving, saved):
        residual, normed, packed, queries, window, flat = saved
        full = gather_ordered(arriving)
        outward_grad = columns_times(flat, full)
        attended_grad = (
            times_rows(full, heads_outward)
            .astype(LOW)
            .reshape(team_rows, groups, 2, head_width)
            .transpose(1, 2, 0, 3)
        )
        queries_grad, keys_grad, values_grad = attend_back(
            offsets, queries, window[0], window[1], attended_grad, query_rows
        )
        flow = jnp.stack([keys_grad, values_grad])
        own = flow[:, :, LONGEST:]
        for step in range(1, halo_steps + 1):
            low = (halo_steps - step) * team_rows
            own = own + here.up(flow[:, :, low : low + team_rows].astype(LOW), -step).astype(WIDE)
        own = own.astype(LOW).astype(WIDE).transpose(0, 2, 1, 3)
        _, pull_heads = jax.vjp(
            lambda values, scales: split_heads(values, scales, cosine_rows, sine_rows),
            packed,
            qk_gains,
        )
        packed_grad, head_gains_grad = pull_heads(
            (queries_grad.astype(WIDE).transpose(2, 0, 1, 3), own[0], own[1])
        )
        low = packed_grad.astype(LOW).reshape(team_rows, -1)
        update = scatter_ordered(times(low, heads_inward))
        inward_grad = columns_times(low, normed)
        grad = jnp.concatenate(
            [
                inward_grad.reshape(groups, -1, model_width),
                outward_grad.reshape(groups, -1, model_width),
            ],
            axis=1,
        )
        leaving, gain_grad = root_norm_back(residual, all_gains[2], update, arriving)
        return leaving, gain_grad, head_gains_grad, grad

    residual = rows_in(tokens)
    residual, mixer_saved = mixer_forward(residual)
    residual, first_saved = feed_forward(residual, all_gains[1], first_inward, first_outward)
    residual, heads_saved = heads_forward(residual)
    residual, second_saved = feed_forward(residual, all_gains[3], second_inward, second_outward)
    output = rows_out(residual)

    flowing = rows_in(cotangent)
    flowing, gain3, second_inward_grad, second_outward_grad = feed_backward(
        flowing, second_saved, all_gains[3], second_inward, second_outward
    )
    flowing, gain2, head_gains_grad, heads_grad = heads_backward(flowing, heads_saved)
    flowing, gain1, first_inward_grad, first_outward_grad = feed_backward(
        flowing, first_saved, all_gains[1], first_inward, first_outward
    )
    flowing, gain0, kernel_grad, mixer_grad = mixer_backward(flowing, mixer_saved)
    input_grad = rows_out(flowing)

    second_outward_grad = scatter_half_first(second_outward_grad, 1)[0]
    second_inward_grad = scatter_half_first(second_inward_grad, 2)
    heads_grad = here.exchange_back(
        here.scatter_half(heads_grad.reshape(-1, model_width).astype(LOW))
    ).astype(LOW)
    heads_grad = heads_grad.reshape(depth, groups_here * heads_size, block_width)
    heads_grad = here.mirrored(heads_grad, here.z)
    heads_grad = here.scatter_z([heads_grad[s] for s in range(depth)])
    heads_grad = heads_grad.reshape(groups_here, heads_size, block_width)
    first_outward_grad = scatter_half_first(first_outward_grad, 1)[0]
    first_inward_grad = scatter_half_first(first_inward_grad, 2)
    mixer_grad = from_ranks(
        here.exchange_back(
            here.scatter_half(here.scatter_z(slots_apart(mixer_grad.astype(LOW), 4)))
        ),
        4,
    )

    def outside(values):
        return values.transpose(2, 0, 1).astype(WIDE)

    kernel_slots = kernel_grad.reshape(taps, depth, share).transpose(1, 0, 2)
    kernel_blocks = here.mirrored(kernel_slots, here.z).transpose(1, 0, 2)
    chosen = (jnp.arange(RANKS) == here.rank).astype(WIDE)
    kernel_whole = (kernel_blocks[:, :, None, :] * chosen[None, None, :, None]).reshape(
        taps, model_width
    )
    small = jnp.concatenate(
        [
            here.turn(jnp.stack([gain0, gain1, gain2, gain3])).reshape(-1),
            kernel_whole.reshape(-1),
            head_gains_grad.reshape(-1),
        ]
    )
    small = here.total(small)
    gain_size, kernel_size = 4 * model_width, taps * model_width
    return (
        output,
        input_grad,
        small[:gain_size].reshape(4, model_width),
        small[gain_size + kernel_size :].reshape(2, head_width),
        small[gain_size : gain_size + kernel_size].reshape(taps, model_width),
        outside(mixer_grad[:3]),
        mixer_grad[3].astype(WIDE),
        outside(first_inward_grad),
        first_outward_grad.astype(WIDE),
        outside(heads_grad[:, : heads_size - heads_rows]),
        heads_grad[:, heads_size - heads_rows :].reshape(attn_out.shape).astype(WIDE),
        outside(second_inward_grad),
        second_outward_grad.astype(WIDE),
    )


def solution(mesh):
    rows = P(("section", "dp"), None, "tensor")
    columns = P("tensor", ("section", "dp"))
    heads = P(("section", "dp"), "tensor", None)
    stream = P("section", "dp", "tensor")
    return jax.shard_map(
        local,
        mesh=mesh,
        in_specs=(
            stream,
            P("dp", None),
            P("section", None),
            P(),
            P(None, "tensor"),
            rows,
            columns,
            rows,
            columns,
            heads,
            columns,
            rows,
            columns,
            stream,
        ),
        out_specs=(
            stream,
            stream,
            P(),
            P(),
            P(),
            rows,
            columns,
            rows,
            columns,
            heads,
            columns,
            rows,
            columns,
        ),
        check_vma=False,
    )
```

profile of v0, /device:TPU:0, one launch (start us, length us, event | category | flops | bytes accessed | tf_op | source)
XLA Modules:
  0.0 1140.8 jit_solution(13361058593742643462)
XLA Ops:
  13.1 8.7 all-gather
  34.9 6.7 collective-permute-start.3
  43.3 18.8 %collective-permute-start.38 = (bf16[1,288,128]{2,1,0:T(8,128)(2,1)}, bf16[1,288,128]{2,1,0:T(8,128)(2,1)S(1)}, u32[]{:S(2)}, u32[]{:S(2)}) collective-permute-start(bf16[1,288,128]{2,1,0:T(8,128)(2,1)} %get-tuple-element.374), channel_id=1, source_target_pairs={{0,8},{1,9},{2,10},{3,11},{4,12},{5,13},{6,14},{7,15},{8,0},{9,1},... | collective-permute-start | bytes 221192 | tf_op jit(solution)/shard_map/ppermute | solution.py:45
  68.1 6.6 collective-permute-done.10
  87.1 6.5 collective-permute-done.12
  165.3 6.6 collective-permute-done.43
  222.9 7.4 collective-permute-done.34
  235.5 7.5 collective-permute-done.32
  244.4 7.1 collective-permute-done.36
  293.2 8.6 collective-permute-done.51
  322.8 7.2 collective-permute-start.106
  330.9 7.6 collective-permute-done.106
  346.9 10.8 collective-permute-done.64
  397.1 17.3 %attend.1 = bf16[2,2,1024,64]{3,2,1,0:T(8,128)(2,1)S(1)} custom-call(s32[1024,1]{1,0:T(8,128)S(1)} %copy-done.2, bf16[2,2,1024,64]{3,2,1,0:T(8,128)(2,1)S(1)} %fusion.81.queries_ref, bf16[2,2048,64]{2,1,0:T(8,128)(2,1)S(1)} %get-tuple-element.227.keys_ref, bf16[2,2048,64]{2,1,0:T(8,128)(2,1)S(1)} %get-tuple-element.226.values_ref), custom_call_target="tpu_custom_call" | custom-call | tf_op jit(solution)/shard_map/attend/pallas_call | solution.py:346
  429.6 8.4 collective-permute-start.75
  446.2 9.3 collective-permute-done.90
  521.4 11.3 collective-permute-done.79
  543.5 8.4 fusion.130
  551.9 9.1 multiply_convert_fusion.3
  572.4 7.2 fusion.16
  579.6 8.3 convolution_convert_fusion
  608.5 7.7 collective-permute-done.187
  634.0 7.8 collective-permute-start.188
  712.3 8.0 collective-permute-start.190
  727.8 24.5 %attend_back.1 = (bf16[2,2,1024,64]{3,2,1,0:T(8,128)(2,1)S(1)}, f32[2,2048,64]{2,1,0:T(8,128)}, f32[2,2048,64]{2,1,0:T(8,128)}) custom-call(s32[1024,1]{1,0:T(8,128)S(1)} %copy-done.3, bf16[2,2,1024,64]{3,2,1,0:T(8,128)(2,1)S(1)} %fusion.81.queries_ref, bf16[2,2048,64]{2,1,0:T(8,128)(2,1)S(1)} %get-tuple-element.227.keys_ref, ...), custom_call_target="tpu_custom_call" | custom-call | tf_op jit(solution)/shard_map/attend_back/pallas_call | solution.py:359
  794.7 9.6 collective-permute-done.174
  852.3 12.8 %collective-permute-done.195 = bf16[1,576,128]{2,1,0:T(8,128)(2,1)S(1)} collective-permute-done((bf16[1,576,128]{2,1,0:T(8,128)(2,1)S(1)}, bf16[1,576,128]{2,1,0:T(8,128)(2,1)S(1)}, u32[]{:S(2)}, u32[]{:S(2)}) %collective-permute-start.195) | collective-permute-done | bytes 147488 | tf_op jit(solution)/shard_map/ppermute | solution.py:45
  904.4 7.6 convolution_convert_fusion.1
  948.4 7.3 collective-permute-done.151
  994.5 6.5 collective-permute-done.156
  1011.2 10.0 collective-permute-done.124
  1092.6 7.2 collective-permute-done.142
  (1360 shorter events, 836.0 us)
Async XLA Ops:
  2.5 72.3 %collective-permute-start.37 = (bf16[1,288,128]{2,1,0:T(8,128)(2,1)}, bf16[1,288,128]{2,1,0:T(8,128)(2,1)S(1)}, u32[]{:S(2)}, u32[]{:S(2)}) collective-permute-start(bf16[1,288,128]{2,1,0:T(8,128)(2,1)} %get-tuple-element.372), channel_id=1, source_target_pairs={{0,1},{1,0},{2,3},{3,2},{4,5},{5,4},{6,7},{7,6},{8,9},{9,8},{10,11... | collective-permute-start | bytes 221192 | tf_op jit(solution)/shard_map/ppermute | solution.py:45
  8.7 32.9 %collective-permute-start.9 = (bf16[1,256,128]{2,1,0:T(8,128)(2,1)}, bf16[1,256,128]{2,1,0:T(8,128)(2,1)}, u32[]{:S(2)}, u32[]{:S(2)}) collective-permute-start(bf16[1,256,128]{2,1,0:T(8,128)(2,1)} %get-tuple-element.386), channel_id=1, source_target_pairs={{0,9},{1,8},{2,11},{3,10},{4,13},{5,12},{6,15},{7,14},{8,1},{9,0},... | collective-permute-start | bytes 196616 | tf_op jit(solution)/shard_map/ppermute | solution.py:45
  43.3 34.0 %collective-permute-start.38 = (bf16[1,288,128]{2,1,0:T(8,128)(2,1)}, bf16[1,288,128]{2,1,0:T(8,128)(2,1)S(1)}, u32[]{:S(2)}, u32[]{:S(2)}) collective-permute-start(bf16[1,288,128]{2,1,0:T(8,128)(2,1)} %get-tuple-element.374), channel_id=1, source_target_pairs={{0,8},{1,9},{2,10},{3,11},{4,12},{5,13},{6,14},{7,15},{8,0},{9,1},... | collective-permute-start | bytes 221192 | tf_op jit(solution)/shard_map/ppermute | solution.py:45
  104.9 43.6 %collective-permute-start.42 = (bf16[288,512]{1,0:T(8,128)(2,1)}, bf16[288,512]{1,0:T(8,128)(2,1)}, u32[]{:S(2)}, u32[]{:S(2)}) collective-permute-start(bf16[288,512]{1,0:T(8,128)(2,1)} %pad_maximum_fusion.71), channel_id=1, source_target_pairs={{2,0},{3,1},{4,2},{5,3},{6,4},{7,5},{10,8},{11,9},{12,10},{13,11},... | collective-permute-start | bytes 884744 | tf_op jit(solution)/shard_map/ppermute | solution.py:45
  116.1 38.3 %collective-permute-start.41 = (bf16[288,512]{1,0:T(8,128)(2,1)}, bf16[288,512]{1,0:T(8,128)(2,1)}, u32[]{:S(2)}, u32[]{:S(2)}) collective-permute-start(bf16[288,512]{1,0:T(8,128)(2,1)} %pad_maximum_fusion.71), channel_id=1, source_target_pairs={{0,2},{1,3},{2,4},{3,5},{4,6},{5,7},{8,10},{9,11},{10,12},{11,13},... | collective-permute-start | bytes 884744 | tf_op jit(solution)/shard_map/ppermute | solution.py:45
  120.6 38.5 %collective-permute-start.40 = (bf16[288,512]{1,0:T(8,128)(2,1)}, bf16[288,512]{1,0:T(8,128)(2,1)}, u32[]{:S(2)}, u32[]{:S(2)}) collective-permute-start(bf16[288,512]{1,0:T(8,128)(2,1)} %pad_maximum_fusion.71), channel_id=1, source_target_pairs={{0,16},{1,17},{2,18},{3,19},{4,20},{5,21},{6,22},{7,23},{8,24},{9,... | collective-permute-start | bytes 884744 | tf_op jit(solution)/shard_map/ppermute | solution.py:45
  146.2 36.8 %collective-permute-start.19 = (bf16[512,1024]{0,1:T(8,128)(2,1)}, bf16[512,1024]{0,1:T(8,128)(2,1)}, u32[]{:S(2)}, u32[]{:S(2)}) collective-permute-start(bf16[512,1024]{0,1:T(8,128)(2,1)} %pad_maximum_fusion.35), channel_id=1, source_target_pairs={{0,1},{1,0},{2,3},{3,2},{4,5},{5,4},{6,7},{7,6},{8,9},{9,8},{10,11... | collective-permute-start | bytes 3145736 | tf_op jit(solution)/shard_map/ppermute | solution.py:45
  204.9 63.8 %collective-permute-start.56 = (bf16[2,384,128]{2,1,0:T(8,128)(2,1)}, bf16[2,384,128]{2,1,0:T(8,128)(2,1)}, u32[]{:S(2)}, u32[]{:S(2)}) collective-permute-start(bf16[2,384,128]{2,1,0:T(8,128)(2,1)} %get-tuple-element.389), channel_id=1, source_target_pairs={{2,0},{3,1},{4,2},{5,3},{6,4},{7,5},{10,8},{11,9},{12,10},{13,11},... | collective-permute-start | bytes 589832 | tf_op jit(solution)/shard_map/ppermute | solution.py:45
  217.4 34.1 %collective-permute-start.36 = (bf16[576,512]{1,0:T(8,128)(2,1)}, bf16[576,512]{1,0:T(8,128)(2,1)S(1)}, u32[]{:S(2)}, u32[]{:S(2)}) collective-permute-start(bf16[576,512]{1,0:T(8,128)(2,1)} %add.677), channel_id=1, source_target_pairs={{0,16},{1,17},{2,18},{3,19},{4,20},{5,21},{6,22},{7,23},{8,24},{9,... | collective-permute-start | bytes 1769480 | tf_op jit(solution)/shard_map/ppermute | solution.py:45
  230.3 39.6 %collective-permute-start.55 = (bf16[2,384,128]{2,1,0:T(8,128)(2,1)}, bf16[2,384,128]{2,1,0:T(8,128)(2,1)S(1)}, u32[]{:S(2)}, u32[]{:S(2)}) collective-permute-start(bf16[2,384,128]{2,1,0:T(8,128)(2,1)} %get-tuple-element.389), channel_id=1, source_target_pairs={{0,2},{1,3},{2,4},{3,5},{4,6},{5,7},{8,10},{9,11},{10,12},{11,13},... | collective-permute-start | bytes 589832 | tf_op jit(solution)/shard_map/ppermute | solution.py:45
  243.0 96.4 %collective-permute-start.71 = (bf16[1,576,128]{2,1,0:T(8,128)(2,1)}, bf16[1,576,128]{2,1,0:T(8,128)(2,1)}, u32[]{:S(2)}, u32[]{:S(2)}) collective-permute-start(bf16[1,576,128]{2,1,0:T(8,128)(2,1)} %get-tuple-element.311), channel_id=1, source_target_pairs={{0,1},{1,0},{2,3},{3,2},{4,5},{5,4},{6,7},{7,6},{8,9},{9,8},{10,11... | collective-permute-start | bytes 442376 | tf_op jit(solution)/shard_map/ppermute | solution.py:45
  253.4 88.1 %collective-permute-start.72 = (bf16[1,576,128]{2,1,0:T(8,128)(2,1)}, bf16[1,576,128]{2,1,0:T(8,128)(2,1)}, u32[]{:S(2)}, u32[]{:S(2)}) collective-permute-start(bf16[1,576,128]{2,1,0:T(8,128)(2,1)} %get-tuple-element.310), channel_id=1, source_target_pairs={{0,8},{1,9},{2,10},{3,11},{4,12},{5,13},{6,14},{7,15},{8,0},{9,1},... | collective-permute-start | bytes 442376 | tf_op jit(solution)/shard_map/ppermute | solution.py:45
  310.7 35.9 %collective-permute-start.53 = (bf16[256,1024]{0,1:T(8,128)(2,1)}, bf16[256,1024]{0,1:T(8,128)(2,1)}, u32[]{:S(2)}, u32[]{:S(2)}) collective-permute-start(bf16[256,1024]{0,1:T(8,128)(2,1)} %fusion.61), channel_id=1, source_target_pairs={{0,8},{1,9},{2,10},{3,11},{4,12},{5,13},{6,14},{7,15},{8,0},{9,1},... | collective-permute-start | bytes 1572872 | tf_op jit(solution)/shard_map/ppermute | solution.py:45
  339.3 89.0 %collective-permute-start.103 = (bf16[256,256]{0,1:T(8,128)(2,1)}, bf16[256,256]{0,1:T(8,128)(2,1)}, u32[]{:S(2)}, u32[]{:S(2)}) collective-permute-start(bf16[256,256]{0,1:T(8,128)(2,1)} %bitcast.169), channel_id=1, source_target_pairs={{0,0},{1,16},{2,1},{3,17},{4,8},{5,24},{6,9},{7,25},{8,2},{9,18},{... | collective-permute-start | bytes 393224 | tf_op jit(solution)/shard_map/ppermute | solution.py:435
  341.5 88.1 %collective-permute-start.89 = (bf16[288,512]{1,0:T(8,128)(2,1)}, bf16[288,512]{1,0:T(8,128)(2,1)}, u32[]{:S(2)}, u32[]{:S(2)}) collective-permute-start(bf16[288,512]{1,0:T(8,128)(2,1)} %pad_maximum_fusion.72), channel_id=1, source_target_pairs={{2,0},{3,1},{4,2},{5,3},{6,4},{7,5},{10,8},{11,9},{12,10},{13,11},... | collective-permute-start | bytes 884744 | tf_op jit(solution)/shard_map/ppermute | solution.py:45
  357.7 81.5 %collective-permute-start.88 = (bf16[288,512]{1,0:T(8,128)(2,1)}, bf16[288,512]{1,0:T(8,128)(2,1)}, u32[]{:S(2)}, u32[]{:S(2)}) collective-permute-start(bf16[288,512]{1,0:T(8,128)(2,1)} %pad_maximum_fusion.72), channel_id=1, source_target_pairs={{0,2},{1,3},{2,4},{3,5},{4,6},{5,7},{8,10},{9,11},{10,12},{11,13},... | collective-permute-start | bytes 884744 | tf_op jit(solution)/shard_map/ppermute | solution.py:45
  362.9 77.7 %collective-permute-start.87 = (bf16[288,512]{1,0:T(8,128)(2,1)}, bf16[288,512]{1,0:T(8,128)(2,1)}, u32[]{:S(2)}, u32[]{:S(2)}) collective-permute-start(bf16[288,512]{1,0:T(8,128)(2,1)} %pad_maximum_fusion.72), channel_id=1, source_target_pairs={{0,16},{1,17},{2,18},{3,19},{4,20},{5,21},{6,22},{7,23},{8,24},{9,... | collective-permute-start | bytes 884744 | tf_op jit(solution)/shard_map/ppermute | solution.py:45
  427.4 44.1 %collective-permute-start.66 = (bf16[512,1024]{0,1:T(8,128)(2,1)}, bf16[512,1024]{0,1:T(8,128)(2,1)}, u32[]{:S(2)}, u32[]{:S(2)}) collective-permute-start(bf16[512,1024]{0,1:T(8,128)(2,1)} %pad_maximum_fusion.37), channel_id=1, source_target_pairs={{0,1},{1,0},{2,3},{3,2},{4,5},{5,4},{6,7},{7,6},{8,9},{9,8},{10,11... | collective-permute-start | bytes 3145736 | tf_op jit(solution)/shard_map/ppermute | solution.py:45
  508.8 32.3 %collective-permute-start.83 = (bf16[576,512]{1,0:T(8,128)(2,1)}, bf16[576,512]{1,0:T(8,128)(2,1)S(1)}, u32[]{:S(2)}, u32[]{:S(2)}) collective-permute-start(bf16[576,512]{1,0:T(8,128)(2,1)} %add.702), channel_id=1, source_target_pairs={{0,16},{1,17},{2,18},{3,19},{4,20},{5,21},{6,22},{7,23},{8,24},{9,... | collective-permute-start | bytes 1769480 | tf_op jit(solution)/shard_map/ppermute | solution.py:45
  515.4 36.5 %collective-permute-start.107 = (bf16[256,1024]{0,1:T(8,128)(2,1)}, bf16[256,1024]{0,1:T(8,128)(2,1)S(1)}, u32[]{:S(2)}, u32[]{:S(2)}) collective-permute-start(bf16[256,1024]{0,1:T(8,128)(2,1)} %maximum_select_fusion.3), channel_id=1, source_target_pairs={{0,1},{1,0},{2,3},{3,2},{4,5},{5,4},{6,7},{7,6},{8,9},{9,8},{10,11... | collective-permute-start | bytes 1572872 | tf_op jit(solution)/shard_map/ppermute | solution.py:45
  598.9 33.8 %collective-permute-start.197 = (bf16[288,512]{1,0:T(8,128)(2,1)S(1)}, bf16[288,512]{1,0:T(8,128)(2,1)S(1)}, u32[]{:S(2)}, u32[]{:S(2)}) collective-permute-start(bf16[288,512]{1,0:T(8,128)(2,1)S(1)} %slice.1013), channel_id=1, source_target_pairs={{0,16},{1,17},{2,18},{3,19},{4,20},{5,21},{6,22},{7,23},{8,24},{9,... | collective-permute-start | bytes 884744 | tf_op jit(solution)/shard_map/ppermute | solution.py:45
  630.4 177.7 %collective-permute-start.184 = (bf16[576,512]{1,0:T(8,128)(2,1)}, bf16[576,512]{1,0:T(8,128)(2,1)}, u32[]{:S(2)}, u32[]{:S(2)}) collective-permute-start(bf16[576,512]{1,0:T(8,128)(2,1)} %slice.997), channel_id=1, source_target_pairs={{0,16},{1,17},{2,18},{3,19},{4,20},{5,21},{6,22},{7,23},{8,24},{9,... | collective-permute-start | bytes 1769480 | tf_op jit(solution)/shard_map/ppermute | solution.py:45
  653.7 56.3 %collective-permute-start.189 = (bf16[576,512]{1,0:T(8,128)(2,1)}, bf16[576,512]{1,0:T(8,128)(2,1)}, u32[]{:S(2)}, u32[]{:S(2)}) collective-permute-start(bf16[576,512]{1,0:T(8,128)(2,1)} %get-tuple-element.244), channel_id=1, source_target_pairs={{0,2},{1,3},{2,4},{3,5},{4,6},{5,7},{8,10},{9,11},{10,12},{11,13},... | collective-permute-start | bytes 1769480 | tf_op jit(solution)/shard_map/ppermute | solution.py:45
  658.4 128.7 %collective-permute-start.192 = (bf16[576,512]{1,0:T(8,128)(2,1)}, bf16[576,512]{1,0:T(8,128)(2,1)}, u32[]{:S(2)}, u32[]{:S(2)}) collective-permute-start(bf16[576,512]{1,0:T(8,128)(2,1)} %get-tuple-element.245), channel_id=1, source_target_pairs={{2,0},{3,1},{4,2},{5,3},{6,4},{7,5},{10,8},{11,9},{12,10},{13,11},... | collective-permute-start | bytes 1769480 | tf_op jit(solution)/shard_map/ppermute | solution.py:45
  674.8 33.8 %collective-permute-start.113 = (bf16[256,1024]{0,1:T(8,128)(2,1)}, bf16[256,1024]{0,1:T(8,128)(2,1)}, u32[]{:S(2)}, u32[]{:S(2)}) collective-permute-start(bf16[256,1024]{0,1:T(8,128)(2,1)} %get-tuple-element.321), channel_id=1, source_target_pairs={{0,8},{1,9},{2,10},{3,11},{4,12},{5,13},{6,14},{7,15},{8,0},{9,1},... | collective-permute-start | bytes 1572872 | tf_op jit(solution)/shard_map/ppermute | solution.py:45
  712.3 95.9 %collective-permute-start.190 = (bf16[576,512]{1,0:T(8,128)(2,1)}, bf16[576,512]{1,0:T(8,128)(2,1)}, u32[]{:S(2)}, u32[]{:S(2)}) collective-permute-start(bf16[576,512]{1,0:T(8,128)(2,1)} %add_convert_fusion.5), channel_id=1, source_target_pairs={{0,2},{1,3},{2,4},{3,5},{4,6},{5,7},{8,10},{9,11},{10,12},{11,13},... | collective-permute-start | bytes 1769480 | tf_op jit(solution)/shard_map/ppermute | solution.py:45
  794.7 33.5 %collective-permute-start.116 = (bf16[512,1024]{0,1:T(8,128)(2,1)}, bf16[512,1024]{0,1:T(8,128)(2,1)S(1)}, u32[]{:S(2)}, u32[]{:S(2)}) collective-permute-start(bf16[512,1024]{0,1:T(8,128)(2,1)} %pad_maximum_fusion.40), channel_id=1, source_target_pairs={{0,1},{1,0},{2,3},{3,2},{4,5},{5,4},{6,7},{7,6},{8,9},{9,8},{10,11... | collective-permute-start | bytes 3145736 | tf_op jit(solution)/shard_map/ppermute | solution.py:45
  888.7 32.9 %collective-permute-start.163 = (bf16[288,512]{1,0:T(8,128)(2,1)}, bf16[288,512]{1,0:T(8,128)(2,1)}, u32[]{:S(2)}, u32[]{:S(2)}) collective-permute-start(bf16[288,512]{1,0:T(8,128)(2,1)} %slice.975), channel_id=1, source_target_pairs={{0,16},{1,17},{2,18},{3,19},{4,20},{5,21},{6,22},{7,23},{8,24},{9,... | collective-permute-start | bytes 884744 | tf_op jit(solution)/shard_map/ppermute | solution.py:45
  921.5 37.8 %collective-permute-start.121 = (bf16[512,1024]{0,1:T(8,128)(2,1)S(1)}, bf16[512,1024]{0,1:T(8,128)(2,1)S(1)}, u32[]{:S(2)}, u32[]{:S(2)}) collective-permute-start(bf16[512,1024]{0,1:T(8,128)(2,1)S(1)} %pad_maximum_fusion.41), channel_id=1, source_target_pairs={{0,1},{1,0},{2,3},{3,2},{4,5},{5,4},{6,7},{7,6},{8,9},{9,8},{10,11... | collective-permute-start | bytes 3145736 | tf_op jit(solution)/shard_map/ppermute | solution.py:45
  939.4 33.5 %collective-permute-start.150 = (bf16[576,512]{1,0:T(8,128)(2,1)}, bf16[576,512]{1,0:T(8,128)(2,1)}, u32[]{:S(2)}, u32[]{:S(2)}) collective-permute-start(bf16[576,512]{1,0:T(8,128)(2,1)} %slice.959), channel_id=1, source_target_pairs={{0,16},{1,17},{2,18},{3,19},{4,20},{5,21},{6,22},{7,23},{8,24},{9,... | collective-permute-start | bytes 1769480 | tf_op jit(solution)/shard_map/ppermute | solution.py:45
  966.3 55.0 %collective-permute-start.148 = (bf16[576,512]{1,0:T(8,128)(2,1)}, bf16[576,512]{1,0:T(8,128)(2,1)}, u32[]{:S(2)}, u32[]{:S(2)}) collective-permute-start(bf16[576,512]{1,0:T(8,128)(2,1)} %slice.953), channel_id=1, source_target_pairs={{0,16},{1,17},{2,18},{3,19},{4,20},{5,21},{6,22},{7,23},{8,24},{9,... | collective-permute-start | bytes 1769480 | tf_op jit(solution)/shard_map/ppermute | solution.py:45
  989.1 32.2 %collective-permute-start.154 = (bf16[576,512]{1,0:T(8,128)(2,1)}, bf16[576,512]{1,0:T(8,128)(2,1)}, u32[]{:S(2)}, u32[]{:S(2)}) collective-permute-start(bf16[576,512]{1,0:T(8,128)(2,1)} %add_convert_fusion.14), channel_id=1, source_target_pairs={{0,2},{1,3},{2,4},{3,5},{4,6},{5,7},{8,10},{9,11},{10,12},{11,13},... | collective-permute-start | bytes 1769480 | tf_op jit(solution)/shard_map/ppermute | solution.py:45
  (417 other events, 6425.3 us)
where the time goes:
time: 1160 us; the launch traced here: 1140 us
  starting transfers between devices  399 us (34%)
  waiting for transfers between devices  279 us (24%)
  other arithmetic  181 us (16%)
  local copies, waits for them, and re-layouts  131 us (11%)
  matrix products  94.8 us (8%)
  Pallas kernels  41.7 us (4%)
    ppermute x194, starting transfers between devices, move(): return lax.ppermute(values, AXES, route)  347 us
    ppermute x194, waiting for transfers between devices, move(): return lax.ppermute(values, AXES, route)  253 us
    unnamed x553, local copies, waits for them, and re-layouts  52.2 us
    dot_general x8, matrix products, times_rows(): lax.dot_general(a, b, (((1,), (1,)), ((), ())), preferred_element_type=WIDE)  35.6 us
    dot_general x8, matrix products, columns_times(): lax.dot_general(a, b, (((0,), (0,)), ((), ())), preferred_element_type=WIDE)  34.1 us
    ppermute x8, starting transfers between devices, rows_in(): pieces.append(lax.ppermute(piece, AXES, sorted(flat_goal(k).items())))  26.6 us
    ppermute x8, starting transfers between devices, rows_out(): pieces.append(lax.ppermute(piece, AXES, route))  25.4 us
    dot_general x8, matrix products, times(): lax.dot_general(a, b, (((1,), (0,)), ((), ())), preferred_element_type=WIDE)  25.1 us
  transfers between devices with their start and end apart: 210, of which 70 were waited for; matrix products, arithmetic and copies ran while one was open for 30% of the time, Pallas kernels for 4%

commit v1 on v0

v1 whole, which is shorter than its diff:
```python
import functools

import jax
import jax.numpy as jnp
from jax import lax
from jax.experimental import pallas as pl
from jax.experimental.pallas import tpu as pltpu
from jax.sharding import Mesh
from jax.sharding import PartitionSpec as P

EPSILON = 1e-05
ROTARY_BASE = 1000000.0
NEGATIVE = -1e30
AXES = ("half", "side", "depth", "ring", "core")
SQUARE = ("half", "side", "ring", "core")
LOW = jnp.bfloat16
WIDE = jnp.float32
RANKS = 4
LONGEST = 1024


class Place:
    def __init__(self):
        self.halves = lax.axis_size("half")
        self.depth = lax.axis_size("depth")
        self.rings = lax.axis_size("ring")
        self.half = lax.axis_index("half")
        self.side = lax.axis_index("side")
        self.z = lax.axis_index("depth")
        self.ring = lax.axis_index("ring")
        self.core = lax.axis_index("core")
        self.rank = 2 * self.side + self.core

    def places(self):
        return [
            (half, side, z, ring, core)
            for half in range(self.halves)
            for side in range(2)
            for z in range(self.depth)
            for ring in range(self.rings)
            for core in range(2)
        ]

    def flat(self, half, side, z, ring, core):
        return (((half * 2 + side) * self.depth + z) * self.rings + ring) * 2 + core

    def route(self, target):
        pairs = [(place, target(*place)) for place in self.places()]
        return [(self.flat(*a), self.flat(*b)) for a, b in pairs if b is not None]

    def move(self, values, target):
        return lax.ppermute(values, AXES, self.route(target))

    def to_rank(self, values, k):
        return self.move(
            values, lambda half, side, z, ring, core: (half, side ^ (k >> 1), z, ring, core ^ (k & 1))
        )

    def up(self, values, distance=1):
        return self.move(
            values,
            lambda half, side, z, ring, core: (half, side, z + distance, ring, core)
            if 0 <= z + distance < self.depth
            else None,
        )

    def by_rank(self, blocks):
        return [
            lax.select_n(jnp.bitwise_xor(self.rank, b), *blocks) for b in range(RANKS)
        ]

    def mirrored(self, stacked, place):
        count = stacked.shape[0]
        flipped = jnp.concatenate([stacked[:1], stacked[:0:-1]], axis=0)
        return lax.dynamic_slice_in_dim(
            jnp.concatenate([flipped, flipped], axis=0), count - place, count, 0
        )

    def rolled(self, stacked, place):
        count = stacked.shape[0]
        return lax.dynamic_slice_in_dim(
            jnp.concatenate([stacked, stacked], axis=0), count - place, count, 0
        )

    def to_half(self, values):
        return self.move(
            values, lambda half, side, z, ring, core: (1 - half, side, z, ring, core)
        )

    def gather_teams(self, values):
        return lax.all_gather(values, ("half", "ring", "depth"), axis=0, tiled=True)

    def gather_rest(self, values):
        return lax.all_gather(values, ("ring", "depth"), axis=0, tiled=True)

    def scatter_half(self, values, *due):
        kept = lax.dynamic_index_in_dim(values, self.half, 0, keepdims=False)
        sent = lax.dynamic_index_in_dim(values, 1 - self.half, 0, keepdims=False)
        came = after(self.to_half(sent), *due)
        return (kept.astype(WIDE) + came.astype(WIDE)).astype(LOW)

    def scatter_teams(self, values):
        return lax.psum_scatter(
            values, ("half", "ring", "depth"), scatter_dimension=0, tiled=True
        )

    def scatter_rest(self, values):
        return lax.psum_scatter(values, ("ring", "depth"), scatter_dimension=0, tiled=True)

    def whole_columns(self, parts):
        parts = lax.all_to_all(parts, SQUARE, 0, 0, tiled=True)
        return parts.transpose(1, 0, 2).reshape(parts.shape[1], -1)

    def whole_rows(self, *packs):
        blocks = lax.axis_size(SQUARE)
        values = jnp.concatenate([pack for pack, _ in packs], axis=0)
        rows, columns = values.shape
        parts = values.reshape(rows, blocks, columns // blocks).transpose(1, 0, 2)
        parts = lax.all_to_all(parts, SQUARE, 0, 0, tiled=True)
        found, low = [], 0
        for pack, kinds in packs:
            share = pack.shape[0] // kinds
            part = parts[:, low : low + kinds * share].reshape(blocks, kinds, share, -1)
            found.append(part.transpose(1, 0, 2, 3).reshape(kinds, blocks * share, -1))
            low += kinds * share
        return found

    def gather_rows(self, values, *due):
        mate = self.to_rank(values, 1)
        across = after(self.to_rank(values, 2), *due)
        return [values, mate, across, self.to_rank(across, 1)]

    def scatter_rows(self, blocks, waiting=(), due=()):
        rows = blocks[0].shape[0]
        came = self.to_rank(jnp.concatenate([blocks[1], blocks[3]], axis=0).astype(LOW), 1)
        came, *waiting = lax.optimization_barrier((came, *waiting))
        across = (blocks[2].astype(WIDE) + came[rows:].astype(WIDE)).astype(LOW)
        own = blocks[0].astype(WIDE) + came[:rows].astype(WIDE)
        across = after(self.to_rank(across, 2), *due)
        return own + across.astype(WIDE), waiting

    def gather_square(self, values, *due):
        beside, opposite = self.to_rank(values, 2), self.to_half(values)
        rows = values.shape[0] // 2
        diagonal = jnp.concatenate(
            [self.to_half(beside[:rows]), self.to_rank(opposite[rows:], 2)], axis=0
        )
        diagonal = after(diagonal, *due)
        blocks = [values, beside, opposite, diagonal]
        return blocks + [self.to_rank(block, 1) for block in blocks]

    def scatter_square(self, values, waiting=(), due=()):
        size = values.shape[0] // 8
        rows = size // 2
        came = self.to_rank(values[4 * size :], 1)
        came, *waiting = lax.optimization_barrier((came, *waiting))
        sums = values[: 4 * size].astype(WIDE) + came.astype(WIDE)
        own, beside, opposite, diagonal = [sums[k * size : (k + 1) * size] for k in range(4)]
        diagonal = diagonal.astype(LOW)
        first = self.to_half(diagonal[:rows]).astype(WIDE)
        second = self.to_rank(diagonal[rows:], 2).astype(WIDE)
        beside = jnp.concatenate([beside[:rows] + first, beside[rows:]], axis=0).astype(LOW)
        opposite = jnp.concatenate([opposite[:rows], opposite[rows:] + second], axis=0).astype(LOW)
        beside, opposite = self.to_rank(beside, 2), self.to_half(opposite)
        beside = after(beside, *due)
        return own + beside.astype(WIDE) + opposite.astype(WIDE), waiting

    def total(self, values):
        sizes = (self.halves, 2, self.depth, self.rings, 2)
        for axis, size in enumerate(sizes):
            bit = 1
            while bit < size:
                values = values + self.move(
                    values, lambda *place: (*place[:axis], place[axis] ^ bit, *place[axis + 1 :])
                )
                bit *= 2
        return values


def after(values, *others):
    return lax.optimization_barrier((values, *others))[0]


def times(a, b):
    return lax.dot_general(a, b, (((1,), (0,)), ((), ())), preferred_element_type=WIDE)


def times_rows(a, b):
    return lax.dot_general(a, b, (((1,), (1,)), ((), ())), preferred_element_type=WIDE)


def columns_times(a, b):
    return lax.dot_general(a, b, (((0,), (0,)), ((), ())), preferred_element_type=WIDE)


def root_norm(values, gain_row):
    return (
        values * lax.rsqrt(jnp.mean(values * values, axis=-1, keepdims=True) + EPSILON) * gain_row
    )


def root_norm_back(inputs, gain_row, grad, arriving):
    widened = inputs.astype(WIDE)
    inverse = lax.rsqrt(jnp.mean(widened * widened, axis=-1, keepdims=True) + EPSILON)
    unit_rows = widened * inverse
    scaled = grad * gain_row
    through = inverse * (scaled - unit_rows * jnp.mean(scaled * unit_rows, axis=-1, keepdims=True))
    gain_grad = jnp.sum(grad * unit_rows, axis=0)
    return ((arriving.astype(WIDE) + through).astype(LOW), gain_grad)


def angles(offsets, head_width):
    inverse = ROTARY_BASE ** (-jnp.arange(0, head_width, 2).astype(WIDE) / head_width)
    phases = offsets.astype(WIDE)[:, None] * inverse[None, :]
    return (jnp.tile(jnp.cos(phases), (1, 4)), jnp.tile(jnp.sin(phases), (1, 4)))


def lanes(shape):
    return lax.broadcasted_iota(jnp.int32, shape, len(shape) - 1)


def pair_mean(values):
    width = values.shape[-1] // 2
    first = lanes(values.shape) < width
    low = jnp.sum(jnp.where(first, values, 0), axis=-1, keepdims=True)
    high = jnp.sum(jnp.where(first, 0, values), axis=-1, keepdims=True)
    return jnp.where(first, low, high) / width


def turned(values):
    width = values.shape[-1]
    quarter = width // 4
    ahead = pltpu.roll(values, width - quarter, 1)
    behind = pltpu.roll(values, quarter, 1)
    return jnp.where(lanes(values.shape) % (width // 2) < quarter, -ahead, behind)


def unit_pair(values):
    inverse = lax.rsqrt(pair_mean(values * values) + EPSILON)
    return values * inverse, inverse


def rotated(values, gain_row, cosine, sine):
    unit, _ = unit_pair(values)
    scaled = unit * gain_row
    return scaled * cosine + turned(scaled) * sine


def rotated_back(values, gain_row, cosine, sine, grad):
    unit, inverse = unit_pair(values)
    scaled_grad = grad * cosine - turned(grad * sine)
    unit_grad = scaled_grad * gain_row
    result = inverse * (unit_grad - unit * pair_mean(unit_grad * unit))
    return result, jnp.sum(scaled_grad * unit, axis=0, keepdims=True)


def heads_kernel(packed_ref, gains_ref, cosine_ref, sine_ref, queries_ref, pairs_ref):
    width = cosine_ref.shape[1]
    cosine, sine = cosine_ref[...], sine_ref[...]
    for g in range(packed_ref.shape[1] // (2 * width)):
        own = slice(g * width, (g + 1) * width)
        values = packed_ref[:, 2 * g * width : (2 * g + 1) * width]
        queries_ref[:, own] = rotated(values, gains_ref[0:1], cosine, sine).astype(LOW)
        values = packed_ref[:, (2 * g + 1) * width : (2 * g + 2) * width]
        keys = rotated(values, gains_ref[1:2], cosine, sine)
        first = lanes(values.shape) < width // 2
        pairs_ref[:, own] = jnp.where(first, keys, values).astype(LOW)


def heads_back_kernel(
    packed_ref, gains_ref, cosine_ref, sine_ref, queries_grad_ref, pairs_grad_ref, out_ref, gain_ref
):
    width = cosine_ref.shape[1]
    cosine, sine = cosine_ref[...], sine_ref[...]

    @pl.when(pl.program_id(0) == 0)
    def _():
        gain_ref[...] = jnp.zeros_like(gain_ref)

    for g in range(packed_ref.shape[1] // (2 * width)):
        own = slice(g * width, (g + 1) * width)
        for part, grad_ref in ((0, queries_grad_ref), (1, pairs_grad_ref)):
            place = slice((2 * g + part) * width, (2 * g + part + 1) * width)
            grad = grad_ref[:, own].astype(WIDE)
            result, gain_grad = rotated_back(
                packed_ref[:, place], gains_ref[part : part + 1], cosine, sine, grad
            )
            if part:
                result = jnp.where(lanes(result.shape) < width // 2, result, grad)
            out_ref[:, place] = result.astype(LOW)
            gain_ref[part : part + 1] += gain_grad


def split_heads(packed, gains, cosine, sine, rows):
    total, columns = packed.shape
    width = cosine.shape[1]
    row_block = lambda size: pl.BlockSpec((rows, size), lambda i: (i, 0))
    return pl.pallas_call(
        heads_kernel,
        grid=(total // rows,),
        in_specs=[
            row_block(columns),
            pl.BlockSpec((2, width), lambda i: (0, 0)),
            row_block(width),
            row_block(width),
        ],
        out_specs=[row_block(columns // 2), row_block(columns // 2)],
        out_shape=[jax.ShapeDtypeStruct((total, columns // 2), LOW)] * 2,
        compiler_params=pltpu.CompilerParams(vmem_limit_bytes=48 << 20),
        name="heads",
    )(packed, gains, cosine, sine)


def split_heads_back(packed, gains, cosine, sine, queries_grad, pairs_grad, rows):
    total, columns = packed.shape
    width = cosine.shape[1]
    row_block = lambda size: pl.BlockSpec((rows, size), lambda i: (i, 0))
    return pl.pallas_call(
        heads_back_kernel,
        grid=(total // rows,),
        in_specs=[
            row_block(columns),
            pl.BlockSpec((2, width), lambda i: (0, 0)),
            row_block(width),
            row_block(width),
            row_block(columns // 2),
            row_block(columns // 2),
        ],
        out_specs=[row_block(columns), pl.BlockSpec((2, width), lambda i: (0, 0))],
        out_shape=[
            jax.ShapeDtypeStruct((total, columns), LOW),
            jax.ShapeDtypeStruct((2, width), WIDE),
        ],
        compiler_params=pltpu.CompilerParams(vmem_limit_bytes=48 << 20),
        name="heads_back",
    )(packed, gains, cosine, sine, queries_grad, pairs_grad)


def block_weights(offsets, queries, keys, scale):
    scores = (
        lax.dot_general(queries, keys, (((1,), (1,)), ((), ())), preferred_element_type=WIDE)
        * scale
    )
    rows, window = offsets.shape[0], keys.shape[0]
    shape = (rows, window)
    back = (
        lax.broadcasted_iota(jnp.int32, shape, 0)
        + LONGEST
        - lax.broadcasted_iota(jnp.int32, shape, 1)
    )
    allowed = (back >= 0) & (back <= offsets)
    allowed = jnp.concatenate([allowed.astype(WIDE)] * (queries.shape[0] // rows), axis=0) > 0.5
    scores = jnp.where(allowed, scores, NEGATIVE)
    weights = jnp.exp(scores - jnp.max(scores, axis=-1, keepdims=True))
    return weights / jnp.sum(weights, axis=-1, keepdims=True)


def over(values):
    width = values.shape[1] // 2
    return jnp.concatenate([values[:, :width], values[:, width:]], axis=0)


def beside(values):
    rows = values.shape[0] // 2
    return jnp.concatenate([values[:rows], values[rows:]], axis=1)


def attend_kernel(scale, offsets_ref, queries_ref, pairs_ref, out_ref):
    rows, width = queries_ref.shape[0], queries_ref.shape[1] // 2
    low = pl.multiple_of(pl.program_id(1) * rows, rows)
    pairs = pairs_ref[pl.ds(low, LONGEST + rows), :]
    weights = block_weights(offsets_ref[...], over(queries_ref[...]), pairs[:, :width], scale)
    result = jnp.dot(weights.astype(LOW), pairs[:, width:], preferred_element_type=WIDE)
    out_ref[...] = beside(result.astype(LOW))


def attend_back_kernel(
    scale, offsets_ref, queries_ref, pairs_ref, grad_ref, queries_grad_ref, pairs_grad_ref
):
    rows, width = queries_ref.shape[0], queries_ref.shape[1] // 2

    @pl.when(pl.program_id(1) == 0)
    def _():
        pairs_grad_ref[...] = jnp.zeros_like(pairs_grad_ref)

    low = pl.multiple_of(pl.program_id(1) * rows, rows)
    window = pl.ds(low, LONGEST + rows)
    queries, grad = over(queries_ref[...]), over(grad_ref[...])
    pairs = pairs_ref[window, :]
    keys, values = pairs[:, :width], pairs[:, width:]
    weights = block_weights(offsets_ref[...], queries, keys, scale)
    flow = lax.dot_general(grad, values, (((1,), (1,)), ((), ())), preferred_element_type=WIDE)
    inner = jnp.sum(weights * flow, axis=-1, keepdims=True)
    score_grad = (weights * (flow - inner)).astype(LOW)
    values_grad = lax.dot_general(
        weights.astype(LOW), grad, (((0,), (0,)), ((), ())), preferred_element_type=WIDE
    )
    keys_grad = lax.dot_general(
        score_grad, queries, (((0,), (0,)), ((), ())), preferred_element_type=WIDE
    )
    pairs_grad_ref[window, :] += jnp.concatenate([keys_grad * scale, values_grad], axis=1)
    queries_grad = jnp.dot(score_grad, keys, preferred_element_type=WIDE) * scale
    queries_grad_ref[...] = beside(queries_grad.astype(LOW))


def attention_specs(queries, pairs, rows, head_width):
    width = 2 * head_width
    grid = (queries.shape[1] // width, queries.shape[0] // rows)
    offsets_spec = pl.BlockSpec((rows, 1), lambda g, i: (i, 0))
    rows_spec = pl.BlockSpec((rows, width), lambda g, i: (i, g))
    pairs_spec = pl.BlockSpec((pairs.shape[0], width), lambda g, i: (0, g))
    return (grid, offsets_spec, rows_spec, pairs_spec)


def attend(offsets, queries, pairs, rows, head_width):
    grid, offsets_spec, rows_spec, pairs_spec = attention_specs(queries, pairs, rows, head_width)
    return pl.pallas_call(
        functools.partial(attend_kernel, head_width ** (-0.5)),
        grid=grid,
        in_specs=[offsets_spec, rows_spec, pairs_spec],
        out_specs=rows_spec,
        out_shape=jax.ShapeDtypeStruct(queries.shape, LOW),
        compiler_params=pltpu.CompilerParams(vmem_limit_bytes=48 << 20),
        name="attend",
    )(offsets[:, None], queries, pairs)


def attend_back(offsets, queries, pairs, grad, rows, head_width):
    grid, offsets_spec, rows_spec, pairs_spec = attention_specs(queries, pairs, rows, head_width)
    return pl.pallas_call(
        functools.partial(attend_back_kernel, head_width ** (-0.5)),
        grid=grid,
        in_specs=[offsets_spec, rows_spec, pairs_spec, rows_spec],
        out_specs=[rows_spec, pairs_spec],
        out_shape=[
            jax.ShapeDtypeStruct(queries.shape, LOW),
            jax.ShapeDtypeStruct(pairs.shape, WIDE),
        ],
        compiler_params=pltpu.CompilerParams(vmem_limit_bytes=48 << 20),
        name="attend_back",
    )(offsets[:, None], queries, pairs, grad)


def whole_rows_of(ref):
    teams, rows, columns = ref.shape
    return ref[...].reshape(teams * rows, columns)


def dot_nt(a, b):
    return lax.dot_general(a, b, (((1,), (1,)), ((), ())), preferred_element_type=WIDE)


def feed_kernel(
    normed_ref, gate_ref, up_ref, outward_ref, gated_ref, raised_ref, hidden_ref, update_ref
):
    normed = normed_ref[...]
    gate = dot_nt(normed, whole_rows_of(gate_ref))
    up = dot_nt(normed, whole_rows_of(up_ref))
    gated_ref[...] = gate.astype(LOW)
    raised_ref[...] = up.astype(LOW)
    hidden = (gate / (1 + jnp.exp(-gate)) * up).astype(LOW)
    hidden_ref[...] = hidden
    update_ref[...] = jnp.dot(
        hidden, whole_rows_of(outward_ref), preferred_element_type=WIDE
    ).astype(LOW)


def feed_back_kernel(
    full_ref,
    gated_ref,
    raised_ref,
    gate_ref,
    up_ref,
    outward_ref,
    gate_grad_ref,
    up_grad_ref,
    update_ref,
):
    hidden_grad = dot_nt(full_ref[...], whole_rows_of(outward_ref))
    gate = gated_ref[...].astype(WIDE)
    up = raised_ref[...].astype(WIDE)
    sigmoid = 1 / (1 + jnp.exp(-gate))
    through = hidden_grad * sigmoid
    gate_grad = (through * up * (1 + gate * (1 - sigmoid))).astype(LOW)
    up_grad = (through * gate).astype(LOW)
    gate_grad_ref[...] = gate_grad
    up_grad_ref[...] = up_grad
    update = jnp.dot(gate_grad, whole_rows_of(gate_ref), preferred_element_type=WIDE)
    update += jnp.dot(up_grad, whole_rows_of(up_ref), preferred_element_type=WIDE)
    update_ref[...] = update.astype(LOW)


def feed_grads_kernel(
    gate_grad_ref, up_grad_ref, hidden_ref, normed_ref, full_ref, out_ref, total_ref
):
    teams, rows, columns = out_ref.shape
    width, step = teams * rows, 128

    def fill(left_ref, right_ref):
        for low in range(0, width, step):
            own = slice(low, min(low + step, width))
            total_ref[own] = lax.dot_general(
                left_ref[:, own],
                right_ref[...],
                (((0,), (0,)), ((), ())),
                preferred_element_type=WIDE,
            )
        out_ref[...] = total_ref[...].astype(LOW).reshape(teams, rows, columns)

    pl.when(pl.program_id(0) == 0)(lambda: fill(gate_grad_ref, normed_ref))
    pl.when(pl.program_id(0) == 1)(lambda: fill(up_grad_ref, normed_ref))
    pl.when(pl.program_id(0) == 2)(lambda: fill(hidden_ref, full_ref))


def kind_spec(pack, k):
    teams, _, rows, columns = pack.shape
    return pl.BlockSpec((teams, None, rows, columns), lambda i: (0, k, 0, 0))


def row_spec(rows, columns):
    return pl.BlockSpec((rows, columns), lambda i: (i, 0))


def feed_call(normed, pack, rows):
    total, columns = normed.shape
    width = pack.shape[0] * pack.shape[2]
    wide = jax.ShapeDtypeStruct((total, width), LOW)
    return pl.pallas_call(
        feed_kernel,
        grid=(total // rows,),
        in_specs=[row_spec(rows, columns)] + [kind_spec(pack, k) for k in range(3)],
        out_specs=[row_spec(rows, width)] * 3 + [row_spec(rows, columns)],
        out_shape=[wide] * 3 + [jax.ShapeDtypeStruct((total, columns), LOW)],
        compiler_params=pltpu.CompilerParams(vmem_limit_bytes=48 << 20),
        name="feed",
    )(normed, pack, pack, pack)


def feed_back_call(full, gated, raised, pack, rows):
    total, columns = full.shape
    width = gated.shape[1]
    wide = jax.ShapeDtypeStruct((total, width), LOW)
    return pl.pallas_call(
        feed_back_kernel,
        grid=(total // rows,),
        in_specs=[row_spec(rows, columns)]
        + [row_spec(rows, width)] * 2
        + [kind_spec(pack, k) for k in range(3)],
        out_specs=[row_spec(rows, width)] * 2 + [row_spec(rows, columns)],
        out_shape=[wide] * 2 + [jax.ShapeDtypeStruct((total, columns), LOW)],
        compiler_params=pltpu.CompilerParams(vmem_limit_bytes=48 << 20),
        name="feed_back",
    )(full, gated, raised, pack, pack, pack)


def feed_grads_call(gate_grad, up_grad, hidden, normed, full, teams):
    total, columns = normed.shape
    width = hidden.shape[1]
    wide_spec = pl.BlockSpec((total, width), lambda k: (0, 0))
    rows_spec = pl.BlockSpec((total, columns), lambda k: (0, 0))
    return pl.pallas_call(
        feed_grads_kernel,
        grid=(3,),
        in_specs=[wide_spec] * 3 + [rows_spec] * 2,
        out_specs=pl.BlockSpec((teams, None, width // teams, columns), lambda k: (0, k, 0, 0)),
        out_shape=jax.ShapeDtypeStruct((teams, 3, width // teams, columns), LOW),
        scratch_shapes=[pltpu.VMEM((width, columns), WIDE)],
        compiler_params=pltpu.CompilerParams(vmem_limit_bytes=58 << 20),
        name="feed_grads",
    )(gate_grad, up_grad, hidden, normed, full)


def local(
    tokens,
    lengths,
    gains,
    qk_gains,
    conv_kernel,
    conv_in,
    conv_out,
    ffn1_in,
    ffn1_out,
    attn_qkv,
    attn_out,
    ffn2_in,
    ffn2_out,
    cotangent,
):
    here = Place()
    depth = here.depth
    stretch = tokens.shape[1]
    slice_width = tokens.shape[2]
    model_width = slice_width * depth
    sections = 2 * here.halves
    stream_rows = sections * stretch
    team_rows = stream_rows // depth
    own_rows = team_rows // RANKS
    head_width = attn_qkv.shape[2] // 4
    groups_here = attn_qkv.shape[1]
    groups = groups_here * depth // RANKS
    block_width = conv_in.shape[0]
    query_rows = min(256, team_rows)
    spare = depth // RANKS

    def row_goal(k):
        def goal(half, side, z, ring, core):
            part = (z + k) % depth
            rank = part % RANKS
            batch = half * 2 + side
            return (core, rank // 2, batch * spare + part // RANKS, ring, rank % 2)

        return goal

    own_part = (here.z % spare) * RANKS + here.rank

    def row_pieces(values):
        grid = values.reshape(depth, own_rows, slice_width)
        return [
            here.move(
                lax.dynamic_index_in_dim(grid, (here.z + k) % depth, 0, keepdims=False),
                row_goal(k),
            )
            for k in range(depth)
        ]

    def rows_in(pieces):
        columns = here.mirrored(jnp.stack(lax.optimization_barrier(tuple(pieces))), own_part)
        return columns.transpose(1, 0, 2).reshape(own_rows, model_width)

    def rows_out(*arrays):
        count = len(arrays)
        grid = jnp.concatenate(arrays, axis=0).reshape(count * own_rows, depth, slice_width)
        grid = grid.transpose(1, 0, 2)
        pieces = []
        for k in range(depth):
            piece = lax.dynamic_index_in_dim(grid, (own_part - k) % depth, 0, keepdims=False)
            route = [(goal, source) for source, goal in here.route(row_goal(k))]
            pieces.append(lax.ppermute(piece, AXES, route))
        rows = here.rolled(jnp.stack(pieces), here.z)
        rows = rows.reshape(depth, count, own_rows, slice_width).transpose(1, 0, 2, 3)
        return list(rows.reshape(count, 1, stretch, slice_width))

    def inward(values):
        return values.transpose(1, 2, 0)

    def by_square(values):
        kinds, rows, columns = values.shape
        blocks = lax.axis_size(SQUARE)
        parts = values.reshape(kinds, blocks, rows // blocks, columns).transpose(1, 0, 2, 3)
        return parts.reshape(blocks, kinds * (rows // blocks), columns)

    rest = here.rings * depth
    teams = here.halves * rest

    def split_kinds(values, kinds):
        grid = values.reshape(here.halves, rest, kinds, -1, model_width)
        return [grid[:, :, k].reshape(-1, model_width) for k in range(kinds)]

    def halves_sum(grads, *due):
        grids = [grad.astype(LOW).reshape(here.halves, rest, -1, model_width) for grad in grads]
        return here.scatter_half(
            jnp.concatenate(grids, axis=2).reshape(here.halves, -1, model_width), *due
        )

    taps = conv_kernel.shape[0]
    square = lax.axis_index(SQUARE)
    share = slice_width // lax.axis_size(SQUARE)
    channels = teams * share

    heads_rows = attn_out.shape[0] // groups_here
    heads_size = attn_qkv.shape[2] + heads_rows

    def heads_goal(half, side, z, ring, core):
        rank = z // spare
        return (half, rank // 2, (2 * side + core) * spare + z % spare, ring, rank % 2)

    heads_part = jnp.concatenate(
        [inward(attn_qkv), attn_out.reshape(groups_here, heads_rows, -1)], axis=1
    )
    heads_flat = heads_part.shape[0] * heads_part.shape[1]
    heads_moved = here.move(heads_part.reshape(heads_flat, block_width), heads_goal)

    def heads_unpack(gathered):
        blocks = gathered.reshape(
            here.halves, here.rings, 2, 2, spare, groups_here * heads_size, block_width
        )
        ordered = [
            blocks[half, ring, side, core].reshape(groups * heads_size, block_width)
            for half in range(here.halves)
            for side in range(2)
            for ring in range(here.rings)
            for core in range(2)
        ]
        weights = jnp.concatenate(ordered, axis=1).reshape(groups, heads_size, model_width)
        return (
            weights[:, : heads_size - heads_rows].reshape(-1, model_width),
            weights[:, heads_size - heads_rows :].reshape(-1, model_width),
        )

    def heads_rows_of(inward_grad, outward_grad):
        grad = jnp.concatenate(
            [
                inward_grad.astype(LOW).reshape(groups, -1, model_width),
                outward_grad.astype(LOW).reshape(groups, -1, model_width),
            ],
            axis=1,
        ).reshape(groups * heads_size, model_width)
        blocks = [
            grad[:, block_width * k : block_width * (k + 1)]
            for k in range(model_width // block_width)
        ]
        ordered = [
            blocks[((half * 2 + side) * here.rings + ring) * 2 + core]
            for half in range(here.halves)
            for ring in range(here.rings)
            for side in range(2)
            for core in range(2)
        ]
        return jnp.concatenate(ordered, axis=0)

    mixer_flat = 4 * share
    feed_rows = 3 * ffn1_out.shape[0] // lax.axis_size(SQUARE)
    mixer_whole = here.whole_columns(
        by_square(jnp.concatenate([inward(conv_in), conv_out[None]], axis=0))
    )
    residual = rows_in(row_pieces(after(tokens, mixer_whole)))
    own_taps = lax.dynamic_slice_in_dim(conv_kernel, square * share, share, 1)
    own_taps = jnp.pad(own_taps, ((0, 16 - taps), (0, model_width - share)))
    mixer_teams = here.gather_teams(jnp.concatenate([mixer_whole, own_taps], axis=0))
    feed_packs = [
        by_square(jnp.concatenate([inward(inner), outer[None]], axis=0))
        for inner, outer in ((ffn1_in, ffn1_out), (ffn2_in, ffn2_out))
    ]
    feed_parts = here.whole_columns(after(jnp.concatenate(feed_packs, axis=1), mixer_whole))
    mixer_part = mixer_teams.reshape(here.halves, rest, -1, model_width)
    mixer_weights = jnp.concatenate(
        split_kinds(mixer_part[:, :, :mixer_flat].reshape(-1, model_width), 4), axis=0
    )
    mixer_inward, mixer_outward = mixer_weights[: 3 * channels], mixer_weights[3 * channels :]
    kernel = (
        mixer_part[:, :, mixer_flat : mixer_flat + taps, :share]
        .transpose(2, 0, 1, 3)
        .reshape(taps, channels)
        .astype(WIDE)
    )

    aligned = feed_rows % 48 == 0
    out_rows = feed_rows // 3

    def feed_pack(gathered):
        pack = gathered.reshape(-1, 3, out_rows, model_width)
        if aligned:
            return pack
        return pack.transpose(1, 0, 2, 3).reshape(1, 3, -1, model_width)

    def feed_teams_of(grad):
        if not aligned:
            grad = grad.reshape(3, -1, out_rows, model_width).transpose(1, 0, 2, 3)
        return grad.reshape(-1, model_width)

    first_rest = here.gather_rest(after(feed_parts[:feed_rows], mixer_teams, residual))
    first_pack = feed_pack(first_rest)

    own_lengths = jnp.where(here.half == here.core, lengths[0], here.to_rank(lengths[0], 1))
    places = here.z * team_rows + jnp.arange(team_rows + 2, dtype=jnp.int32)
    passed = (places[:, None] >= jnp.cumsum(own_lengths)[None, :]).astype(jnp.int32)
    offsets = places - jnp.sum(passed * own_lengths[None, :], axis=1)
    first_mask = (offsets >= 1).astype(WIDE)[:, None]
    second_mask = (offsets >= 2).astype(WIDE)[:, None]
    offsets = offsets[:team_rows]
    cosine_rows, sine_rows = angles(offsets, head_width)
    beside_gains = here.to_rank(gains, 2)
    half_gains = jnp.where(
        here.side == 0,
        jnp.concatenate([gains, beside_gains]),
        jnp.concatenate([beside_gains, gains]),
    )
    all_gains = half_gains
    if here.halves > 1:
        other_gains = here.to_half(half_gains)
        all_gains = jnp.where(
            here.half == 0,
            jnp.concatenate([half_gains, other_gains]),
            jnp.concatenate([other_gains, half_gains]),
        )
    pair_gains = jnp.tile(qk_gains, (1, 2))

    def gather_ordered(values, *due):
        return jnp.concatenate(here.by_rank(here.gather_rows(values, *due)), axis=0)

    def gather_any(values, *due):
        return jnp.concatenate(here.gather_rows(values, *due), axis=0)

    def scatter_ordered(values, waiting=(), due=()):
        grid = values.astype(LOW).reshape(RANKS, own_rows, model_width)
        blocks = [
            lax.dynamic_index_in_dim(grid, jnp.bitwise_xor(here.rank, k), 0, keepdims=False)
            for k in range(RANKS)
        ]
        return here.scatter_rows(blocks, waiting, due)

    def scatter_any(values, waiting=(), due=()):
        grid = values.astype(LOW).reshape(RANKS, own_rows, model_width)
        return here.scatter_rows([grid[k] for k in range(RANKS)], waiting, due)

    def joined(residual, update):
        return (residual.astype(WIDE) + update).astype(LOW)

    def mixer_forward(residual):
        normed = gather_ordered(root_norm(residual.astype(WIDE), all_gains[0]).astype(LOW))
        projected = times_rows(normed, mixer_inward)
        before, gate, behind = (
            projected[:, :channels],
            projected[:, channels : 2 * channels],
            projected[:, 2 * channels :],
        )
        product = before * behind
        tail = here.up(product[-2:], 1)
        extended = jnp.concatenate([tail, product], axis=0)
        once = extended[1:-1] * first_mask[:team_rows]
        twice = extended[:-2] * second_mask[:team_rows]
        mixed = kernel[2] * product + kernel[1] * once + kernel[0] * twice
        gated = (gate * mixed).astype(LOW)
        update, _ = scatter_ordered(times(gated, mixer_outward))
        return joined(residual, update), (
            residual, normed, before, gate, behind, product, once, twice, mixed, gated,
        )

    def mixer_backward(arriving, saved, *due):
        residual, normed, before, gate, behind, product, once, twice, mixed, gated = saved
        full = gather_ordered(arriving, *due)
        gated_grad = times_rows(full, mixer_outward)
        gate_grad = gated_grad * mixed
        mixed_grad = gated_grad * gate
        following = here.up(mixed_grad[:2], -1)
        extended = jnp.concatenate([mixed_grad, following], axis=0)
        product_grad = (
            kernel[2] * mixed_grad
            + kernel[1] * extended[1:-1] * first_mask[1:-1]
            + kernel[0] * extended[2:] * second_mask[2:]
        )
        kernel_grad = jnp.stack(
            [
                jnp.sum(mixed_grad * twice, axis=0),
                jnp.sum(mixed_grad * once, axis=0),
                jnp.sum(mixed_grad * product, axis=0),
            ]
        )
        low = jnp.concatenate(
            [product_grad * behind, gate_grad, product_grad * before], axis=1
        ).astype(LOW)
        update, (low, full) = scatter_ordered(times(low, mixer_inward), (low, full))
        grad = [columns_times(low[:, k * channels : (k + 1) * channels], normed) for k in range(3)]
        grad.append(columns_times(gated, full))
        leaving, gain_grad = root_norm_back(residual, all_gains[0], update, arriving)
        return leaving, gain_grad, kernel_grad, grad, low

    def square_rows(values, *due):
        return jnp.concatenate(here.gather_square(values, *due), axis=0)

    def square_sums(values, waiting=(), due=()):
        return here.scatter_square(values.astype(LOW), waiting, due)

    def feed_forward(residual, gain_row, pack, gather, *due):
        normed = gather(root_norm(residual.astype(WIDE), gain_row).astype(LOW), *due)
        gated, raised, hidden, update = feed_call(normed, pack, query_rows)
        return update, (residual, normed, gated, raised, hidden)

    def feed_joined(residual, update, scatter, due=()):
        return joined(residual, scatter(update, (), due)[0])

    def feed_backward(arriving, saved, gain_row, pack, gather, scatter, *due):
        residual, normed, gated, raised, hidden = saved
        full = gather(arriving, *due)
        gate_grad, up_grad, update = feed_back_call(full, gated, raised, pack, query_rows)
        update, (gate_grad, up_grad, full) = scatter(update, (gate_grad, up_grad, full))
        grad = feed_grads_call(gate_grad, up_grad, hidden, normed, full, pack.shape[0])
        update = after(update, grad)
        leaving, gain_grad = root_norm_back(residual, gain_row, update, arriving)
        return leaving, gain_grad, feed_teams_of(grad)

    halo_steps = LONGEST // team_rows

    def heads_forward(residual, due):
        normed = root_norm(residual.astype(WIDE), all_gains[2]).astype(LOW)
        normed = gather_ordered(normed, *due[0])
        packed = times_rows(normed, heads_inward)
        queries, pairs = split_heads(packed, pair_gains, cosine_rows, sine_rows, query_rows)
        window = jnp.concatenate(
            [here.up(pairs, step) for step in range(halo_steps, 0, -1)] + [pairs], axis=0
        )
        window = after(window, *due[1])
        attended = attend(offsets, queries, window, query_rows, head_width)
        update, _ = scatter_ordered(times(attended, heads_outward), (), due[2])
        return joined(residual, update), (residual, normed, packed, queries, window, attended)

    def heads_backward(arriving, saved):
        residual, normed, packed, queries, window, attended = saved
        full = gather_ordered(arriving)
        attended_grad = times_rows(full, heads_outward).astype(LOW)
        queries_grad, pairs_grad = attend_back(
            offsets, queries, window, attended_grad, query_rows, head_width
        )
        own = pairs_grad[LONGEST:]
        for step in range(1, halo_steps + 1):
            low = (halo_steps - step) * team_rows
            moved = here.up(pairs_grad[low : low + team_rows].astype(LOW), -step)
            own = own + moved.astype(WIDE)
        own = own.astype(LOW)
        low, pair_gains_grad = split_heads_back(
            packed, pair_gains, cosine_rows, sine_rows, queries_grad, own, query_rows
        )
        update, (low, full) = scatter_ordered(times(low, heads_inward), (low, full))
        inward_grad = columns_times(low, normed)
        outward_grad = columns_times(attended, full)
        leaving, gain_grad = root_norm_back(residual, all_gains[2], update, arriving)
        width = head_width
        head_gains_grad = jnp.stack(
            [pair_gains_grad[0, :width] + pair_gains_grad[0, width:], pair_gains_grad[1, :width]]
        )
        return leaving, gain_grad, head_gains_grad, inward_grad, outward_grad, own

    residual, mixer_saved = mixer_forward(residual)
    heads_teams = here.gather_teams(after(heads_moved, first_rest, residual))
    heads_inward, heads_outward = heads_unpack(heads_teams)
    update, first_saved = feed_forward(residual, all_gains[1], first_pack, square_rows)
    residual = feed_joined(residual, update, square_sums)
    second_teams = here.gather_teams(after(feed_parts[feed_rows:], heads_teams, update))
    second_pack = feed_pack(second_teams)
    pieces = row_pieces(after(cotangent, residual))
    residual, heads_saved = heads_forward(
        residual, [(heads_inward, heads_outward, *pieces[:1]), pieces[1:2], pieces[2:3]]
    )
    last_update, second_saved = feed_forward(
        residual, all_gains[3], second_pack, gather_any, *pieces[3:]
    )
    flowing = rows_in(pieces)

    flowing, gain3, second_grad = feed_backward(
        flowing, second_saved, all_gains[3], second_pack, gather_any, scatter_any
    )
    second_sum = here.scatter_teams(after(second_grad, flowing))
    flowing, gain2, head_gains_grad, heads_inward_grad, heads_outward_grad, _ = heads_backward(
        flowing, heads_saved
    )
    output = feed_joined(residual, after(last_update, flowing), scatter_any)
    heads_grad = heads_rows_of(heads_inward_grad, heads_outward_grad)
    heads_half = here.scatter_half(heads_grad.reshape(here.halves, -1, block_width))
    flowing, gain1, first_grad = feed_backward(
        flowing,
        first_saved,
        all_gains[1],
        first_pack,
        square_rows,
        square_sums,
        heads_grad,
    )
    first_sum = here.scatter_rest(after(first_grad, flowing, second_sum))
    flowing, gain0, kernel_grad, mixer_grad, low = mixer_backward(
        flowing, mixer_saved, output
    )
    mixer_half = halves_sum([mixer_grad[k] for k in range(4)])
    output, input_grad = rows_out(output, after(flowing, mixer_half))
    late = [part.reshape(rest, -1, model_width) for part in (heads_half, mixer_half)]
    late_sum = here.scatter_rest(
        after(jnp.concatenate(late, axis=1).reshape(-1, model_width), first_sum)
    )
    (second_grad,) = here.whole_rows((after(second_sum, input_grad), 3))

    heads_route = [(b, a) for a, b in here.route(heads_goal)]
    (first_grad,) = here.whole_rows((after(first_sum, second_grad), 3))
    heads_wide = heads_flat * block_width // model_width
    heads_grad = late_sum[:heads_wide].reshape(heads_flat, block_width)
    heads_grad = lax.ppermute(heads_grad, AXES, heads_route).reshape(heads_part.shape)
    (mixer_grad,) = here.whole_rows((late_sum[heads_wide:], 4))

    def outside(values):
        return values.transpose(2, 0, 1).astype(WIDE)

    kernel_blocks = kernel_grad.reshape(taps, here.halves, 1, here.rings, depth, 1, share)
    sides = (jnp.arange(2) == here.side).astype(WIDE).reshape(2, 1, 1, 1, 1)
    cores = (jnp.arange(2) == here.core).astype(WIDE).reshape(2, 1)
    kernel_whole = (kernel_blocks * sides * cores).transpose(0, 4, 1, 2, 3, 5, 6)
    small = jnp.concatenate(
        [
            jnp.stack([gain0, gain1, gain2, gain3]).reshape(-1),
            kernel_whole.reshape(-1),
            head_gains_grad.reshape(-1),
        ]
    )
    small = here.total(after(small, input_grad))
    gain_size, kernel_size = 4 * model_width, taps * model_width
    return (
        output,
        input_grad,
        small[:gain_size].reshape(4, model_width),
        small[gain_size + kernel_size :].reshape(2, head_width),
        small[gain_size : gain_size + kernel_size].reshape(taps, model_width),
        outside(mixer_grad[:3]),
        mixer_grad[3].astype(WIDE),
        outside(first_grad[:2]),
        first_grad[2].astype(WIDE),
        outside(heads_grad[:, : heads_size - heads_rows]),
        heads_grad[:, heads_size - heads_rows :].reshape(attn_out.shape).astype(WIDE),
        outside(second_grad[:2]),
        second_grad[2].astype(WIDE),
    )


def solution(mesh):
    sections, depth, replicas = mesh.devices.shape
    fine = Mesh(mesh.devices.reshape(sections // 2, 2, depth, replicas // 2, 2), AXES)
    rows = P(SQUARE, None, "depth")
    columns = P("depth", SQUARE)
    heads = P(SQUARE, "depth", None)
    stream = P(("half", "side"), ("ring", "core"), "depth")
    return jax.shard_map(
        local,
        mesh=fine,
        in_specs=(
            stream,
            P(("ring", "core"), None),
            P(("half", "side"), None),
            P(),
            P(None, "depth"),
            rows,
            columns,
            rows,
            columns,
            heads,
            columns,
            rows,
            columns,
            stream,
        ),
        out_specs=(
            stream,
            stream,
            P(),
            P(),
            P(),
            rows,
            columns,
            rows,
            columns,
            heads,
            columns,
            rows,
            columns,
        ),
        check_vma=False,
    )
```

time: 1160 us -> 871 us (0.75)
  starting transfers between devices: 399 us -> 178 us
  other arithmetic: 181 us -> 69.3 us
  Pallas kernels: 41.7 us -> 144 us
  waiting for transfers between devices: 279 us -> 365 us
  matrix products: 94.8 us -> 21.4 us
  local copies, waits for them, and re-layouts: 131 us -> 65.6 us
    ppermute x202 -> x80, starting transfers between devices: 373 us -> 124 us  [the longest x79 123 us: move(): return lax.ppermute(values, AXES, self.route(target))]
    pallas_call x2 -> x10, Pallas kernels: 41.7 us -> 144 us  [the longest x2 35.3 us: feed_back_call(): pl.pallas_call(feed_back_kernel, grid=(total // rows,), in_specs=[row_spe...]
    all_gather x0 -> x4, waiting for transfers between devices: none -> 36.7 us  [the longest x1 36 us: gather_rest(): return lax.all_gather(values, ('ring', 'depth'), axis=0, tiled=True)]
    all_to_all x0 -> x5, starting transfers between devices: none -> 30.8 us  [the longest x3 21.9 us: whole_rows(): parts = lax.all_to_all(parts, SQUARE, 0, 0, tiled=True)]
    ppermute x202 -> x80, waiting for transfers between devices: 269 us -> 299 us  [the longest x79 299 us: move(): return lax.ppermute(values, AXES, self.route(target))]
    dot_general x8 -> x6, matrix products: 34.1 us -> 4.91 us  [columns_times(): lax.dot_general(a, b, (((0,), (0,)), ((), ())), preferred_element_type=WIDE)]
    dot_general x8 -> x4, matrix products: 35.6 us -> 10.8 us  [times_rows(): lax.dot_general(a, b, (((1,), (1,)), ((), ())), preferred_element_type=WIDE)]
    convert_element_type x36 -> x11, other arithmetic: 34.5 us -> 11.5 us  [the longest x2 4.85 us: scatter_half(): return (kept.astype(WIDE) + came.astype(WIDE)).astype(LOW)]
  transfers between devices with their start and end apart: 210 -> 96, of which waited for: 70 -> 57; matrix products, arithmetic and copies ran while one was open for 30% -> 14% of each run, Pallas kernels for 4% -> 11%
where the time goes in v1:
time: 871 us; the launch traced here: 862 us
  waiting for transfers between devices  365 us (42%)
  starting transfers between devices  178 us (20%)
  Pallas kernels  144 us (17%)
  other arithmetic  69.3 us (8%)
  local copies, waits for them, and re-layouts  65.6 us (8%)
  matrix products  21.4 us (2%)
  between operations  17.7 us (2%)
    ppermute x79, waiting for transfers between devices, move(): return lax.ppermute(values, AXES, self.route(target))  299 us
    ppermute x79, starting transfers between devices, move(): return lax.ppermute(values, AXES, self.route(target))  123 us
    all_gather x1, waiting for transfers between devices, gather_rest(): return lax.all_gather(values, ('ring', 'depth'), axis=0, tiled=True)  36 us
    pallas_call x2, Pallas kernels, feed_back_call(): pl.pallas_call(feed_back_kernel, grid=(total // rows,), in_specs=[row_spe...  35.3 us
    unnamed x331, local copies, waits for them, and re-layouts  31.9 us
    pallas_call x2, Pallas kernels, feed_grads_call(): pl.pallas_call(feed_grads_kernel, grid=(3,), in_specs=[wide_spec] * 3 + [...  30.3 us
    pallas_call x2, Pallas kernels, feed_call(): pl.pallas_call(feed_kernel, grid=(total // rows,), in_specs=[row_spec(row...  28.3 us
    pallas_call x1, Pallas kernels, attend_back(): pl.pallas_call(functools.partial(attend_back_kernel, head_width ** (-0.5)...  23.9 us
  transfers between devices with their start and end apart: 96, of which 57 were waited for; matrix products, arithmetic and copies ran while one was open for 14% of the time, Pallas kernels for 11%

profile of v1, /device:TPU:0, one launch (start us, length us, event | category | flops | bytes accessed | tf_op | source)
XLA Modules:
  0.0 862.2 jit_solution(11812867850982235457)
XLA Ops:
  51.1 17.8 %collective-permute-done.2 = bf16[256,256]{1,0:T(8,128)(2,1)S(1)} collective-permute-done((bf16[256,256]{1,0:T(8,128)(2,1)S(1)}, bf16[256,256]{1,0:T(8,128)(2,1)S(1)}, u32[]{:S(2)}, u32[]{:S(2)}) %collective-permute-start.2) | collective-permute-done | bytes 131104 | tf_op jit(solution)/shard_map/ppermute | solution.py:52
  68.9 16.8 %collective-permute-done.3 = bf16[256,256]{1,0:T(8,128)(2,1)S(1)} collective-permute-done((bf16[256,256]{1,0:T(8,128)(2,1)S(1)}, bf16[256,256]{1,0:T(8,128)(2,1)S(1)}, u32[]{:S(2)}, u32[]{:S(2)}) %collective-permute-start.3) | collective-permute-done | bytes 131104 | tf_op jit(solution)/shard_map/ppermute | solution.py:52
  127.8 13.0 %collective-permute-done.12 = bf16[256,1024]{1,0:T(8,128)(2,1)} collective-permute-done((bf16[256,1024]{1,0:T(8,128)(2,1)}, bf16[256,1024]{1,0:T(8,128)(2,1)}, u32[]{:S(2)}, u32[]{:S(2)}) %collective-permute-start.12) | collective-permute-done | bytes 524320 | tf_op jit(solution)/shard_map/ppermute | solution.py:52
  142.4 36.0 %all-gather.7.cloned.1.call-done = bf16[1728,1024]{1,0:T(8,128)(2,1)} async-done(((bf16[432,1024]{1,0:T(8,128)(2,1)}), bf16[1728,1024]{1,0:T(8,128)(2,1)}) %all-gather.7.cloned.1.call-update) | async-done | bytes 3538960 | tf_op jit(solution)/shard_map/all_gather | solution.py:94
  180.5 12.1 %collective-permute-done.13 = bf16[256,1024]{1,0:T(8,128)(2,1)S(1)} collective-permute-done((bf16[256,1024]{1,0:T(8,128)(2,1)S(1)}, bf16[256,1024]{1,0:T(8,128)(2,1)S(1)}, u32[]{:S(2)}, u32[]{:S(2)}) %collective-permute-start.13) | collective-permute-done | bytes 524320 | tf_op jit(solution)/shard_map/ppermute | solution.py:52
  206.1 14.7 %feed.2 = (bf16[2048,576]{1,0:T(8,128)(2,1)S(1)}, bf16[2048,576]{1,0:T(8,128)(2,1)S(1)}, bf16[2048,576]{1,0:T(8,128)(2,1)}, bf16[2048,1024]{1,0:T(8,128)(2,1)}) custom-call(bf16[2048,1024]{1,0:T(8,128)(2,1)} %copy-done.26, bf16[4,3,144,1024]{3,2,1,0:T(8,128)(2,1)} %bitcast.293, bf16[4,3,144,1024]{3,2,1,0:T(8,128)(2,1)} %bitcast.294, ...), custom_call_target="tpu_custom_call" | custom-call | tf_op jit(solution)/shard_map/feed/pallas_call | solution.py:528
  237.1 11.0 %collective-permute-done.22 = bf16[128,1024]{1,0:T(8,128)(2,1)S(1)} collective-permute-done((bf16[128,1024]{1,0:T(8,128)(2,1)S(1)}, bf16[128,1024]{1,0:T(8,128)(2,1)S(1)}, u32[]{:S(2)}, u32[]{:S(2)}) %collective-permute-start.22) | collective-permute-done | bytes 262176 | tf_op jit(solution)/shard_map/ppermute | solution.py:52
  254.3 9.5 %collective-permute-done.23 = bf16[256,1024]{1,0:T(8,128)(2,1)S(1)} collective-permute-done((bf16[256,1024]{1,0:T(8,128)(2,1)S(1)}, bf16[256,1024]{1,0:T(8,128)(2,1)S(1)}, u32[]{:S(2)}, u32[]{:S(2)}) %collective-permute-start.23) | collective-permute-done | bytes 524320 | tf_op jit(solution)/shard_map/ppermute | solution.py:52
  304.1 19.6 %collective-permute-done.31 = bf16[1024,256]{1,0:T(8,128)(2,1)} collective-permute-done((bf16[1024,256]{1,0:T(8,128)(2,1)S(1)}, bf16[1024,256]{1,0:T(8,128)(2,1)}, u32[]{:S(2)}, u32[]{:S(2)}) %collective-permute-start.31) | collective-permute-done | bytes 524320 | tf_op jit(solution)/shard_map/ppermute | solution.py:52
  324.9 18.0 %attend.1 = bf16[1024,256]{1,0:T(8,128)(2,1)S(1)} custom-call(s32[1024,1]{1,0:T(8,128)S(1)} %copy.191.offsets_ref, bf16[1024,256]{1,0:T(8,128)(2,1)S(1)} %get-tuple-element.87.queries_ref, bf16[2048,256]{1,0:T(8,128)(2,1)S(1)} %pad_maximum_fusion.15.pairs_ref), custom_call_target="tpu_custom_call" | custom-call | tf_op jit(solution)/shard_map/attend/pallas_call | solution.py:417
  346.8 9.0 %collective-permute-start.34 = (bf16[256,1024]{1,0:T(8,128)(2,1)S(1)}, bf16[256,1024]{1,0:T(8,128)(2,1)}, u32[]{:S(2)}, u32[]{:S(2)}) collective-permute-start(bf16[256,1024]{1,0:T(8,128)(2,1)S(1)} %fusion.69), channel_id=1, source_target_pairs={{0,8},{1,9},{2,10},{3,11},{4,12},{5,13},{6,14},{7,15},{8,0},{9,1},... | collective-permute-start | bytes 1572872 | tf_op jit(solution)/shard_map/ppermute | solution.py:52
  355.9 19.2 %collective-permute-start.38 = (bf16[256,256]{1,0:T(8,128)(2,1)S(1)}, bf16[256,256]{1,0:T(8,128)(2,1)S(1)}, u32[]{:S(2)}, u32[]{:S(2)}) collective-permute-start(bf16[256,256]{1,0:T(8,128)(2,1)S(1)} %get-tuple-element.302), channel_id=1, source_target_pairs={{0,9},{1,25},{2,0},{3,16},{4,1},{5,17},{6,8},{7,24},{8,11},{9,27},... | collective-permute-start | bytes 393224 | tf_op jit(solution)/shard_map/ppermute | solution.py:52
  378.1 10.0 %collective-permute-start.41 = (bf16[256,1024]{1,0:T(8,128)(2,1)S(1)}, bf16[256,1024]{1,0:T(8,128)(2,1)S(1)}, u32[]{:S(2)}, u32[]{:S(2)}) collective-permute-start(bf16[256,1024]{1,0:T(8,128)(2,1)S(1)} %bitcast.327), channel_id=1, source_target_pairs={{0,8},{1,9},{2,10},{3,11},{4,12},{5,13},{6,14},{7,15},{8,0},{9,1},... | collective-permute-start | bytes 1572872 | tf_op jit(solution)/shard_map/ppermute | solution.py:52
  390.7 10.2 %collective-permute-done.41 = bf16[256,1024]{1,0:T(8,128)(2,1)S(1)} collective-permute-done((bf16[256,1024]{1,0:T(8,128)(2,1)S(1)}, bf16[256,1024]{1,0:T(8,128)(2,1)S(1)}, u32[]{:S(2)}, u32[]{:S(2)}) %collective-permute-start.41) | collective-permute-done | bytes 524320 | tf_op jit(solution)/shard_map/ppermute | solution.py:52
  401.4 10.5 %collective-permute-done.37 = bf16[256,1024]{1,0:T(8,128)(2,1)S(1)} collective-permute-done((bf16[256,1024]{1,0:T(8,128)(2,1)S(1)}, bf16[256,1024]{1,0:T(8,128)(2,1)S(1)}, u32[]{:S(2)}, u32[]{:S(2)}) %collective-permute-start.37) | collective-permute-done | bytes 524320 | tf_op jit(solution)/shard_map/ppermute | solution.py:52
  414.0 13.6 %feed.3 = (bf16[1024,1152]{1,0:T(8,128)(2,1)}, bf16[1024,1152]{1,0:T(8,128)(2,1)}, bf16[1024,1152]{1,0:T(8,128)(2,1)}, bf16[1024,1024]{1,0:T(8,128)(2,1)S(1)}) custom-call(bf16[1024,1024]{1,0:T(8,128)(2,1)S(1)} %pad_maximum_fusion.2.normed_ref, bf16[8,3,144,1024]{3,2,1,0:T(8,128)(2,1)} %bitcast.287, bf16[8,3,144,1024]{3,2,1,0:T(8,128)(2,1)} %bitcast.288, ...), custom_call_target="tpu_custom_call" | custom-call | tf_op jit(solution)/shard_map/feed/pallas_call | solution.py:528
  427.6 14.4 %feed_back.2 = (bf16[1024,1152]{1,0:T(8,128)(2,1)}, bf16[1024,1152]{1,0:T(8,128)(2,1)}, bf16[1024,1024]{1,0:T(8,128)(2,1)S(1)}) custom-call(bf16[1024,1024]{1,0:T(8,128)(2,1)S(1)} %copy-done.3, bf16[1024,1152]{1,0:T(8,128)(2,1)} %get-tuple-element.98.gated_ref, bf16[1024,1152]{1,0:T(8,128)(2,1)} %get-tuple-element.99.raised_ref, ...), custom_call_target="tpu_custom_call" | custom-call | tf_op jit(solution)/shard_map/feed_back/pallas_call | solution.py:543
  447.4 13.9 %feed_grads.2 = bf16[8,3,144,1024]{3,2,1,0:T(8,128)(2,1)} custom-call(bf16[1024,1152]{1,0:T(8,128)(2,1)} %get-tuple-element.104.gate_grad_ref, bf16[1024,1152]{1,0:T(8,128)(2,1)} %get-tuple-element.105.up_grad_ref, bf16[1024,1152]{1,0:T(8,128)(2,1)} %get-tuple-element.106.hidden_ref, bf16[1024,1024]{1,0:T(8,128)(2,1)} %copy-done.2, ...), custom_call_target="tpu_custom_call" | custom-call | tf_op jit(solution)/shard_map/feed_grads/pallas_call | solution.py:561
  464.4 13.0 %collective-permute-done.46 = bf16[256,1024]{1,0:T(8,128)(2,1)S(1)} collective-permute-done((bf16[256,1024]{1,0:T(8,128)(2,1)S(1)}, bf16[256,1024]{1,0:T(8,128)(2,1)S(1)}, u32[]{:S(2)}, u32[]{:S(2)}) %collective-permute-start.46) | collective-permute-done | bytes 524320 | tf_op jit(solution)/shard_map/ppermute | solution.py:52
  482.3 23.9 %attend_back.1 = (bf16[1024,256]{1,0:T(8,128)(2,1)S(1)}, f32[2048,256]{1,0:T(8,128)S(1)}) custom-call(s32[1024,1]{1,0:T(8,128)S(1)} %copy-done.7, bf16[1024,256]{1,0:T(8,128)(2,1)S(1)} %copy-done.19, bf16[2048,256]{1,0:T(8,128)(2,1)S(1)} %pad_maximum_fusion.15.pairs_ref, bf16[1024,256]{1,0:T(8,128)(2,1)S(1)} %convolution_convert_fusion.10.grad_ref), custom_call_target="tpu_custom_call" | custom-call | tf_op jit(solution)/shard_map/attend_back/pallas_call | solution.py:430
  509.7 14.8 %collective-permute-done.48 = bf16[1024,256]{1,0:T(8,128)(2,1)} collective-permute-done((bf16[1024,256]{1,0:T(8,128)(2,1)}, bf16[1024,256]{1,0:T(8,128)(2,1)}, u32[]{:S(2)}, u32[]{:S(2)}) %collective-permute-start.48) | collective-permute-done | bytes 524320 | tf_op jit(solution)/shard_map/ppermute | solution.py:52
  539.9 10.8 %collective-permute-done.50 = bf16[256,1024]{1,0:T(8,128)(2,1)S(1)} collective-permute-done((bf16[256,1024]{1,0:T(8,128)(2,1)S(1)}, bf16[256,1024]{1,0:T(8,128)(2,1)S(1)}, u32[]{:S(2)}, u32[]{:S(2)}) %collective-permute-start.50) | collective-permute-done | bytes 524320 | tf_op jit(solution)/shard_map/ppermute | solution.py:52
  556.3 8.7 %collective-permute-done.53 = bf16[256,1024]{1,0:T(8,128)(2,1)S(1)} collective-permute-done((bf16[256,1024]{1,0:T(8,128)(2,1)S(1)}, bf16[256,1024]{1,0:T(8,128)(2,1)S(1)}, u32[]{:S(2)}, u32[]{:S(2)}) %collective-permute-start.53) | collective-permute-done | bytes 524320 | tf_op jit(solution)/shard_map/ppermute | solution.py:52
  569.0 9.3 %collective-permute-done.54 = bf16[256,1024]{1,0:T(8,128)(2,1)S(1)} collective-permute-done((bf16[256,1024]{1,0:T(8,128)(2,1)S(1)}, bf16[256,1024]{1,0:T(8,128)(2,1)S(1)}, u32[]{:S(2)}, u32[]{:S(2)}) %collective-permute-start.54) | collective-permute-done | bytes 524320 | tf_op jit(solution)/shard_map/ppermute | solution.py:52
  588.9 20.9 %feed_back.3 = (bf16[2048,576]{1,0:T(8,128)(2,1)S(1)}, bf16[2048,576]{1,0:T(8,128)(2,1)S(1)}, bf16[2048,1024]{1,0:T(8,128)(2,1)}) custom-call(bf16[2048,1024]{1,0:T(8,128)(2,1)} %copy-done.25, bf16[2048,576]{1,0:T(8,128)(2,1)} %copy-done.14, bf16[2048,576]{1,0:T(8,128)(2,1)} %copy-done.15, bf16[4,3,144,1024]{3,2,1,0:T(8,128)(2,1)} %bitcast.296, ...), custom_call_target="tpu_custom_call" | custom-call | tf_op jit(solution)/shard_map/feed_back/pallas_call | solution.py:543
  622.1 9.2 %collective-permute-done.62 = bf16[128,1024]{1,0:T(8,128)(2,1)S(1)} collective-permute-done((bf16[128,1024]{1,0:T(8,128)(2,1)S(1)}, bf16[128,1024]{1,0:T(8,128)(2,1)S(1)}, u32[]{:S(2)}, u32[]{:S(2)}) %collective-permute-start.62) | collective-permute-done | bytes 262176 | tf_op jit(solution)/shard_map/ppermute | solution.py:52
  637.0 16.4 %feed_grads.3 = bf16[4,3,144,1024]{3,2,1,0:T(8,128)(2,1)} custom-call(bf16[2048,576]{1,0:T(8,128)(2,1)} %copy-done.16, bf16[2048,576]{1,0:T(8,128)(2,1)} %copy-done.17, bf16[2048,576]{1,0:T(8,128)(2,1)} %get-tuple-element.125.hidden_ref, bf16[2048,1024]{1,0:T(8,128)(2,1)} %copy-done.26, bf16[2048,1024]{1,0:T(8,128)(2,1)} %copy-done.25), custom_call_target="tpu_custom_call" | custom-call | tf_op jit(solution)/shard_map/feed_grads/pallas_call | solution.py:561
  680.2 9.6 %collective-permute-done.69 = f32[2,256]{1,0:T(2,128)S(1)} collective-permute-done((f32[2,256]{1,0:T(2,128)S(1)}, f32[2,256]{1,0:T(2,128)S(1)}, u32[]{:S(2)}, u32[]{:S(2)}) %collective-permute-start.69) | collective-permute-done | bytes 2080 | tf_op jit(solution)/shard_map/ppermute | solution.py:52
  738.0 17.0 %collective-permute-start.74 = (bf16[512,256]{1,0:T(8,128)(2,1)S(1)}, bf16[512,256]{1,0:T(8,128)(2,1)S(1)}, u32[]{:S(2)}, u32[]{:S(2)}) collective-permute-start(bf16[512,256]{1,0:T(8,128)(2,1)S(1)} %bitcast.403), channel_id=1, source_target_pairs={{1,0},{17,1},{8,2},{24,3},{9,4},{25,5},{0,6},{16,7},{3,8},{19,9},{... | collective-permute-start | bytes 786440 | tf_op jit(solution)/shard_map/ppermute | solution.py:638
  773.7 13.2 %all-to-all-start.4 = ((bf16[8,432,128]{2,1,0:T(8,128)(2,1)}), bf16[8,432,128]{2,1,0:T(8,128)(2,1)S(1)}, u32[]{:S(2)}, u32[]{:S(2)}) async-start(bf16[8,432,128]{2,1,0:T(8,128)(2,1)} %copy.208), calls=%async_computation.7 | async-start | bytes 1769472 | tf_op jit(solution)/shard_map/all_to_all | solution.py:119
  789.4 8.6 collective-permute-done.77
  826.7 8.7 %all-to-all-done.3 = bf16[8,432,128]{2,1,0:T(8,128)(2,1)S(1)} async-done(((bf16[8,432,128]{2,1,0:T(8,128)(2,1)}), bf16[8,432,128]{2,1,0:T(8,128)(2,1)S(1)}, u32[]{:S(2)}, u32[]{:S(2)}) %all-to-all-start.3) | async-done | bytes 884768 | tf_op jit(solution)/shard_map/all_to_all | solution.py:119
  (725 shorter events, 391.3 us)
Async XLA Ops:
  15.3 83.7 %all-gather.5.cloned.1.call-start = ((), (), s32[]{:S(2)}) async-start(), calls=%async_computation.8 | async-start | bytes 2654208 | tf_op jit(solution)/shard_map/all_gather | solution.py:91
  30.8 65.9 %all-to-all-start.1 = ((bf16[8,864,128]{2,1,0:T(8,128)(2,1)}), bf16[8,864,128]{2,1,0:T(8,128)(2,1)S(1)}, u32[]{:S(2)}, u32[]{:S(2)}) async-start(bf16[8,864,128]{2,1,0:T(8,128)(2,1)} %pad_maximum_fusion.8), calls=%async_computation.1 | async-start | bytes 3538944 | tf_op jit(solution)/shard_map/all_to_all | solution.py:111
  34.5 143.9 %all-gather.7.cloned.1.call-start = ((), (), s32[]{:S(2)}) async-start(), calls=%async_computation.9 | async-start | bytes 4423680 | tf_op jit(solution)/shard_map/all_gather | solution.py:94
  40.4 28.5 %collective-permute-start.2 = (bf16[256,256]{1,0:T(8,128)(2,1)S(1)}, bf16[256,256]{1,0:T(8,128)(2,1)S(1)}, u32[]{:S(2)}, u32[]{:S(2)}) collective-permute-start(bf16[256,256]{1,0:T(8,128)(2,1)S(1)} %get-tuple-element.307), channel_id=1, source_target_pairs={{0,8},{1,24},{2,9},{3,25},{4,0},{5,16},{6,1},{7,17},{8,10},{9,26},... | collective-permute-start | bytes 393224 | tf_op jit(solution)/shard_map/ppermute | solution.py:52
  42.7 43.0 %collective-permute-start.3 = (bf16[256,256]{1,0:T(8,128)(2,1)S(1)}, bf16[256,256]{1,0:T(8,128)(2,1)S(1)}, u32[]{:S(2)}, u32[]{:S(2)}) collective-permute-start(bf16[256,256]{1,0:T(8,128)(2,1)S(1)} %get-tuple-element.306), channel_id=1, source_target_pairs={{0,9},{1,25},{2,0},{3,16},{4,1},{5,17},{6,8},{7,24},{8,11},{9,27},... | collective-permute-start | bytes 393224 | tf_op jit(solution)/shard_map/ppermute | solution.py:52
  99.0 125.5 %all-gather.9.cloned.1.call-start = ((), (), s32[]{:S(2)}) async-start(), calls=%async_computation.10 | async-start | bytes 1769472 | tf_op jit(solution)/shard_map/all_gather | solution.py:91
  178.4 235.6 %all-gather.11.cloned.1.call-start = ((), (), s32[]{:S(2)}) async-start(), calls=%async_computation.11 | async-start | bytes 7962624 | tf_op jit(solution)/shard_map/all_gather | solution.py:91
  178.9 16.2 %collective-permute-start.14 = (bf16[256,1024]{1,0:T(8,128)(2,1)S(1)}, bf16[256,1024]{1,0:T(8,128)(2,1)S(1)}, u32[]{:S(2)}, u32[]{:S(2)}) collective-permute-start(bf16[256,1024]{1,0:T(8,128)(2,1)S(1)} %get-tuple-element.228), channel_id=1, source_target_pairs={{0,16},{1,17},{2,18},{3,19},{4,20},{5,21},{6,22},{7,23},{8,24},{9,... | collective-permute-start | bytes 1572872 | tf_op jit(solution)/shard_map/ppermute | solution.py:52
  224.5 453.9 %reduce-scatter.4.cloned.1.call-start = ((), (), s32[]{:S(2)}) async-start(), calls=%async_computation.12 | async-start | bytes 7962624 | tf_op jit(solution)/shard_map/reduce_scatter | solution.py:103
  296.6 27.1 %collective-permute-start.31 = (bf16[1024,256]{1,0:T(8,128)(2,1)S(1)}, bf16[1024,256]{1,0:T(8,128)(2,1)}, u32[]{:S(2)}, u32[]{:S(2)}) collective-permute-start(bf16[1024,256]{1,0:T(8,128)(2,1)S(1)} %get-tuple-element.88), channel_id=1, source_target_pairs={{0,2},{1,3},{2,4},{3,5},{4,6},{5,7},{8,10},{9,11},{10,12},{11,13},... | collective-permute-start | bytes 1572872 | tf_op jit(solution)/shard_map/ppermute | solution.py:52
  301.6 23.2 %collective-permute-start.32 = (bf16[256,256]{1,0:T(8,128)(2,1)}, bf16[256,256]{1,0:T(8,128)(2,1)S(1)}, u32[]{:S(2)}, u32[]{:S(2)}) collective-permute-start(bf16[256,256]{1,0:T(8,128)(2,1)} %get-tuple-element.304), channel_id=1, source_target_pairs={{0,1},{1,17},{2,8},{3,24},{4,9},{5,25},{6,0},{7,16},{8,3},{9,19},{... | collective-permute-start | bytes 393224 | tf_op jit(solution)/shard_map/ppermute | solution.py:52
  346.8 41.3 %collective-permute-start.34 = (bf16[256,1024]{1,0:T(8,128)(2,1)S(1)}, bf16[256,1024]{1,0:T(8,128)(2,1)}, u32[]{:S(2)}, u32[]{:S(2)}) collective-permute-start(bf16[256,1024]{1,0:T(8,128)(2,1)S(1)} %fusion.69), channel_id=1, source_target_pairs={{0,8},{1,9},{2,10},{3,11},{4,12},{5,13},{6,14},{7,15},{8,0},{9,1},... | collective-permute-start | bytes 1572872 | tf_op jit(solution)/shard_map/ppermute | solution.py:52
  355.8 20.8 %collective-permute-start.35 = (bf16[256,256]{1,0:T(8,128)(2,1)S(1)}, bf16[256,256]{1,0:T(8,128)(2,1)S(1)}, u32[]{:S(2)}, u32[]{:S(2)}) collective-permute-start(bf16[256,256]{1,0:T(8,128)(2,1)S(1)} %get-tuple-element.303), channel_id=1, source_target_pairs={{0,8},{1,24},{2,9},{3,25},{4,0},{5,16},{6,1},{7,17},{8,10},{9,26},... | collective-permute-start | bytes 393224 | tf_op jit(solution)/shard_map/ppermute | solution.py:52
  355.9 21.7 %collective-permute-start.38 = (bf16[256,256]{1,0:T(8,128)(2,1)S(1)}, bf16[256,256]{1,0:T(8,128)(2,1)S(1)}, u32[]{:S(2)}, u32[]{:S(2)}) collective-permute-start(bf16[256,256]{1,0:T(8,128)(2,1)S(1)} %get-tuple-element.302), channel_id=1, source_target_pairs={{0,9},{1,25},{2,0},{3,16},{4,1},{5,17},{6,8},{7,24},{8,11},{9,27},... | collective-permute-start | bytes 393224 | tf_op jit(solution)/shard_map/ppermute | solution.py:52
  378.1 22.8 %collective-permute-start.41 = (bf16[256,1024]{1,0:T(8,128)(2,1)S(1)}, bf16[256,1024]{1,0:T(8,128)(2,1)S(1)}, u32[]{:S(2)}, u32[]{:S(2)}) collective-permute-start(bf16[256,1024]{1,0:T(8,128)(2,1)S(1)} %bitcast.327), channel_id=1, source_target_pairs={{0,8},{1,9},{2,10},{3,11},{4,12},{5,13},{6,14},{7,15},{8,0},{9,1},... | collective-permute-start | bytes 1572872 | tf_op jit(solution)/shard_map/ppermute | solution.py:52
  389.9 22.0 %collective-permute-start.37 = (bf16[256,1024]{1,0:T(8,128)(2,1)S(1)}, bf16[256,1024]{1,0:T(8,128)(2,1)S(1)}, u32[]{:S(2)}, u32[]{:S(2)}) collective-permute-start(bf16[256,1024]{1,0:T(8,128)(2,1)S(1)} %fusion.51), channel_id=1, source_target_pairs={{0,8},{1,9},{2,10},{3,11},{4,12},{5,13},{6,14},{7,15},{8,0},{9,1},... | collective-permute-start | bytes 1572872 | tf_op jit(solution)/shard_map/ppermute | solution.py:52
  390.7 21.2 %collective-permute-start.40 = (bf16[256,1024]{1,0:T(8,128)(2,1)S(1)}, bf16[256,1024]{1,0:T(8,128)(2,1)S(1)}, u32[]{:S(2)}, u32[]{:S(2)}) collective-permute-start(bf16[256,1024]{1,0:T(8,128)(2,1)S(1)} %bitcast.328), channel_id=1, source_target_pairs={{0,1},{1,0},{2,3},{3,2},{4,5},{5,4},{6,7},{7,6},{8,9},{9,8},{10,11... | collective-permute-start | bytes 1572872 | tf_op jit(solution)/shard_map/ppermute | solution.py:52
  509.7 252.6 %reduce-scatter.6.cloned.1.call-start = ((), (), s32[]{:S(2)}) async-start(), calls=%async_computation.13 | async-start | bytes 4423680 | tf_op jit(solution)/shard_map/reduce_scatter | solution.py:108
  552.5 25.8 %collective-permute-start.54 = (bf16[256,1024]{1,0:T(8,128)(2,1)S(1)}, bf16[256,1024]{1,0:T(8,128)(2,1)S(1)}, u32[]{:S(2)}, u32[]{:S(2)}) collective-permute-start(bf16[256,1024]{1,0:T(8,128)(2,1)S(1)} %get-tuple-element.222), channel_id=1, source_target_pairs={{0,16},{1,17},{2,18},{3,19},{4,20},{5,21},{6,22},{7,23},{8,24},{9,... | collective-permute-start | bytes 1572872 | tf_op jit(solution)/shard_map/ppermute | solution.py:52
  556.2 28.8 %collective-permute-start.57 = (bf16[256,1024]{1,0:T(8,128)(2,1)S(1)}, bf16[256,1024]{1,0:T(8,128)(2,1)S(1)}, u32[]{:S(2)}, u32[]{:S(2)}) collective-permute-start(bf16[256,1024]{1,0:T(8,128)(2,1)S(1)} %get-tuple-element.222), channel_id=1, source_target_pairs={{0,1},{1,0},{2,3},{3,2},{4,5},{5,4},{6,7},{7,6},{8,9},{9,8},{10,11... | collective-permute-start | bytes 1572872 | tf_op jit(solution)/shard_map/ppermute | solution.py:52
  565.0 17.3 %collective-permute-start.55 = (bf16[128,1024]{1,0:T(8,128)(2,1)S(1)}, bf16[128,1024]{1,0:T(8,128)(2,1)S(1)}, u32[]{:S(2)}, u32[]{:S(2)}) collective-permute-start(bf16[128,1024]{1,0:T(8,128)(2,1)S(1)} %slice.564), channel_id=1, source_target_pairs={{0,16},{1,17},{2,18},{3,19},{4,20},{5,21},{6,22},{7,23},{8,24},{9,... | collective-permute-start | bytes 786440 | tf_op jit(solution)/shard_map/ppermute | solution.py:52
  614.7 20.7 %collective-permute-start.51 = (bf16[512,1024]{1,0:T(8,128)(2,1)S(1)}, bf16[512,1024]{1,0:T(8,128)(2,1)S(1)}, u32[]{:S(2)}, u32[]{:S(2)}) collective-permute-start(bf16[512,1024]{1,0:T(8,128)(2,1)S(1)} %pad_maximum_fusion.19), channel_id=1, source_target_pairs={{0,1},{1,0},{2,3},{3,2},{4,5},{5,4},{6,7},{7,6},{8,9},{9,8},{10,11... | collective-permute-start | bytes 3145736 | tf_op jit(solution)/shard_map/ppermute | solution.py:52
  631.5 21.9 %collective-permute-start.63 = (bf16[256,1024]{1,0:T(8,128)(2,1)S(1)}, bf16[256,1024]{1,0:T(8,128)(2,1)}, u32[]{:S(2)}, u32[]{:S(2)}) collective-permute-start(bf16[256,1024]{1,0:T(8,128)(2,1)S(1)} %pad_maximum_fusion.28), channel_id=1, source_target_pairs={{0,8},{1,9},{2,10},{3,11},{4,12},{5,13},{6,14},{7,15},{8,0},{9,1},... | collective-permute-start | bytes 1572872 | tf_op jit(solution)/shard_map/ppermute | solution.py:52
  633.5 19.9 %collective-permute-start.65 = (bf16[256,1024]{1,0:T(8,128)(2,1)}, bf16[256,1024]{1,0:T(8,128)(2,1)}, u32[]{:S(2)}, u32[]{:S(2)}) collective-permute-start(bf16[256,1024]{1,0:T(8,128)(2,1)} %pad_maximum_fusion.29), channel_id=1, source_target_pairs={{0,16},{1,17},{2,18},{3,19},{4,20},{5,21},{6,22},{7,23},{8,24},{9,... | collective-permute-start | bytes 1572872 | tf_op jit(solution)/shard_map/ppermute | solution.py:52
  636.3 21.1 %collective-permute-start.52 = (bf16[256,1024]{1,0:T(8,128)(2,1)}, bf16[256,1024]{1,0:T(8,128)(2,1)}, u32[]{:S(2)}, u32[]{:S(2)}) collective-permute-start(bf16[256,1024]{1,0:T(8,128)(2,1)} %add_convert_fusion), channel_id=1, source_target_pairs={{0,8},{1,9},{2,10},{3,11},{4,12},{5,13},{6,14},{7,15},{8,0},{9,1},... | collective-permute-start | bytes 1572872 | tf_op jit(solution)/shard_map/ppermute | solution.py:52
  678.5 157.8 %reduce-scatter.8.cloned.1.call-start = ((), (), s32[]{:S(2)}) async-start(), calls=%async_computation.14 | async-start | bytes 2293760 | tf_op jit(solution)/shard_map/reduce_scatter | solution.py:108
  679.7 19.9 %collective-permute-start.82 = (bf16[3072,128]{1,0:T(8,128)(2,1)}, bf16[3072,128]{1,0:T(8,128)(2,1)}, u32[]{:S(2)}, u32[]{:S(2)}) collective-permute-start(bf16[3072,128]{1,0:T(8,128)(2,1)} %dynamic-slice_bitcast_fusion.1), channel_id=1, source_target_pairs={{0,16},{1,17},{2,18},{3,19},{4,20},{5,21},{6,22},{7,23},{8,24},{9,... | collective-permute-start | bytes 2359304 | tf_op jit(solution)/shard_map/ppermute | solution.py:52
  706.7 24.7 %collective-permute-start.72 = (bf16[512,1024]{1,0:T(8,128)(2,1)}, bf16[512,1024]{1,0:T(8,128)(2,1)}, u32[]{:S(2)}, u32[]{:S(2)}) collective-permute-start(bf16[512,1024]{1,0:T(8,128)(2,1)} %dynamic-slice_bitcast_fusion), channel_id=1, source_target_pairs={{0,16},{1,17},{2,18},{3,19},{4,20},{5,21},{6,22},{7,23},{8,24},{9,... | collective-permute-start | bytes 3145736 | tf_op jit(solution)/shard_map/ppermute | solution.py:52
  737.1 25.1 %collective-permute-start.73 = (bf16[512,256]{1,0:T(8,128)(2,1)S(1)}, bf16[512,256]{1,0:T(8,128)(2,1)S(1)}, u32[]{:S(2)}, u32[]{:S(2)}) collective-permute-start(bf16[512,256]{1,0:T(8,128)(2,1)S(1)} %bitcast.402), channel_id=1, source_target_pairs={{0,0},{16,1},{1,2},{17,3},{8,4},{24,5},{9,6},{25,7},{2,8},{18,9},{... | collective-permute-start | bytes 786440 | tf_op jit(solution)/shard_map/ppermute | solution.py:638
  738.0 24.3 %collective-permute-start.74 = (bf16[512,256]{1,0:T(8,128)(2,1)S(1)}, bf16[512,256]{1,0:T(8,128)(2,1)S(1)}, u32[]{:S(2)}, u32[]{:S(2)}) collective-permute-start(bf16[512,256]{1,0:T(8,128)(2,1)S(1)} %bitcast.403), channel_id=1, source_target_pairs={{1,0},{17,1},{8,2},{24,3},{9,4},{25,5},{0,6},{16,7},{3,8},{19,9},{... | collective-permute-start | bytes 786440 | tf_op jit(solution)/shard_map/ppermute | solution.py:638
  773.7 44.6 %all-to-all-start.4 = ((bf16[8,432,128]{2,1,0:T(8,128)(2,1)}), bf16[8,432,128]{2,1,0:T(8,128)(2,1)S(1)}, u32[]{:S(2)}, u32[]{:S(2)}) async-start(bf16[8,432,128]{2,1,0:T(8,128)(2,1)} %copy.208), calls=%async_computation.7 | async-start | bytes 1769472 | tf_op jit(solution)/shard_map/all_to_all | solution.py:119
  818.3 17.1 %all-to-all-start.3 = ((bf16[8,432,128]{2,1,0:T(8,128)(2,1)}), bf16[8,432,128]{2,1,0:T(8,128)(2,1)S(1)}, u32[]{:S(2)}, u32[]{:S(2)}) async-start(bf16[8,432,128]{2,1,0:T(8,128)(2,1)} %copy.205), calls=%async_computation.6 | async-start | bytes 1769472 | tf_op jit(solution)/shard_map/all_to_all | solution.py:119
  (206 other events, 2180.6 us)
Sparse Core Ops, SparseCore 0:
  23.5 74.1 all-gather.4
  99.3 78.9 all-gather.6
  181.0 43.4 all-gather.8
  226.4 120.4 all-gather.10
  509.8 145.5 reduce-scatter.3
  678.6 80.4 reduce-scatter.5
  762.4 56.6 reduce-scatter.7

commit v2 on v1

--- a/solution.py
+++ b/solution.py
@@ -178,7 +178,7 @@
 
 
 def after(values, *others):
-    return lax.optimization_barrier((values, *others))[0]
+    return lax.optimization_barrier((values, *others))[0] if others else values
 
 
 def times(a, b):
@@ -352,7 +352,7 @@
     allowed = jnp.concatenate([allowed.astype(WIDE)] * (queries.shape[0] // rows), axis=0) > 0.5
     scores = jnp.where(allowed, scores, NEGATIVE)
     weights = jnp.exp(scores - jnp.max(scores, axis=-1, keepdims=True))
-    return weights / jnp.sum(weights, axis=-1, keepdims=True)
+    return weights * (1 / jnp.sum(weights, axis=-1, keepdims=True))
 
 
 def over(values):
@@ -369,9 +369,26 @@
     rows, width = queries_ref.shape[0], queries_ref.shape[1] // 2
     low = pl.multiple_of(pl.program_id(1) * rows, rows)
     pairs = pairs_ref[pl.ds(low, LONGEST + rows), :]
-    weights = block_weights(offsets_ref[...], over(queries_ref[...]), pairs[:, :width], scale)
-    result = jnp.dot(weights.astype(LOW), pairs[:, width:], preferred_element_type=WIDE)
-    out_ref[...] = beside(result.astype(LOW))
+    keys, values = pairs[:, :width], pairs[:, width:]
+    shape = (rows, pairs.shape[0])
+    back = (
+        lax.broadcasted_iota(jnp.int32, shape, 0)
+        + LONGEST
+        - lax.broadcasted_iota(jnp.int32, shape, 1)
+    )
+    allowed = (back >= 0) & (back <= offsets_ref[...])
+    results = []
+    for head in range(2):
+        queries = queries_ref[:, head * width : (head + 1) * width]
+        scores = lax.dot_general(
+            queries, keys, (((1,), (1,)), ((), ())), preferred_element_type=WIDE
+        )
+        scores = jnp.where(allowed, scores, NEGATIVE)
+        weights = jnp.exp((scores - jnp.max(scores, axis=-1, keepdims=True)) * scale)
+        weights = weights * (1 / jnp.sum(weights, axis=-1, keepdims=True))
+        result = jnp.dot(weights.astype(LOW), values, preferred_element_type=WIDE)
+        results.append(result.astype(LOW))
+    out_ref[...] = jnp.concatenate(results, axis=1)
 
 
 def attend_back_kernel(
@@ -475,8 +492,19 @@
     gate_grad_ref,
     up_grad_ref,
     update_ref,
+    *turned_ref,
 ):
-    hidden_grad = dot_nt(full_ref[...], whole_rows_of(outward_ref))
+    if turned_ref:
+
+        @pl.when(pl.program_id(0) == 0)
+        def _():
+            turned_ref[0][...] = whole_rows_of(outward_ref).T
+
+        hidden_grad = jnp.dot(
+            full_ref[...], turned_ref[0][...], preferred_element_type=WIDE
+        )
+    else:
+        hidden_grad = dot_nt(full_ref[...], whole_rows_of(outward_ref))
     gate = gated_ref[...].astype(WIDE)
     up = raised_ref[...].astype(WIDE)
     sigmoid = 1 / (1 + jnp.exp(-gate))
@@ -536,7 +564,7 @@
     )(normed, pack, pack, pack)
 
 
-def feed_back_call(full, gated, raised, pack, rows):
+def feed_back_call(full, gated, raised, pack, rows, turned):
     total, columns = full.shape
     width = gated.shape[1]
     wide = jax.ShapeDtypeStruct((total, width), LOW)
@@ -548,6 +576,7 @@
         + [kind_spec(pack, k) for k in range(3)],
         out_specs=[row_spec(rows, width)] * 2 + [row_spec(rows, columns)],
         out_shape=[wide] * 2 + [jax.ShapeDtypeStruct((total, columns), LOW)],
+        scratch_shapes=[pltpu.VMEM((columns, width), LOW)] if turned else [],
         compiler_params=pltpu.CompilerParams(vmem_limit_bytes=48 << 20),
         name="feed_back",
     )(full, gated, raised, pack, pack, pack)
@@ -600,6 +629,7 @@
     groups = groups_here * depth // RANKS
     block_width = conv_in.shape[0]
     query_rows = min(256, team_rows)
+    feed_block = min(512, team_rows)
     spare = depth // RANKS
 
     def row_goal(k):
@@ -863,7 +893,7 @@
 
     def feed_forward(residual, gain_row, pack, gather, *due):
         normed = gather(root_norm(residual.astype(WIDE), gain_row).astype(LOW), *due)
-        gated, raised, hidden, update = feed_call(normed, pack, query_rows)
+        gated, raised, hidden, update = feed_call(normed, pack, feed_block)
         return update, (residual, normed, gated, raised, hidden)
 
     def feed_joined(residual, update, scatter, due=()):
@@ -872,7 +902,10 @@
     def feed_backward(arriving, saved, gain_row, pack, gather, scatter, *due):
         residual, normed, gated, raised, hidden = saved
         full = gather(arriving, *due)
-        gate_grad, up_grad, update = feed_back_call(full, gated, raised, pack, query_rows)
+        square = full.shape[0] > team_rows
+        gate_grad, up_grad, update = feed_back_call(
+            full, gated, raised, pack, query_rows if square else feed_block, square
+        )
         update, (gate_grad, up_grad, full) = scatter(update, (gate_grad, up_grad, full))
         grad = feed_grads_call(gate_grad, up_grad, hidden, normed, full, pack.shape[0])
         update = after(update, grad)
@@ -939,10 +972,10 @@
     flowing, gain3, second_grad = feed_backward(
         flowing, second_saved, all_gains[3], second_pack, gather_any, scatter_any
     )
-    second_sum = here.scatter_teams(after(second_grad, flowing))
-    flowing, gain2, head_gains_grad, heads_inward_grad, heads_outward_grad, _ = heads_backward(
-        flowing, heads_saved
-    )
+    flowing, gain2, head_gains_grad, heads_inward_grad, heads_outward_grad, pairs_low = (
+        heads_backward(flowing, heads_saved)
+    )
+    second_sum = here.scatter_teams(after(second_grad, pairs_low))
     output = feed_joined(residual, after(last_update, flowing), scatter_any)
     heads_grad = heads_rows_of(heads_inward_grad, heads_outward_grad)
     heads_half = here.scatter_half(heads_grad.reshape(here.halves, -1, block_width))
@@ -965,9 +998,9 @@
     late_sum = here.scatter_rest(
         after(jnp.concatenate(late, axis=1).reshape(-1, model_width), first_sum)
     )
+
+    heads_route = [(b, a) for a, b in here.route(heads_goal)]
     (second_grad,) = here.whole_rows((after(second_sum, input_grad), 3))
-
-    heads_route = [(b, a) for a, b in here.route(heads_goal)]
     (first_grad,) = here.whole_rows((after(first_sum, second_grad), 3))
     heads_wide = heads_flat * block_width // model_width
     heads_grad = late_sum[:heads_wide].reshape(heads_flat, block_width)

time: 871 us -> 851 us (0.977)
  starting transfers between devices: 178 us -> 154 us
  waiting for transfers between devices: 365 us -> 389 us
  other arithmetic: 69.3 us -> 56.1 us
    ppermute x79, waiting for transfers between devices: 299 us -> 321 us  [move(): return lax.ppermute(values, AXES, self.route(target))]
    ppermute x79, starting transfers between devices: 123 us -> 111 us  [move(): return lax.ppermute(values, AXES, self.route(target))]
    ppermute x4, starting transfers between devices: 22.8 us -> 11.5 us  [rows_out(): pieces.append(lax.ppermute(piece, AXES, route))]
    unnamed x331 -> x351, local copies, waits for them, and re-layouts: 31.9 us -> 39.7 us
  transfers between devices with their start and end apart: 96 -> 96, of which waited for: 57 -> 59; matrix products, arithmetic and copies ran while one was open for 14% -> 13% of each run, Pallas kernels for 11% -> 10%
where the time goes in v2:
time: 851 us; the launch traced here: 842 us
  waiting for transfers between devices  389 us (46%)
  starting transfers between devices  154 us (18%)
  Pallas kernels  136 us (16%)
  local copies, waits for them, and re-layouts  72.3 us (8%)
  other arithmetic  56.1 us (7%)
  between operations  17.5 us (2%)
  matrix products  16.3 us (2%)
    ppermute x79, waiting for transfers between devices, move(): return lax.ppermute(values, AXES, self.route(target))  321 us
    ppermute x79, starting transfers between devices, move(): return lax.ppermute(values, AXES, self.route(target))  111 us
    unnamed x351, local copies, waits for them, and re-layouts  39.7 us
    all_gather x1, waiting for transfers between devices, gather_rest(): return lax.all_gather(values, ('ring', 'depth'), axis=0, tiled=True)  37.7 us
    pallas_call x2, Pallas kernels, feed_grads_call(): pl.pallas_call(feed_grads_kernel, grid=(3,), in_specs=[wide_spec] * 3 + [...  31 us
    pallas_call x2, Pallas kernels, feed_back_call(): pl.pallas_call(feed_back_kernel, grid=(total // rows,), in_specs=[row_spe...  28.8 us
    pallas_call x2, Pallas kernels, feed_call(): pl.pallas_call(feed_kernel, grid=(total // rows,), in_specs=[row_spec(row...  26.8 us
    pallas_call x1, Pallas kernels, attend_back(): pl.pallas_call(functools.partial(attend_back_kernel, head_width ** (-0.5)...  23.9 us
  transfers between devices with their start and end apart: 96, of which 59 were waited for; matrix products, arithmetic and copies ran while one was open for 13% of the time, Pallas kernels for 10%

profile of v2, /device:TPU:0, one launch (start us, length us, event | category | flops | bytes accessed | tf_op | source)
XLA Modules:
  0.0 841.6 jit_solution(15341340801778087752)
XLA Ops:
  51.1 17.8 %collective-permute-done.2 = bf16[256,256]{1,0:T(8,128)(2,1)S(1)} collective-permute-done((bf16[256,256]{1,0:T(8,128)(2,1)S(1)}, bf16[256,256]{1,0:T(8,128)(2,1)S(1)}, u32[]{:S(2)}, u32[]{:S(2)}) %collective-permute-start.2) | collective-permute-done | bytes 131104 | tf_op jit(solution)/shard_map/ppermute | solution.py:52
  68.9 16.8 %collective-permute-done.3 = bf16[256,256]{1,0:T(8,128)(2,1)S(1)} collective-permute-done((bf16[256,256]{1,0:T(8,128)(2,1)S(1)}, bf16[256,256]{1,0:T(8,128)(2,1)S(1)}, u32[]{:S(2)}, u32[]{:S(2)}) %collective-permute-start.3) | collective-permute-done | bytes 131104 | tf_op jit(solution)/shard_map/ppermute | solution.py:52
  126.0 13.0 %collective-permute-done.12 = bf16[256,1024]{1,0:T(8,128)(2,1)} collective-permute-done((bf16[256,1024]{1,0:T(8,128)(2,1)}, bf16[256,1024]{1,0:T(8,128)(2,1)}, u32[]{:S(2)}, u32[]{:S(2)}) %collective-permute-start.12) | collective-permute-done | bytes 524320 | tf_op jit(solution)/shard_map/ppermute | solution.py:52
  140.7 37.7 %all-gather.7.cloned.1.call-done = bf16[1728,1024]{1,0:T(8,128)(2,1)} async-done(((bf16[432,1024]{1,0:T(8,128)(2,1)}), bf16[1728,1024]{1,0:T(8,128)(2,1)}) %all-gather.7.cloned.1.call-update) | async-done | bytes 3538960 | tf_op jit(solution)/shard_map/all_gather | solution.py:94
  180.6 12.1 %collective-permute-done.13 = bf16[256,1024]{1,0:T(8,128)(2,1)S(1)} collective-permute-done((bf16[256,1024]{1,0:T(8,128)(2,1)S(1)}, bf16[256,1024]{1,0:T(8,128)(2,1)S(1)}, u32[]{:S(2)}, u32[]{:S(2)}) %collective-permute-start.13) | collective-permute-done | bytes 524320 | tf_op jit(solution)/shard_map/ppermute | solution.py:52
  206.4 14.0 %feed.2 = (bf16[2048,576]{1,0:T(8,128)(2,1)S(1)}, bf16[2048,576]{1,0:T(8,128)(2,1)S(1)}, bf16[2048,576]{1,0:T(8,128)(2,1)}, bf16[2048,1024]{1,0:T(8,128)(2,1)}) custom-call(bf16[2048,1024]{1,0:T(8,128)(2,1)} %copy-done.27, bf16[4,3,144,1024]{3,2,1,0:T(8,128)(2,1)} %bitcast.293, bf16[4,3,144,1024]{3,2,1,0:T(8,128)(2,1)} %bitcast.294, ...), custom_call_target="tpu_custom_call" | custom-call | tf_op jit(solution)/shard_map/feed/pallas_call | solution.py:556
  236.6 11.6 %collective-permute-done.22 = bf16[128,1024]{1,0:T(8,128)(2,1)S(1)} collective-permute-done((bf16[128,1024]{1,0:T(8,128)(2,1)S(1)}, bf16[128,1024]{1,0:T(8,128)(2,1)S(1)}, u32[]{:S(2)}, u32[]{:S(2)}) %collective-permute-start.22) | collective-permute-done | bytes 262176 | tf_op jit(solution)/shard_map/ppermute | solution.py:52
  252.9 10.2 %collective-permute-done.23 = bf16[256,1024]{1,0:T(8,128)(2,1)S(1)} collective-permute-done((bf16[256,1024]{1,0:T(8,128)(2,1)S(1)}, bf16[256,1024]{1,0:T(8,128)(2,1)S(1)}, u32[]{:S(2)}, u32[]{:S(2)}) %collective-permute-start.23) | collective-permute-done | bytes 524320 | tf_op jit(solution)/shard_map/ppermute | solution.py:52
  272.6 9.2 %collective-permute-done.27 = bf16[256,1024]{1,0:T(8,128)(2,1)} collective-permute-done((bf16[256,1024]{1,0:T(8,128)(2,1)}, bf16[256,1024]{1,0:T(8,128)(2,1)}, u32[]{:S(2)}, u32[]{:S(2)}) %collective-permute-start.27) | collective-permute-done | bytes 524320 | tf_op jit(solution)/shard_map/ppermute | solution.py:52
  303.1 19.6 %collective-permute-done.31 = bf16[1024,256]{1,0:T(8,128)(2,1)} collective-permute-done((bf16[1024,256]{1,0:T(8,128)(2,1)S(1)}, bf16[1024,256]{1,0:T(8,128)(2,1)}, u32[]{:S(2)}, u32[]{:S(2)}) %collective-permute-start.31) | collective-permute-done | bytes 524320 | tf_op jit(solution)/shard_map/ppermute | solution.py:52
  323.8 16.7 %attend.1 = bf16[1024,256]{1,0:T(8,128)(2,1)S(1)} custom-call(s32[1024,1]{1,0:T(8,128)S(1)} %copy.191.offsets_ref, bf16[1024,256]{1,0:T(8,128)(2,1)S(1)} %get-tuple-element.87.queries_ref, bf16[2048,256]{1,0:T(8,128)(2,1)S(1)} %pad_maximum_fusion.14.pairs_ref), custom_call_target="tpu_custom_call" | custom-call | tf_op jit(solution)/shard_map/attend/pallas_call | solution.py:434
  353.9 19.6 %collective-permute-start.38 = (bf16[256,256]{1,0:T(8,128)(2,1)S(1)}, bf16[256,256]{1,0:T(8,128)(2,1)S(1)}, u32[]{:S(2)}, u32[]{:S(2)}) collective-permute-start(bf16[256,256]{1,0:T(8,128)(2,1)S(1)} %copy-done.118), channel_id=1, source_target_pairs={{0,9},{1,25},{2,0},{3,16},{4,1},{5,17},{6,8},{7,24},{8,11},{9,27},... | collective-permute-start | bytes 393224 | tf_op jit(solution)/shard_map/ppermute | solution.py:52
  386.2 10.6 %collective-permute-done.41 = bf16[256,1024]{1,0:T(8,128)(2,1)S(1)} collective-permute-done((bf16[256,1024]{1,0:T(8,128)(2,1)S(1)}, bf16[256,1024]{1,0:T(8,128)(2,1)S(1)}, u32[]{:S(2)}, u32[]{:S(2)}) %collective-permute-start.41) | collective-permute-done | bytes 524320 | tf_op jit(solution)/shard_map/ppermute | solution.py:52
  397.3 10.3 %collective-permute-done.37 = bf16[256,1024]{1,0:T(8,128)(2,1)S(1)} collective-permute-done((bf16[256,1024]{1,0:T(8,128)(2,1)S(1)}, bf16[256,1024]{1,0:T(8,128)(2,1)S(1)}, u32[]{:S(2)}, u32[]{:S(2)}) %collective-permute-start.37) | collective-permute-done | bytes 524320 | tf_op jit(solution)/shard_map/ppermute | solution.py:52
  409.8 12.8 %feed.3 = (bf16[1024,1152]{1,0:T(8,128)(2,1)}, bf16[1024,1152]{1,0:T(8,128)(2,1)}, bf16[1024,1152]{1,0:T(8,128)(2,1)}, bf16[1024,1024]{1,0:T(8,128)(2,1)S(1)}) custom-call(bf16[1024,1024]{1,0:T(8,128)(2,1)S(1)} %pad_maximum_fusion.2.normed_ref, bf16[8,3,144,1024]{3,2,1,0:T(8,128)(2,1)} %bitcast.287, bf16[8,3,144,1024]{3,2,1,0:T(8,128)(2,1)} %bitcast.288, ...), custom_call_target="tpu_custom_call" | custom-call | tf_op jit(solution)/shard_map/feed/pallas_call | solution.py:556
  422.5 13.3 %feed_back.2 = (bf16[1024,1152]{1,0:T(8,128)(2,1)}, bf16[1024,1152]{1,0:T(8,128)(2,1)}, bf16[1024,1024]{1,0:T(8,128)(2,1)S(1)}) custom-call(bf16[1024,1024]{1,0:T(8,128)(2,1)S(1)} %copy-done.4, bf16[1024,1152]{1,0:T(8,128)(2,1)} %get-tuple-element.98.gated_ref, bf16[1024,1152]{1,0:T(8,128)(2,1)} %get-tuple-element.99.raised_ref, ...), custom_call_target="tpu_custom_call" | custom-call | tf_op jit(solution)/shard_map/feed_back/pallas_call | solution.py:571
  440.6 14.0 %feed_grads.2 = bf16[8,3,144,1024]{3,2,1,0:T(8,128)(2,1)} custom-call(bf16[1024,1152]{1,0:T(8,128)(2,1)} %get-tuple-element.104.gate_grad_ref, bf16[1024,1152]{1,0:T(8,128)(2,1)} %get-tuple-element.105.up_grad_ref, bf16[1024,1152]{1,0:T(8,128)(2,1)} %get-tuple-element.106.hidden_ref, bf16[1024,1024]{1,0:T(8,128)(2,1)} %copy-done.2, bf16[1024,1024]{1,0:T(8,128)(2,1)} %copy-done.3), custom_call_target="tpu_custom_call" | custom-call | tf_op jit(solution)/shard_map/feed_grads/pallas_call | solution.py:590
  457.0 13.3 %collective-permute-done.46 = bf16[256,1024]{1,0:T(8,128)(2,1)S(1)} collective-permute-done((bf16[256,1024]{1,0:T(8,128)(2,1)S(1)}, bf16[256,1024]{1,0:T(8,128)(2,1)S(1)}, u32[]{:S(2)}, u32[]{:S(2)}) %collective-permute-start.46) | collective-permute-done | bytes 524320 | tf_op jit(solution)/shard_map/ppermute | solution.py:52
  475.4 23.9 %attend_back.1 = (bf16[1024,256]{1,0:T(8,128)(2,1)S(1)}, f32[2048,256]{1,0:T(8,128)S(1)}) custom-call(s32[1024,1]{1,0:T(8,128)S(1)} %copy-done.8, bf16[1024,256]{1,0:T(8,128)(2,1)S(1)} %copy-done.20, bf16[2048,256]{1,0:T(8,128)(2,1)S(1)} %pad_maximum_fusion.14.pairs_ref, bf16[1024,256]{1,0:T(8,128)(2,1)S(1)} %convolution_convert_fusion.10.grad_ref), custom_call_target="tpu_custom_call" | custom-call | tf_op jit(solution)/shard_map/attend_back/pallas_call | solution.py:447
  500.7 14.6 %collective-permute-done.48 = bf16[1024,256]{1,0:T(8,128)(2,1)S(1)} collective-permute-done((bf16[1024,256]{1,0:T(8,128)(2,1)S(1)}, bf16[1024,256]{1,0:T(8,128)(2,1)S(1)}, u32[]{:S(2)}, u32[]{:S(2)}) %collective-permute-start.48) | collective-permute-done | bytes 524320 | tf_op jit(solution)/shard_map/ppermute | solution.py:52
  532.5 11.0 %collective-permute-done.50 = bf16[256,1024]{1,0:T(8,128)(2,1)S(1)} collective-permute-done((bf16[256,1024]{1,0:T(8,128)(2,1)S(1)}, bf16[256,1024]{1,0:T(8,128)(2,1)S(1)}, u32[]{:S(2)}, u32[]{:S(2)}) %collective-permute-start.50) | collective-permute-done | bytes 524320 | tf_op jit(solution)/shard_map/ppermute | solution.py:52
  548.1 9.8 %collective-permute-done.53 = bf16[256,1024]{1,0:T(8,128)(2,1)S(1)} collective-permute-done((bf16[256,1024]{1,0:T(8,128)(2,1)S(1)}, bf16[256,1024]{1,0:T(8,128)(2,1)S(1)}, u32[]{:S(2)}, u32[]{:S(2)}) %collective-permute-start.53) | collective-permute-done | bytes 524320 | tf_op jit(solution)/shard_map/ppermute | solution.py:52
  563.7 9.0 %collective-permute-done.55 = bf16[128,1024]{1,0:T(8,128)(2,1)S(1)} collective-permute-done((bf16[128,1024]{1,0:T(8,128)(2,1)S(1)}, bf16[128,1024]{1,0:T(8,128)(2,1)S(1)}, u32[]{:S(2)}, u32[]{:S(2)}) %collective-permute-start.55) | collective-permute-done | bytes 262176 | tf_op jit(solution)/shard_map/ppermute | solution.py:52
  576.8 15.5 %feed_back.3 = (bf16[2048,576]{1,0:T(8,128)(2,1)S(1)}, bf16[2048,576]{1,0:T(8,128)(2,1)S(1)}, bf16[2048,1024]{1,0:T(8,128)(2,1)}) custom-call(bf16[2048,1024]{1,0:T(8,128)(2,1)} %copy-done.26, bf16[2048,576]{1,0:T(8,128)(2,1)} %copy-done.15, bf16[2048,576]{1,0:T(8,128)(2,1)} %copy-done.16, bf16[4,3,144,1024]{3,2,1,0:T(8,128)(2,1)} %bitcast.296, ...), custom_call_target="tpu_custom_call" | custom-call | tf_op jit(solution)/shard_map/feed_back/pallas_call | solution.py:571
  604.6 10.9 %collective-permute-done.62 = bf16[128,1024]{1,0:T(8,128)(2,1)S(1)} collective-permute-done((bf16[128,1024]{1,0:T(8,128)(2,1)S(1)}, bf16[128,1024]{1,0:T(8,128)(2,1)S(1)}, u32[]{:S(2)}, u32[]{:S(2)}) %collective-permute-start.62) | collective-permute-done | bytes 262176 | tf_op jit(solution)/shard_map/ppermute | solution.py:52
  619.1 17.1 %feed_grads.3 = bf16[4,3,144,1024]{3,2,1,0:T(8,128)(2,1)} custom-call(bf16[2048,576]{1,0:T(8,128)(2,1)} %copy-done.17, bf16[2048,576]{1,0:T(8,128)(2,1)} %copy-done.18, bf16[2048,576]{1,0:T(8,128)(2,1)} %get-tuple-element.125.hidden_ref, bf16[2048,1024]{1,0:T(8,128)(2,1)} %copy-done.27, bf16[2048,1024]{1,0:T(8,128)(2,1)} %copy-done.26), custom_call_target="tpu_custom_call" | custom-call | tf_op jit(solution)/shard_map/feed_grads/pallas_call | solution.py:590
  642.8 9.1 %collective-permute-done.67 = bf16[256,1024]{1,0:T(8,128)(2,1)S(1)} collective-permute-done((bf16[256,1024]{1,0:T(8,128)(2,1)S(1)}, bf16[256,1024]{1,0:T(8,128)(2,1)S(1)}, u32[]{:S(2)}, u32[]{:S(2)}) %collective-permute-start.67) | collective-permute-done | bytes 524320 | tf_op jit(solution)/shard_map/ppermute | solution.py:52
  658.6 13.1 %collective-permute-done.69 = f32[2,256]{1,0:T(2,128)S(1)} collective-permute-done((f32[2,256]{1,0:T(2,128)S(1)}, f32[2,256]{1,0:T(2,128)S(1)}, u32[]{:S(2)}, u32[]{:S(2)}) %collective-permute-start.69) | collective-permute-done | bytes 2080 | tf_op jit(solution)/shard_map/ppermute | solution.py:52
  692.0 9.9 %collective-permute-done.82 = bf16[3072,128]{1,0:T(8,128)(2,1)S(1)} collective-permute-done((bf16[3072,128]{1,0:T(8,128)(2,1)S(1)}, bf16[3072,128]{1,0:T(8,128)(2,1)S(1)}, u32[]{:S(2)}, u32[]{:S(2)}) %collective-permute-start.82) | collective-permute-done | bytes 786464 | tf_op jit(solution)/shard_map/ppermute | solution.py:52
  709.8 14.3 %collective-permute-done.72 = bf16[512,1024]{1,0:T(8,128)(2,1)} collective-permute-done((bf16[512,1024]{1,0:T(8,128)(2,1)}, bf16[512,1024]{1,0:T(8,128)(2,1)}, u32[]{:S(2)}, u32[]{:S(2)}) %collective-permute-start.72) | collective-permute-done | bytes 1048608 | tf_op jit(solution)/shard_map/ppermute | solution.py:52
  754.5 12.7 %all-to-all-start.4 = ((bf16[8,432,128]{2,1,0:T(8,128)(2,1)}), bf16[8,432,128]{2,1,0:T(8,128)(2,1)S(1)}, u32[]{:S(2)}, u32[]{:S(2)}) async-start(bf16[8,432,128]{2,1,0:T(8,128)(2,1)} %copy.208), calls=%async_computation.7 | async-start | bytes 1769472 | tf_op jit(solution)/shard_map/all_to_all | solution.py:119
  806.1 8.7 %all-to-all-done.3 = bf16[8,432,128]{2,1,0:T(8,128)(2,1)S(1)} async-done(((bf16[8,432,128]{2,1,0:T(8,128)(2,1)}), bf16[8,432,128]{2,1,0:T(8,128)(2,1)S(1)}, u32[]{:S(2)}, u32[]{:S(2)}) %all-to-all-start.3) | async-done | bytes 884768 | tf_op jit(solution)/shard_map/all_to_all | solution.py:119
  (745 shorter events, 371.9 us)
Async XLA Ops:
  15.3 83.7 %all-gather.5.cloned.1.call-start = ((), (), s32[]{:S(2)}) async-start(), calls=%async_computation.8 | async-start | bytes 2654208 | tf_op jit(solution)/shard_map/all_gather | solution.py:91
  30.8 65.9 %all-to-all-start.1 = ((bf16[8,864,128]{2,1,0:T(8,128)(2,1)}), bf16[8,864,128]{2,1,0:T(8,128)(2,1)S(1)}, u32[]{:S(2)}, u32[]{:S(2)}) async-start(bf16[8,864,128]{2,1,0:T(8,128)(2,1)} %pad_maximum_fusion.7), calls=%async_computation.1 | async-start | bytes 3538944 | tf_op jit(solution)/shard_map/all_to_all | solution.py:111
  34.5 143.9 %all-gather.7.cloned.1.call-start = ((), (), s32[]{:S(2)}) async-start(), calls=%async_computation.9 | async-start | bytes 4423680 | tf_op jit(solution)/shard_map/all_gather | solution.py:94
  35.2 15.8 %collective-permute-start.1 = (bf16[256,256]{1,0:T(8,128)(2,1)S(1)}, bf16[256,256]{1,0:T(8,128)(2,1)S(1)}, u32[]{:S(2)}, u32[]{:S(2)}) collective-permute-start(bf16[256,256]{1,0:T(8,128)(2,1)S(1)} %get-tuple-element.308), channel_id=1, source_target_pairs={{0,1},{1,17},{2,8},{3,24},{4,9},{5,25},{6,0},{7,16},{8,3},{9,19},{... | collective-permute-start | bytes 393224 | tf_op jit(solution)/shard_map/ppermute | solution.py:52
  40.4 28.5 %collective-permute-start.2 = (bf16[256,256]{1,0:T(8,128)(2,1)S(1)}, bf16[256,256]{1,0:T(8,128)(2,1)S(1)}, u32[]{:S(2)}, u32[]{:S(2)}) collective-permute-start(bf16[256,256]{1,0:T(8,128)(2,1)S(1)} %get-tuple-element.307), channel_id=1, source_target_pairs={{0,8},{1,24},{2,9},{3,25},{4,0},{5,16},{6,1},{7,17},{8,10},{9,26},... | collective-permute-start | bytes 393224 | tf_op jit(solution)/shard_map/ppermute | solution.py:52
  42.7 43.0 %collective-permute-start.3 = (bf16[256,256]{1,0:T(8,128)(2,1)S(1)}, bf16[256,256]{1,0:T(8,128)(2,1)S(1)}, u32[]{:S(2)}, u32[]{:S(2)}) collective-permute-start(bf16[256,256]{1,0:T(8,128)(2,1)S(1)} %get-tuple-element.306), channel_id=1, source_target_pairs={{0,9},{1,25},{2,0},{3,16},{4,1},{5,17},{6,8},{7,24},{8,11},{9,27},... | collective-permute-start | bytes 393224 | tf_op jit(solution)/shard_map/ppermute | solution.py:52
  99.0 125.5 %all-gather.9.cloned.1.call-start = ((), (), s32[]{:S(2)}) async-start(), calls=%async_computation.10 | async-start | bytes 1769472 | tf_op jit(solution)/shard_map/all_gather | solution.py:91
  178.4 231.4 %all-gather.11.cloned.1.call-start = ((), (), s32[]{:S(2)}) async-start(), calls=%async_computation.11 | async-start | bytes 7962624 | tf_op jit(solution)/shard_map/all_gather | solution.py:91
  179.0 16.2 %collective-permute-start.14 = (bf16[256,1024]{1,0:T(8,128)(2,1)S(1)}, bf16[256,1024]{1,0:T(8,128)(2,1)S(1)}, u32[]{:S(2)}, u32[]{:S(2)}) collective-permute-start(bf16[256,1024]{1,0:T(8,128)(2,1)S(1)} %get-tuple-element.228), channel_id=1, source_target_pairs={{0,16},{1,17},{2,18},{3,19},{4,20},{5,21},{6,22},{7,23},{8,24},{9,... | collective-permute-start | bytes 1572872 | tf_op jit(solution)/shard_map/ppermute | solution.py:52
  224.6 433.8 %reduce-scatter.4.cloned.1.call-start = ((), (), s32[]{:S(2)}) async-start(), calls=%async_computation.12 | async-start | bytes 7962624 | tf_op jit(solution)/shard_map/reduce_scatter | solution.py:103
  293.9 28.8 %collective-permute-start.31 = (bf16[1024,256]{1,0:T(8,128)(2,1)S(1)}, bf16[1024,256]{1,0:T(8,128)(2,1)}, u32[]{:S(2)}, u32[]{:S(2)}) collective-permute-start(bf16[1024,256]{1,0:T(8,128)(2,1)S(1)} %get-tuple-element.88), channel_id=1, source_target_pairs={{0,2},{1,3},{2,4},{3,5},{4,6},{5,7},{8,10},{9,11},{10,12},{11,13},... | collective-permute-start | bytes 1572872 | tf_op jit(solution)/shard_map/ppermute | solution.py:52
  300.5 23.3 %collective-permute-start.32 = (bf16[256,256]{1,0:T(8,128)(2,1)S(1)}, bf16[256,256]{1,0:T(8,128)(2,1)S(1)}, u32[]{:S(2)}, u32[]{:S(2)}) collective-permute-start(bf16[256,256]{1,0:T(8,128)(2,1)S(1)} %get-tuple-element.304), channel_id=1, source_target_pairs={{0,1},{1,17},{2,8},{3,24},{4,9},{5,25},{6,0},{7,16},{8,3},{9,19},{... | collective-permute-start | bytes 393224 | tf_op jit(solution)/shard_map/ppermute | solution.py:52
  345.2 38.9 %collective-permute-start.34 = (bf16[256,1024]{1,0:T(8,128)(2,1)}, bf16[256,1024]{1,0:T(8,128)(2,1)}, u32[]{:S(2)}, u32[]{:S(2)}) collective-permute-start(bf16[256,1024]{1,0:T(8,128)(2,1)} %fusion.69), channel_id=1, source_target_pairs={{0,8},{1,9},{2,10},{3,11},{4,12},{5,13},{6,14},{7,15},{8,0},{9,1},... | collective-permute-start | bytes 1572872 | tf_op jit(solution)/shard_map/ppermute | solution.py:52
  353.9 21.9 %collective-permute-start.35 = (bf16[256,256]{1,0:T(8,128)(2,1)S(1)}, bf16[256,256]{1,0:T(8,128)(2,1)S(1)}, u32[]{:S(2)}, u32[]{:S(2)}) collective-permute-start(bf16[256,256]{1,0:T(8,128)(2,1)S(1)} %copy-done.119), channel_id=1, source_target_pairs={{0,8},{1,24},{2,9},{3,25},{4,0},{5,16},{6,1},{7,17},{8,10},{9,26},... | collective-permute-start | bytes 393224 | tf_op jit(solution)/shard_map/ppermute | solution.py:52
  353.9 22.1 %collective-permute-start.38 = (bf16[256,256]{1,0:T(8,128)(2,1)S(1)}, bf16[256,256]{1,0:T(8,128)(2,1)S(1)}, u32[]{:S(2)}, u32[]{:S(2)}) collective-permute-start(bf16[256,256]{1,0:T(8,128)(2,1)S(1)} %copy-done.118), channel_id=1, source_target_pairs={{0,9},{1,25},{2,0},{3,16},{4,1},{5,17},{6,8},{7,24},{8,11},{9,27},... | collective-permute-start | bytes 393224 | tf_op jit(solution)/shard_map/ppermute | solution.py:52
  376.5 20.3 %collective-permute-start.41 = (bf16[256,1024]{1,0:T(8,128)(2,1)S(1)}, bf16[256,1024]{1,0:T(8,128)(2,1)S(1)}, u32[]{:S(2)}, u32[]{:S(2)}) collective-permute-start(bf16[256,1024]{1,0:T(8,128)(2,1)S(1)} %bitcast.327), channel_id=1, source_target_pairs={{0,8},{1,9},{2,10},{3,11},{4,12},{5,13},{6,14},{7,15},{8,0},{9,1},... | collective-permute-start | bytes 1572872 | tf_op jit(solution)/shard_map/ppermute | solution.py:52
  386.0 21.7 %collective-permute-start.37 = (bf16[256,1024]{1,0:T(8,128)(2,1)S(1)}, bf16[256,1024]{1,0:T(8,128)(2,1)S(1)}, u32[]{:S(2)}, u32[]{:S(2)}) collective-permute-start(bf16[256,1024]{1,0:T(8,128)(2,1)S(1)} %fusion.51), channel_id=1, source_target_pairs={{0,8},{1,9},{2,10},{3,11},{4,12},{5,13},{6,14},{7,15},{8,0},{9,1},... | collective-permute-start | bytes 1572872 | tf_op jit(solution)/shard_map/ppermute | solution.py:52
  386.2 21.5 %collective-permute-start.40 = (bf16[256,1024]{1,0:T(8,128)(2,1)S(1)}, bf16[256,1024]{1,0:T(8,128)(2,1)S(1)}, u32[]{:S(2)}, u32[]{:S(2)}) collective-permute-start(bf16[256,1024]{1,0:T(8,128)(2,1)S(1)} %bitcast.328), channel_id=1, source_target_pairs={{0,1},{1,0},{2,3},{3,2},{4,5},{5,4},{6,7},{7,6},{8,9},{9,8},{10,11... | collective-permute-start | bytes 1572872 | tf_op jit(solution)/shard_map/ppermute | solution.py:52
  439.0 15.6 %collective-permute-start.44 = (bf16[256,1024]{1,0:T(8,128)(2,1)S(1)}, bf16[256,1024]{1,0:T(8,128)(2,1)S(1)}, u32[]{:S(2)}, u32[]{:S(2)}) collective-permute-start(bf16[256,1024]{1,0:T(8,128)(2,1)S(1)} %add_convert_fusion.2), channel_id=1, source_target_pairs={{0,8},{1,9},{2,10},{3,11},{4,12},{5,13},{6,14},{7,15},{8,0},{9,1},... | collective-permute-start | bytes 1572872 | tf_op jit(solution)/shard_map/ppermute | solution.py:52
  499.4 15.9 %collective-permute-start.48 = (bf16[1024,256]{1,0:T(8,128)(2,1)S(1)}, bf16[1024,256]{1,0:T(8,128)(2,1)S(1)}, u32[]{:S(2)}, u32[]{:S(2)}) collective-permute-start(bf16[1024,256]{1,0:T(8,128)(2,1)S(1)} %slice.718), channel_id=1, source_target_pairs={{2,0},{3,1},{4,2},{5,3},{6,4},{7,5},{10,8},{11,9},{12,10},{13,11},... | collective-permute-start | bytes 1572872 | tf_op jit(solution)/shard_map/ppermute | solution.py:52
  516.3 226.6 %reduce-scatter.6.cloned.1.call-start = ((), (), s32[]{:S(2)}) async-start(), calls=%async_computation.13 | async-start | bytes 4423680 | tf_op jit(solution)/shard_map/reduce_scatter | solution.py:108
  545.1 17.8 %collective-permute-start.54 = (bf16[256,1024]{1,0:T(8,128)(2,1)S(1)}, bf16[256,1024]{1,0:T(8,128)(2,1)S(1)}, u32[]{:S(2)}, u32[]{:S(2)}) collective-permute-start(bf16[256,1024]{1,0:T(8,128)(2,1)S(1)} %get-tuple-element.222), channel_id=1, source_target_pairs={{0,16},{1,17},{2,18},{3,19},{4,20},{5,21},{6,22},{7,23},{8,24},{9,... | collective-permute-start | bytes 1572872 | tf_op jit(solution)/shard_map/ppermute | solution.py:52
  548.0 25.0 %collective-permute-start.57 = (bf16[256,1024]{1,0:T(8,128)(2,1)S(1)}, bf16[256,1024]{1,0:T(8,128)(2,1)S(1)}, u32[]{:S(2)}, u32[]{:S(2)}) collective-permute-start(bf16[256,1024]{1,0:T(8,128)(2,1)S(1)} %get-tuple-element.222), channel_id=1, source_target_pairs={{0,1},{1,0},{2,3},{3,2},{4,5},{5,4},{6,7},{7,6},{8,9},{9,8},{10,11... | collective-permute-start | bytes 1572872 | tf_op jit(solution)/shard_map/ppermute | solution.py:52
  597.2 20.5 %collective-permute-start.51 = (bf16[512,1024]{1,0:T(8,128)(2,1)S(1)}, bf16[512,1024]{1,0:T(8,128)(2,1)S(1)}, u32[]{:S(2)}, u32[]{:S(2)}) collective-permute-start(bf16[512,1024]{1,0:T(8,128)(2,1)S(1)} %pad_maximum_fusion.18), channel_id=1, source_target_pairs={{0,1},{1,0},{2,3},{3,2},{4,5},{5,4},{6,7},{7,6},{8,9},{9,8},{10,11... | collective-permute-start | bytes 3145736 | tf_op jit(solution)/shard_map/ppermute | solution.py:52
  615.7 20.5 %collective-permute-start.63 = (bf16[256,1024]{1,0:T(8,128)(2,1)S(1)}, bf16[256,1024]{1,0:T(8,128)(2,1)}, u32[]{:S(2)}, u32[]{:S(2)}) collective-permute-start(bf16[256,1024]{1,0:T(8,128)(2,1)S(1)} %pad_maximum_fusion.27), channel_id=1, source_target_pairs={{0,8},{1,9},{2,10},{3,11},{4,12},{5,13},{6,14},{7,15},{8,0},{9,1},... | collective-permute-start | bytes 1572872 | tf_op jit(solution)/shard_map/ppermute | solution.py:52
  616.9 20.2 %collective-permute-start.65 = (bf16[256,1024]{1,0:T(8,128)(2,1)}, bf16[256,1024]{1,0:T(8,128)(2,1)S(1)}, u32[]{:S(2)}, u32[]{:S(2)}) collective-permute-start(bf16[256,1024]{1,0:T(8,128)(2,1)} %pad_maximum_fusion.28), channel_id=1, source_target_pairs={{0,16},{1,17},{2,18},{3,19},{4,20},{5,21},{6,22},{7,23},{8,24},{9,... | collective-permute-start | bytes 1572872 | tf_op jit(solution)/shard_map/ppermute | solution.py:52
  617.9 23.7 %collective-permute-start.52 = (bf16[256,1024]{1,0:T(8,128)(2,1)S(1)}, bf16[256,1024]{1,0:T(8,128)(2,1)S(1)}, u32[]{:S(2)}, u32[]{:S(2)}) collective-permute-start(bf16[256,1024]{1,0:T(8,128)(2,1)S(1)} %add_convert_fusion), channel_id=1, source_target_pairs={{0,8},{1,9},{2,10},{3,11},{4,12},{5,13},{6,14},{7,15},{8,0},{9,1},... | collective-permute-start | bytes 1572872 | tf_op jit(solution)/shard_map/ppermute | solution.py:52
  658.4 157.3 %reduce-scatter.8.cloned.1.call-start = ((), (), s32[]{:S(2)}) async-start(), calls=%async_computation.14 | async-start | bytes 2293760 | tf_op jit(solution)/shard_map/reduce_scatter | solution.py:108
  681.5 20.4 %collective-permute-start.82 = (bf16[3072,128]{1,0:T(8,128)(2,1)S(1)}, bf16[3072,128]{1,0:T(8,128)(2,1)S(1)}, u32[]{:S(2)}, u32[]{:S(2)}) collective-permute-start(bf16[3072,128]{1,0:T(8,128)(2,1)S(1)} %dynamic-slice_bitcast_fusion.1), channel_id=1, source_target_pairs={{0,16},{1,17},{2,18},{3,19},{4,20},{5,21},{6,22},{7,23},{8,24},{9,... | collective-permute-start | bytes 2359304 | tf_op jit(solution)/shard_map/ppermute | solution.py:52
  689.0 35.1 %collective-permute-start.72 = (bf16[512,1024]{1,0:T(8,128)(2,1)}, bf16[512,1024]{1,0:T(8,128)(2,1)}, u32[]{:S(2)}, u32[]{:S(2)}) collective-permute-start(bf16[512,1024]{1,0:T(8,128)(2,1)} %dynamic-slice_bitcast_fusion), channel_id=1, source_target_pairs={{0,16},{1,17},{2,18},{3,19},{4,20},{5,21},{6,22},{7,23},{8,24},{9,... | collective-permute-start | bytes 3145736 | tf_op jit(solution)/shard_map/ppermute | solution.py:52
  754.5 43.2 %all-to-all-start.4 = ((bf16[8,432,128]{2,1,0:T(8,128)(2,1)}), bf16[8,432,128]{2,1,0:T(8,128)(2,1)S(1)}, u32[]{:S(2)}, u32[]{:S(2)}) async-start(bf16[8,432,128]{2,1,0:T(8,128)(2,1)} %copy.208), calls=%async_computation.7 | async-start | bytes 1769472 | tf_op jit(solution)/shard_map/all_to_all | solution.py:119
  797.6 17.1 %all-to-all-start.3 = ((bf16[8,432,128]{2,1,0:T(8,128)(2,1)}), bf16[8,432,128]{2,1,0:T(8,128)(2,1)S(1)}, u32[]{:S(2)}, u32[]{:S(2)}) async-start(bf16[8,432,128]{2,1,0:T(8,128)(2,1)} %copy.205), calls=%async_computation.6 | async-start | bytes 1769472 | tf_op jit(solution)/shard_map/all_to_all | solution.py:119
  (214 other events, 2051.3 us)
Sparse Core Ops, SparseCore 0:
  23.5 74.1 all-gather.4
  99.3 78.9 all-gather.6
  181.0 43.4 all-gather.8
  226.5 119.4 all-gather.10
  516.4 141.5 reduce-scatter.3
  660.3 75.5 reduce-scatter.5
  743.0 54.2 reduce-scatter.7

commit v3 on v2

--- a/solution.py
+++ b/solution.py
@@ -167,13 +167,26 @@
 
     def total(self, values):
         sizes = (self.halves, 2, self.depth, self.rings, 2)
-        for axis, size in enumerate(sizes):
-            bit = 1
-            while bit < size:
-                values = values + self.move(
-                    values, lambda *place: (*place[:axis], place[axis] ^ bit, *place[axis + 1 :])
-                )
-                bit *= 2
+        bits = [
+            (axis, 1 << power)
+            for axis, size in enumerate(sizes)
+            for power in range(size.bit_length() - 1)
+        ]
+
+        def moved(values, flips):
+            def goal(*place):
+                place = list(place)
+                for axis, bit in flips:
+                    place[axis] ^= bit
+                return tuple(place)
+
+            return self.move(values, goal)
+
+        for k in range(0, len(bits), 2):
+            own = values + moved(values, bits[k : k + 1])
+            if k + 1 < len(bits):
+                own = own + (moved(values, bits[k + 1 : k + 2]) + moved(values, bits[k : k + 2]))
+            values = own
         return values
 
 

time: 851 us -> 850 us (level)
    ppermute x79 -> x81, waiting for transfers between devices: 321 us -> 315 us  [move(): return lax.ppermute(values, AXES, self.route(target))]
    unnamed x351 -> x349, local copies, waits for them, and re-layouts: 39.7 us -> 36.1 us
    ppermute x79 -> x81, starting transfers between devices: 111 us -> 112 us  [move(): return lax.ppermute(values, AXES, self.route(target))]
  transfers between devices with their start and end apart: 96 -> 98, of which waited for: 59 -> 61; matrix products, arithmetic and copies ran while one was open for 13% -> 13% of each run, Pallas kernels for 10% -> 10%
where the time goes in v3:
time: 850 us; the launch traced here: 841 us
  waiting for transfers between devices  387 us (46%)
  starting transfers between devices  160 us (19%)
  Pallas kernels  136 us (16%)
  local copies, waits for them, and re-layouts  69 us (8%)
  other arithmetic  56.6 us (7%)
  between operations  17.5 us (2%)
  matrix products  16.3 us (2%)
    ppermute x81, waiting for transfers between devices, move(): return lax.ppermute(values, AXES, self.route(target))  315 us
    ppermute x81, starting transfers between devices, move(): return lax.ppermute(values, AXES, self.route(target))  112 us
    all_gather x1, waiting for transfers between devices, gather_rest(): return lax.all_gather(values, ('ring', 'depth'), axis=0, tiled=True)  37.7 us
    unnamed x349, local copies, waits for them, and re-layouts  36.1 us
    pallas_call x2, Pallas kernels, feed_grads_call(): pl.pallas_call(feed_grads_kernel, grid=(3,), in_specs=[wide_spec] * 3 + [...  31 us
    pallas_call x2, Pallas kernels, feed_back_call(): pl.pallas_call(feed_back_kernel, grid=(total // rows,), in_specs=[row_spe...  28.8 us
    pallas_call x2, Pallas kernels, feed_call(): pl.pallas_call(feed_kernel, grid=(total // rows,), in_specs=[row_spec(row...  26.7 us
    all_to_all x3, starting transfers between devices, whole_rows(): parts = lax.all_to_all(parts, SQUARE, 0, 0, tiled=True)  26 us
  transfers between devices with their start and end apart: 98, of which 61 were waited for; matrix products, arithmetic and copies ran while one was open for 13% of the time, Pallas kernels for 10%

profile of v3, /device:TPU:0, one launch (start us, length us, event | category | flops | bytes accessed | tf_op | source)
XLA Modules:
  0.0 841.4 jit_solution(10126028696574310436)
XLA Ops:
  51.1 17.8 %collective-permute-done.2 = bf16[256,256]{1,0:T(8,128)(2,1)S(1)} collective-permute-done((bf16[256,256]{1,0:T(8,128)(2,1)S(1)}, bf16[256,256]{1,0:T(8,128)(2,1)S(1)}, u32[]{:S(2)}, u32[]{:S(2)}) %collective-permute-start.2) | collective-permute-done | bytes 131104 | tf_op jit(solution)/shard_map/ppermute | solution.py:52
  68.9 16.8 %collective-permute-done.3 = bf16[256,256]{1,0:T(8,128)(2,1)S(1)} collective-permute-done((bf16[256,256]{1,0:T(8,128)(2,1)S(1)}, bf16[256,256]{1,0:T(8,128)(2,1)S(1)}, u32[]{:S(2)}, u32[]{:S(2)}) %collective-permute-start.3) | collective-permute-done | bytes 131104 | tf_op jit(solution)/shard_map/ppermute | solution.py:52
  126.0 13.0 %collective-permute-done.12 = bf16[256,1024]{1,0:T(8,128)(2,1)} collective-permute-done((bf16[256,1024]{1,0:T(8,128)(2,1)}, bf16[256,1024]{1,0:T(8,128)(2,1)}, u32[]{:S(2)}, u32[]{:S(2)}) %collective-permute-start.12) | collective-permute-done | bytes 524320 | tf_op jit(solution)/shard_map/ppermute | solution.py:52
  140.7 37.7 %all-gather.7.cloned.1.call-done = bf16[1728,1024]{1,0:T(8,128)(2,1)} async-done(((bf16[432,1024]{1,0:T(8,128)(2,1)}), bf16[1728,1024]{1,0:T(8,128)(2,1)}) %all-gather.7.cloned.1.call-update) | async-done | bytes 3538960 | tf_op jit(solution)/shard_map/all_gather | solution.py:94
  180.6 12.1 %collective-permute-done.13 = bf16[256,1024]{1,0:T(8,128)(2,1)S(1)} collective-permute-done((bf16[256,1024]{1,0:T(8,128)(2,1)S(1)}, bf16[256,1024]{1,0:T(8,128)(2,1)S(1)}, u32[]{:S(2)}, u32[]{:S(2)}) %collective-permute-start.13) | collective-permute-done | bytes 524320 | tf_op jit(solution)/shard_map/ppermute | solution.py:52
  206.5 14.0 %feed.2 = (bf16[2048,576]{1,0:T(8,128)(2,1)S(1)}, bf16[2048,576]{1,0:T(8,128)(2,1)S(1)}, bf16[2048,576]{1,0:T(8,128)(2,1)}, bf16[2048,1024]{1,0:T(8,128)(2,1)}) custom-call(bf16[2048,1024]{1,0:T(8,128)(2,1)} %copy-done.27, bf16[4,3,144,1024]{3,2,1,0:T(8,128)(2,1)} %bitcast.293, bf16[4,3,144,1024]{3,2,1,0:T(8,128)(2,1)} %bitcast.294, ...), custom_call_target="tpu_custom_call" | custom-call | tf_op jit(solution)/shard_map/feed/pallas_call | solution.py:569
  236.6 11.6 %collective-permute-done.22 = bf16[128,1024]{1,0:T(8,128)(2,1)S(1)} collective-permute-done((bf16[128,1024]{1,0:T(8,128)(2,1)S(1)}, bf16[128,1024]{1,0:T(8,128)(2,1)S(1)}, u32[]{:S(2)}, u32[]{:S(2)}) %collective-permute-start.22) | collective-permute-done | bytes 262176 | tf_op jit(solution)/shard_map/ppermute | solution.py:52
  252.9 10.2 %collective-permute-done.23 = bf16[256,1024]{1,0:T(8,128)(2,1)S(1)} collective-permute-done((bf16[256,1024]{1,0:T(8,128)(2,1)S(1)}, bf16[256,1024]{1,0:T(8,128)(2,1)S(1)}, u32[]{:S(2)}, u32[]{:S(2)}) %collective-permute-start.23) | collective-permute-done | bytes 524320 | tf_op jit(solution)/shard_map/ppermute | solution.py:52
  272.6 9.2 %collective-permute-done.27 = bf16[256,1024]{1,0:T(8,128)(2,1)} collective-permute-done((bf16[256,1024]{1,0:T(8,128)(2,1)}, bf16[256,1024]{1,0:T(8,128)(2,1)}, u32[]{:S(2)}, u32[]{:S(2)}) %collective-permute-start.27) | collective-permute-done | bytes 524320 | tf_op jit(solution)/shard_map/ppermute | solution.py:52
  303.1 19.6 %collective-permute-done.31 = bf16[1024,256]{1,0:T(8,128)(2,1)} collective-permute-done((bf16[1024,256]{1,0:T(8,128)(2,1)S(1)}, bf16[1024,256]{1,0:T(8,128)(2,1)}, u32[]{:S(2)}, u32[]{:S(2)}) %collective-permute-start.31) | collective-permute-done | bytes 524320 | tf_op jit(solution)/shard_map/ppermute | solution.py:52
  323.8 16.7 %attend.1 = bf16[1024,256]{1,0:T(8,128)(2,1)S(1)} custom-call(s32[1024,1]{1,0:T(8,128)S(1)} %copy.191.offsets_ref, bf16[1024,256]{1,0:T(8,128)(2,1)S(1)} %get-tuple-element.87.queries_ref, bf16[2048,256]{1,0:T(8,128)(2,1)S(1)} %pad_maximum_fusion.14.pairs_ref), custom_call_target="tpu_custom_call" | custom-call | tf_op jit(solution)/shard_map/attend/pallas_call | solution.py:447
  345.2 8.7 %collective-permute-start.34 = (bf16[256,1024]{1,0:T(8,128)(2,1)}, bf16[256,1024]{1,0:T(8,128)(2,1)}, u32[]{:S(2)}, u32[]{:S(2)}) collective-permute-start(bf16[256,1024]{1,0:T(8,128)(2,1)} %fusion.69), channel_id=1, source_target_pairs={{0,8},{1,9},{2,10},{3,11},{4,12},{5,13},{6,14},{7,15},{8,0},{9,1},... | collective-permute-start | bytes 1572872 | tf_op jit(solution)/shard_map/ppermute | solution.py:52
  353.9 19.6 %collective-permute-start.38 = (bf16[256,256]{1,0:T(8,128)(2,1)S(1)}, bf16[256,256]{1,0:T(8,128)(2,1)S(1)}, u32[]{:S(2)}, u32[]{:S(2)}) collective-permute-start(bf16[256,256]{1,0:T(8,128)(2,1)S(1)} %copy-done.117), channel_id=1, source_target_pairs={{0,9},{1,25},{2,0},{3,16},{4,1},{5,17},{6,8},{7,24},{8,11},{9,27},... | collective-permute-start | bytes 393224 | tf_op jit(solution)/shard_map/ppermute | solution.py:52
  386.1 10.6 %collective-permute-done.41 = bf16[256,1024]{1,0:T(8,128)(2,1)S(1)} collective-permute-done((bf16[256,1024]{1,0:T(8,128)(2,1)S(1)}, bf16[256,1024]{1,0:T(8,128)(2,1)S(1)}, u32[]{:S(2)}, u32[]{:S(2)}) %collective-permute-start.41) | collective-permute-done | bytes 524320 | tf_op jit(solution)/shard_map/ppermute | solution.py:52
  397.3 10.4 %collective-permute-done.37 = bf16[256,1024]{1,0:T(8,128)(2,1)S(1)} collective-permute-done((bf16[256,1024]{1,0:T(8,128)(2,1)S(1)}, bf16[256,1024]{1,0:T(8,128)(2,1)S(1)}, u32[]{:S(2)}, u32[]{:S(2)}) %collective-permute-start.37) | collective-permute-done | bytes 524320 | tf_op jit(solution)/shard_map/ppermute | solution.py:52
  409.8 12.7 %feed.3 = (bf16[1024,1152]{1,0:T(8,128)(2,1)}, bf16[1024,1152]{1,0:T(8,128)(2,1)}, bf16[1024,1152]{1,0:T(8,128)(2,1)}, bf16[1024,1024]{1,0:T(8,128)(2,1)S(1)}) custom-call(bf16[1024,1024]{1,0:T(8,128)(2,1)S(1)} %pad_maximum_fusion.2.normed_ref, bf16[8,3,144,1024]{3,2,1,0:T(8,128)(2,1)} %bitcast.287, bf16[8,3,144,1024]{3,2,1,0:T(8,128)(2,1)} %bitcast.288, ...), custom_call_target="tpu_custom_call" | custom-call | tf_op jit(solution)/shard_map/feed/pallas_call | solution.py:569
  422.5 13.3 %feed_back.2 = (bf16[1024,1152]{1,0:T(8,128)(2,1)}, bf16[1024,1152]{1,0:T(8,128)(2,1)}, bf16[1024,1024]{1,0:T(8,128)(2,1)S(1)}) custom-call(bf16[1024,1024]{1,0:T(8,128)(2,1)S(1)} %copy-done.4, bf16[1024,1152]{1,0:T(8,128)(2,1)} %get-tuple-element.98.gated_ref, bf16[1024,1152]{1,0:T(8,128)(2,1)} %get-tuple-element.99.raised_ref, ...), custom_call_target="tpu_custom_call" | custom-call | tf_op jit(solution)/shard_map/feed_back/pallas_call | solution.py:584
  440.6 14.0 %feed_grads.2 = bf16[8,3,144,1024]{3,2,1,0:T(8,128)(2,1)} custom-call(bf16[1024,1152]{1,0:T(8,128)(2,1)} %get-tuple-element.104.gate_grad_ref, bf16[1024,1152]{1,0:T(8,128)(2,1)} %get-tuple-element.105.up_grad_ref, bf16[1024,1152]{1,0:T(8,128)(2,1)} %get-tuple-element.106.hidden_ref, bf16[1024,1024]{1,0:T(8,128)(2,1)} %copy-done.2, bf16[1024,1024]{1,0:T(8,128)(2,1)} %copy-done.3), custom_call_target="tpu_custom_call" | custom-call | tf_op jit(solution)/shard_map/feed_grads/pallas_call | solution.py:603
  457.0 13.2 %collective-permute-done.46 = bf16[256,1024]{1,0:T(8,128)(2,1)S(1)} collective-permute-done((bf16[256,1024]{1,0:T(8,128)(2,1)S(1)}, bf16[256,1024]{1,0:T(8,128)(2,1)S(1)}, u32[]{:S(2)}, u32[]{:S(2)}) %collective-permute-start.46) | collective-permute-done | bytes 524320 | tf_op jit(solution)/shard_map/ppermute | solution.py:52
  475.4 23.9 %attend_back.1 = (bf16[1024,256]{1,0:T(8,128)(2,1)S(1)}, f32[2048,256]{1,0:T(8,128)S(1)}) custom-call(s32[1024,1]{1,0:T(8,128)S(1)} %copy-done.8, bf16[1024,256]{1,0:T(8,128)(2,1)S(1)} %copy-done.20, bf16[2048,256]{1,0:T(8,128)(2,1)S(1)} %pad_maximum_fusion.14.pairs_ref, bf16[1024,256]{1,0:T(8,128)(2,1)S(1)} %convolution_convert_fusion.10.grad_ref), custom_call_target="tpu_custom_call" | custom-call | tf_op jit(solution)/shard_map/attend_back/pallas_call | solution.py:460
  500.7 14.6 %collective-permute-done.48 = bf16[1024,256]{1,0:T(8,128)(2,1)S(1)} collective-permute-done((bf16[1024,256]{1,0:T(8,128)(2,1)S(1)}, bf16[1024,256]{1,0:T(8,128)(2,1)S(1)}, u32[]{:S(2)}, u32[]{:S(2)}) %collective-permute-start.48) | collective-permute-done | bytes 524320 | tf_op jit(solution)/shard_map/ppermute | solution.py:52
  532.5 11.0 %collective-permute-done.50 = bf16[256,1024]{1,0:T(8,128)(2,1)S(1)} collective-permute-done((bf16[256,1024]{1,0:T(8,128)(2,1)S(1)}, bf16[256,1024]{1,0:T(8,128)(2,1)S(1)}, u32[]{:S(2)}, u32[]{:S(2)}) %collective-permute-start.50) | collective-permute-done | bytes 524320 | tf_op jit(solution)/shard_map/ppermute | solution.py:52
  548.1 9.8 %collective-permute-done.53 = bf16[256,1024]{1,0:T(8,128)(2,1)S(1)} collective-permute-done((bf16[256,1024]{1,0:T(8,128)(2,1)S(1)}, bf16[256,1024]{1,0:T(8,128)(2,1)S(1)}, u32[]{:S(2)}, u32[]{:S(2)}) %collective-permute-start.53) | collective-permute-done | bytes 524320 | tf_op jit(solution)/shard_map/ppermute | solution.py:52
  563.7 9.0 %collective-permute-done.55 = bf16[128,1024]{1,0:T(8,128)(2,1)S(1)} collective-permute-done((bf16[128,1024]{1,0:T(8,128)(2,1)S(1)}, bf16[128,1024]{1,0:T(8,128)(2,1)S(1)}, u32[]{:S(2)}, u32[]{:S(2)}) %collective-permute-start.55) | collective-permute-done | bytes 262176 | tf_op jit(solution)/shard_map/ppermute | solution.py:52
  576.8 15.5 %feed_back.3 = (bf16[2048,576]{1,0:T(8,128)(2,1)S(1)}, bf16[2048,576]{1,0:T(8,128)(2,1)S(1)}, bf16[2048,1024]{1,0:T(8,128)(2,1)}) custom-call(bf16[2048,1024]{1,0:T(8,128)(2,1)} %copy-done.26, bf16[2048,576]{1,0:T(8,128)(2,1)} %copy-done.15, bf16[2048,576]{1,0:T(8,128)(2,1)} %copy-done.16, bf16[4,3,144,1024]{3,2,1,0:T(8,128)(2,1)} %bitcast.296, ...), custom_call_target="tpu_custom_call" | custom-call | tf_op jit(solution)/shard_map/feed_back/pallas_call | solution.py:584
  604.5 10.9 %collective-permute-done.62 = bf16[128,1024]{1,0:T(8,128)(2,1)S(1)} collective-permute-done((bf16[128,1024]{1,0:T(8,128)(2,1)S(1)}, bf16[128,1024]{1,0:T(8,128)(2,1)S(1)}, u32[]{:S(2)}, u32[]{:S(2)}) %collective-permute-start.62) | collective-permute-done | bytes 262176 | tf_op jit(solution)/shard_map/ppermute | solution.py:52
  619.1 17.1 %feed_grads.3 = bf16[4,3,144,1024]{3,2,1,0:T(8,128)(2,1)} custom-call(bf16[2048,576]{1,0:T(8,128)(2,1)} %copy-done.17, bf16[2048,576]{1,0:T(8,128)(2,1)} %copy-done.18, bf16[2048,576]{1,0:T(8,128)(2,1)} %get-tuple-element.125.hidden_ref, bf16[2048,1024]{1,0:T(8,128)(2,1)} %copy-done.27, bf16[2048,1024]{1,0:T(8,128)(2,1)} %copy-done.26), custom_call_target="tpu_custom_call" | custom-call | tf_op jit(solution)/shard_map/feed_grads/pallas_call | solution.py:603
  642.7 9.2 %collective-permute-done.67 = bf16[256,1024]{1,0:T(8,128)(2,1)S(1)} collective-permute-done((bf16[256,1024]{1,0:T(8,128)(2,1)S(1)}, bf16[256,1024]{1,0:T(8,128)(2,1)S(1)}, u32[]{:S(2)}, u32[]{:S(2)}) %collective-permute-start.67) | collective-permute-done | bytes 524320 | tf_op jit(solution)/shard_map/ppermute | solution.py:52
  657.6 13.3 %collective-permute-done.69 = f32[2,256]{1,0:T(2,128)S(1)} collective-permute-done((f32[2,256]{1,0:T(2,128)S(1)}, f32[2,256]{1,0:T(2,128)S(1)}, u32[]{:S(2)}, u32[]{:S(2)}) %collective-permute-start.69) | collective-permute-done | bytes 2080 | tf_op jit(solution)/shard_map/ppermute | solution.py:52
  690.3 9.9 %collective-permute-done.84 = bf16[3072,128]{1,0:T(8,128)(2,1)S(1)} collective-permute-done((bf16[3072,128]{1,0:T(8,128)(2,1)S(1)}, bf16[3072,128]{1,0:T(8,128)(2,1)S(1)}, u32[]{:S(2)}, u32[]{:S(2)}) %collective-permute-start.84) | collective-permute-done | bytes 786464 | tf_op jit(solution)/shard_map/ppermute | solution.py:52
  707.9 14.3 %collective-permute-done.72 = bf16[512,1024]{1,0:T(8,128)(2,1)} collective-permute-done((bf16[512,1024]{1,0:T(8,128)(2,1)}, bf16[512,1024]{1,0:T(8,128)(2,1)}, u32[]{:S(2)}, u32[]{:S(2)}) %collective-permute-start.72) | collective-permute-done | bytes 1048608 | tf_op jit(solution)/shard_map/ppermute | solution.py:52
  755.2 13.9 %all-to-all-start.4 = ((bf16[8,432,128]{2,1,0:T(8,128)(2,1)}), bf16[8,432,128]{2,1,0:T(8,128)(2,1)S(1)}, u32[]{:S(2)}, u32[]{:S(2)}) async-start(bf16[8,432,128]{2,1,0:T(8,128)(2,1)} %copy.208), calls=%async_computation.7 | async-start | bytes 1769472 | tf_op jit(solution)/shard_map/all_to_all | solution.py:119
  (745 shorter events, 370.4 us)
Async XLA Ops:
  15.3 83.7 %all-gather.5.cloned.1.call-start = ((), (), s32[]{:S(2)}) async-start(), calls=%async_computation.8 | async-start | bytes 2654208 | tf_op jit(solution)/shard_map/all_gather | solution.py:91
  30.8 65.9 %all-to-all-start.1 = ((bf16[8,864,128]{2,1,0:T(8,128)(2,1)}), bf16[8,864,128]{2,1,0:T(8,128)(2,1)S(1)}, u32[]{:S(2)}, u32[]{:S(2)}) async-start(bf16[8,864,128]{2,1,0:T(8,128)(2,1)} %pad_maximum_fusion.7), calls=%async_computation.1 | async-start | bytes 3538944 | tf_op jit(solution)/shard_map/all_to_all | solution.py:111
  34.5 143.9 %all-gather.7.cloned.1.call-start = ((), (), s32[]{:S(2)}) async-start(), calls=%async_computation.9 | async-start | bytes 4423680 | tf_op jit(solution)/shard_map/all_gather | solution.py:94
  35.2 15.8 %collective-permute-start.1 = (bf16[256,256]{1,0:T(8,128)(2,1)S(1)}, bf16[256,256]{1,0:T(8,128)(2,1)S(1)}, u32[]{:S(2)}, u32[]{:S(2)}) collective-permute-start(bf16[256,256]{1,0:T(8,128)(2,1)S(1)} %get-tuple-element.308), channel_id=1, source_target_pairs={{0,1},{1,17},{2,8},{3,24},{4,9},{5,25},{6,0},{7,16},{8,3},{9,19},{... | collective-permute-start | bytes 393224 | tf_op jit(solution)/shard_map/ppermute | solution.py:52
  40.4 28.5 %collective-permute-start.2 = (bf16[256,256]{1,0:T(8,128)(2,1)S(1)}, bf16[256,256]{1,0:T(8,128)(2,1)S(1)}, u32[]{:S(2)}, u32[]{:S(2)}) collective-permute-start(bf16[256,256]{1,0:T(8,128)(2,1)S(1)} %get-tuple-element.307), channel_id=1, source_target_pairs={{0,8},{1,24},{2,9},{3,25},{4,0},{5,16},{6,1},{7,17},{8,10},{9,26},... | collective-permute-start | bytes 393224 | tf_op jit(solution)/shard_map/ppermute | solution.py:52
  42.7 43.0 %collective-permute-start.3 = (bf16[256,256]{1,0:T(8,128)(2,1)S(1)}, bf16[256,256]{1,0:T(8,128)(2,1)S(1)}, u32[]{:S(2)}, u32[]{:S(2)}) collective-permute-start(bf16[256,256]{1,0:T(8,128)(2,1)S(1)} %get-tuple-element.306), channel_id=1, source_target_pairs={{0,9},{1,25},{2,0},{3,16},{4,1},{5,17},{6,8},{7,24},{8,11},{9,27},... | collective-permute-start | bytes 393224 | tf_op jit(solution)/shard_map/ppermute | solution.py:52
  99.0 125.5 %all-gather.9.cloned.1.call-start = ((), (), s32[]{:S(2)}) async-start(), calls=%async_computation.10 | async-start | bytes 1769472 | tf_op jit(solution)/shard_map/all_gather | solution.py:91
  178.4 231.4 %all-gather.11.cloned.1.call-start = ((), (), s32[]{:S(2)}) async-start(), calls=%async_computation.11 | async-start | bytes 7962624 | tf_op jit(solution)/shard_map/all_gather | solution.py:91
  179.0 16.2 %collective-permute-start.14 = (bf16[256,1024]{1,0:T(8,128)(2,1)S(1)}, bf16[256,1024]{1,0:T(8,128)(2,1)S(1)}, u32[]{:S(2)}, u32[]{:S(2)}) collective-permute-start(bf16[256,1024]{1,0:T(8,128)(2,1)S(1)} %get-tuple-element.228), channel_id=1, source_target_pairs={{0,16},{1,17},{2,18},{3,19},{4,20},{5,21},{6,22},{7,23},{8,24},{9,... | collective-permute-start | bytes 1572872 | tf_op jit(solution)/shard_map/ppermute | solution.py:52
  224.6 448.0 %reduce-scatter.4.cloned.1.call-start = ((), (), s32[]{:S(2)}) async-start(), calls=%async_computation.12 | async-start | bytes 7962624 | tf_op jit(solution)/shard_map/reduce_scatter | solution.py:103
  293.9 28.8 %collective-permute-start.31 = (bf16[1024,256]{1,0:T(8,128)(2,1)S(1)}, bf16[1024,256]{1,0:T(8,128)(2,1)}, u32[]{:S(2)}, u32[]{:S(2)}) collective-permute-start(bf16[1024,256]{1,0:T(8,128)(2,1)S(1)} %get-tuple-element.88), channel_id=1, source_target_pairs={{0,2},{1,3},{2,4},{3,5},{4,6},{5,7},{8,10},{9,11},{10,12},{11,13},... | collective-permute-start | bytes 1572872 | tf_op jit(solution)/shard_map/ppermute | solution.py:52
  300.5 23.3 %collective-permute-start.32 = (bf16[256,256]{1,0:T(8,128)(2,1)S(1)}, bf16[256,256]{1,0:T(8,128)(2,1)S(1)}, u32[]{:S(2)}, u32[]{:S(2)}) collective-permute-start(bf16[256,256]{1,0:T(8,128)(2,1)S(1)} %get-tuple-element.304), channel_id=1, source_target_pairs={{0,1},{1,17},{2,8},{3,24},{4,9},{5,25},{6,0},{7,16},{8,3},{9,19},{... | collective-permute-start | bytes 393224 | tf_op jit(solution)/shard_map/ppermute | solution.py:52
  345.2 38.9 %collective-permute-start.34 = (bf16[256,1024]{1,0:T(8,128)(2,1)}, bf16[256,1024]{1,0:T(8,128)(2,1)}, u32[]{:S(2)}, u32[]{:S(2)}) collective-permute-start(bf16[256,1024]{1,0:T(8,128)(2,1)} %fusion.69), channel_id=1, source_target_pairs={{0,8},{1,9},{2,10},{3,11},{4,12},{5,13},{6,14},{7,15},{8,0},{9,1},... | collective-permute-start | bytes 1572872 | tf_op jit(solution)/shard_map/ppermute | solution.py:52
  353.9 21.9 %collective-permute-start.35 = (bf16[256,256]{1,0:T(8,128)(2,1)S(1)}, bf16[256,256]{1,0:T(8,128)(2,1)S(1)}, u32[]{:S(2)}, u32[]{:S(2)}) collective-permute-start(bf16[256,256]{1,0:T(8,128)(2,1)S(1)} %copy-done.118), channel_id=1, source_target_pairs={{0,8},{1,24},{2,9},{3,25},{4,0},{5,16},{6,1},{7,17},{8,10},{9,26},... | collective-permute-start | bytes 393224 | tf_op jit(solution)/shard_map/ppermute | solution.py:52
  353.9 22.1 %collective-permute-start.38 = (bf16[256,256]{1,0:T(8,128)(2,1)S(1)}, bf16[256,256]{1,0:T(8,128)(2,1)S(1)}, u32[]{:S(2)}, u32[]{:S(2)}) collective-permute-start(bf16[256,256]{1,0:T(8,128)(2,1)S(1)} %copy-done.117), channel_id=1, source_target_pairs={{0,9},{1,25},{2,0},{3,16},{4,1},{5,17},{6,8},{7,24},{8,11},{9,27},... | collective-permute-start | bytes 393224 | tf_op jit(solution)/shard_map/ppermute | solution.py:52
  376.5 20.3 %collective-permute-start.41 = (bf16[256,1024]{1,0:T(8,128)(2,1)S(1)}, bf16[256,1024]{1,0:T(8,128)(2,1)S(1)}, u32[]{:S(2)}, u32[]{:S(2)}) collective-permute-start(bf16[256,1024]{1,0:T(8,128)(2,1)S(1)} %bitcast.327), channel_id=1, source_target_pairs={{0,8},{1,9},{2,10},{3,11},{4,12},{5,13},{6,14},{7,15},{8,0},{9,1},... | collective-permute-start | bytes 1572872 | tf_op jit(solution)/shard_map/ppermute | solution.py:52
  386.0 21.7 %collective-permute-start.37 = (bf16[256,1024]{1,0:T(8,128)(2,1)S(1)}, bf16[256,1024]{1,0:T(8,128)(2,1)S(1)}, u32[]{:S(2)}, u32[]{:S(2)}) collective-permute-start(bf16[256,1024]{1,0:T(8,128)(2,1)S(1)} %fusion.51), channel_id=1, source_target_pairs={{0,8},{1,9},{2,10},{3,11},{4,12},{5,13},{6,14},{7,15},{8,0},{9,1},... | collective-permute-start | bytes 1572872 | tf_op jit(solution)/shard_map/ppermute | solution.py:52
  386.1 21.6 %collective-permute-start.40 = (bf16[256,1024]{1,0:T(8,128)(2,1)S(1)}, bf16[256,1024]{1,0:T(8,128)(2,1)S(1)}, u32[]{:S(2)}, u32[]{:S(2)}) collective-permute-start(bf16[256,1024]{1,0:T(8,128)(2,1)S(1)} %bitcast.328), channel_id=1, source_target_pairs={{0,1},{1,0},{2,3},{3,2},{4,5},{5,4},{6,7},{7,6},{8,9},{9,8},{10,11... | collective-permute-start | bytes 1572872 | tf_op jit(solution)/shard_map/ppermute | solution.py:52
  499.4 15.9 %collective-permute-start.48 = (bf16[1024,256]{1,0:T(8,128)(2,1)S(1)}, bf16[1024,256]{1,0:T(8,128)(2,1)S(1)}, u32[]{:S(2)}, u32[]{:S(2)}) collective-permute-start(bf16[1024,256]{1,0:T(8,128)(2,1)S(1)} %slice.718), channel_id=1, source_target_pairs={{2,0},{3,1},{4,2},{5,3},{6,4},{7,5},{10,8},{11,9},{12,10},{13,11},... | collective-permute-start | bytes 1572872 | tf_op jit(solution)/shard_map/ppermute | solution.py:52
  516.2 232.0 %reduce-scatter.6.cloned.1.call-start = ((), (), s32[]{:S(2)}) async-start(), calls=%async_computation.13 | async-start | bytes 4423680 | tf_op jit(solution)/shard_map/reduce_scatter | solution.py:108
  545.1 17.8 %collective-permute-start.54 = (bf16[256,1024]{1,0:T(8,128)(2,1)S(1)}, bf16[256,1024]{1,0:T(8,128)(2,1)S(1)}, u32[]{:S(2)}, u32[]{:S(2)}) collective-permute-start(bf16[256,1024]{1,0:T(8,128)(2,1)S(1)} %get-tuple-element.222), channel_id=1, source_target_pairs={{0,16},{1,17},{2,18},{3,19},{4,20},{5,21},{6,22},{7,23},{8,24},{9,... | collective-permute-start | bytes 1572872 | tf_op jit(solution)/shard_map/ppermute | solution.py:52
  548.0 25.0 %collective-permute-start.57 = (bf16[256,1024]{1,0:T(8,128)(2,1)S(1)}, bf16[256,1024]{1,0:T(8,128)(2,1)S(1)}, u32[]{:S(2)}, u32[]{:S(2)}) collective-permute-start(bf16[256,1024]{1,0:T(8,128)(2,1)S(1)} %get-tuple-element.222), channel_id=1, source_target_pairs={{0,1},{1,0},{2,3},{3,2},{4,5},{5,4},{6,7},{7,6},{8,9},{9,8},{10,11... | collective-permute-start | bytes 1572872 | tf_op jit(solution)/shard_map/ppermute | solution.py:52
  597.2 20.4 %collective-permute-start.51 = (bf16[512,1024]{1,0:T(8,128)(2,1)S(1)}, bf16[512,1024]{1,0:T(8,128)(2,1)S(1)}, u32[]{:S(2)}, u32[]{:S(2)}) collective-permute-start(bf16[512,1024]{1,0:T(8,128)(2,1)S(1)} %pad_maximum_fusion.18), channel_id=1, source_target_pairs={{0,1},{1,0},{2,3},{3,2},{4,5},{5,4},{6,7},{7,6},{8,9},{9,8},{10,11... | collective-permute-start | bytes 3145736 | tf_op jit(solution)/shard_map/ppermute | solution.py:52
  615.6 20.5 %collective-permute-start.63 = (bf16[256,1024]{1,0:T(8,128)(2,1)S(1)}, bf16[256,1024]{1,0:T(8,128)(2,1)}, u32[]{:S(2)}, u32[]{:S(2)}) collective-permute-start(bf16[256,1024]{1,0:T(8,128)(2,1)S(1)} %pad_maximum_fusion.27), channel_id=1, source_target_pairs={{0,8},{1,9},{2,10},{3,11},{4,12},{5,13},{6,14},{7,15},{8,0},{9,1},... | collective-permute-start | bytes 1572872 | tf_op jit(solution)/shard_map/ppermute | solution.py:52
  616.9 20.1 %collective-permute-start.65 = (bf16[256,1024]{1,0:T(8,128)(2,1)}, bf16[256,1024]{1,0:T(8,128)(2,1)S(1)}, u32[]{:S(2)}, u32[]{:S(2)}) collective-permute-start(bf16[256,1024]{1,0:T(8,128)(2,1)} %pad_maximum_fusion.28), channel_id=1, source_target_pairs={{0,16},{1,17},{2,18},{3,19},{4,20},{5,21},{6,22},{7,23},{8,24},{9,... | collective-permute-start | bytes 1572872 | tf_op jit(solution)/shard_map/ppermute | solution.py:52
  617.8 23.6 %collective-permute-start.52 = (bf16[256,1024]{1,0:T(8,128)(2,1)S(1)}, bf16[256,1024]{1,0:T(8,128)(2,1)S(1)}, u32[]{:S(2)}, u32[]{:S(2)}) collective-permute-start(bf16[256,1024]{1,0:T(8,128)(2,1)S(1)} %add_convert_fusion), channel_id=1, source_target_pairs={{0,8},{1,9},{2,10},{3,11},{4,12},{5,13},{6,14},{7,15},{8,0},{9,1},... | collective-permute-start | bytes 1572872 | tf_op jit(solution)/shard_map/ppermute | solution.py:52
  672.6 139.7 %reduce-scatter.8.cloned.1.call-start = ((), (), s32[]{:S(2)}) async-start(), calls=%async_computation.14 | async-start | bytes 2293760 | tf_op jit(solution)/shard_map/reduce_scatter | solution.py:108
  679.8 20.4 %collective-permute-start.84 = (bf16[3072,128]{1,0:T(8,128)(2,1)S(1)}, bf16[3072,128]{1,0:T(8,128)(2,1)S(1)}, u32[]{:S(2)}, u32[]{:S(2)}) collective-permute-start(bf16[3072,128]{1,0:T(8,128)(2,1)S(1)} %dynamic-slice_bitcast_fusion.1), channel_id=1, source_target_pairs={{0,16},{1,17},{2,18},{3,19},{4,20},{5,21},{6,22},{7,23},{8,24},{9,... | collective-permute-start | bytes 2359304 | tf_op jit(solution)/shard_map/ppermute | solution.py:52
  687.2 35.0 %collective-permute-start.72 = (bf16[512,1024]{1,0:T(8,128)(2,1)}, bf16[512,1024]{1,0:T(8,128)(2,1)}, u32[]{:S(2)}, u32[]{:S(2)}) collective-permute-start(bf16[512,1024]{1,0:T(8,128)(2,1)} %dynamic-slice_bitcast_fusion), channel_id=1, source_target_pairs={{0,16},{1,17},{2,18},{3,19},{4,20},{5,21},{6,22},{7,23},{8,24},{9,... | collective-permute-start | bytes 3145736 | tf_op jit(solution)/shard_map/ppermute | solution.py:52
  734.8 17.6 %collective-permute-start.76 = (bf16[512,256]{1,0:T(8,128)(2,1)S(1)}, bf16[512,256]{1,0:T(8,128)(2,1)S(1)}, u32[]{:S(2)}, u32[]{:S(2)}) collective-permute-start(bf16[512,256]{1,0:T(8,128)(2,1)S(1)} %bitcast.401), channel_id=1, source_target_pairs={{9,0},{25,1},{0,2},{16,3},{1,4},{17,5},{8,6},{24,7},{11,8},{27,9},... | collective-permute-start | bytes 786440 | tf_op jit(solution)/shard_map/ppermute | solution.py:681
  755.2 39.1 %all-to-all-start.4 = ((bf16[8,432,128]{2,1,0:T(8,128)(2,1)}), bf16[8,432,128]{2,1,0:T(8,128)(2,1)S(1)}, u32[]{:S(2)}, u32[]{:S(2)}) async-start(bf16[8,432,128]{2,1,0:T(8,128)(2,1)} %copy.208), calls=%async_computation.7 | async-start | bytes 1769472 | tf_op jit(solution)/shard_map/all_to_all | solution.py:119
  794.3 17.1 %all-to-all-start.3 = ((bf16[8,432,128]{2,1,0:T(8,128)(2,1)}), bf16[8,432,128]{2,1,0:T(8,128)(2,1)S(1)}, u32[]{:S(2)}, u32[]{:S(2)}) async-start(bf16[8,432,128]{2,1,0:T(8,128)(2,1)} %copy.205), calls=%async_computation.6 | async-start | bytes 1769472 | tf_op jit(solution)/shard_map/all_to_all | solution.py:119
  (215 other events, 2087.1 us)
Sparse Core Ops, SparseCore 0:
  23.5 74.1 all-gather.4
  99.3 78.9 all-gather.6
  181.0 43.4 all-gather.8
  226.5 119.4 all-gather.10
  516.3 141.8 reduce-scatter.3
  672.7 69.1 reduce-scatter.5
  748.4 54.3 reduce-scatter.7
